TPU v7x, 32 devices: a whole 2x2x4 slice. The times are simulated.
32 devices in a mesh: row: 4 (over x, core), chan: 8 (over z, y).
Axes of the slice: x: 2, y: 2, z: 4, core: 2. Of those that a mesh axis runs over, the one named last changes fastest.
Arguments:
- tokens: bfloat16 [16384, 1024], P(('row', 'chan')), may hold values from -6 to 6
- starts: int32 [4, 4096], P('row'), may hold values 0 or 1
- layer_norm_gain: float32 [1024], replicated, may hold values from 0.5 to 1.5
- ln_bias: float32 [1024], replicated, may hold values from -3 to 3
- w_up: bfloat16 [1024, 3072], replicated, may hold values from -0.1875 to 0.1875
- w_val: bfloat16 [1024, 512], replicated, may hold values from -0.1875 to 0.1875
- w_mix: bfloat16 [512, 3072], replicated, may hold values from -0.25 to 0.25
- w_down: bfloat16 [3072, 1024], replicated, may hold values from -0.15625 to 0.15625
- decay_rate: float32 [512, 512], P('chan'), may hold values from 0.0002 to 0.05
- mix_coef: float32 [512, 512], P('chan'), may hold values from -0.006 to 0.006
- out_grad: bfloat16 [16384, 1024], P(('row', 'chan')), may hold values from -6 to 6
Outputs:
- block_out: bfloat16 [16384, 1024], P(('row', 'chan'))
- tokens_grad: float32 [16384, 1024], P(('row', 'chan'))
- gain_grad: float32 [1024], P(('row', 'chan'))
- bias_grad: float32 [1024], P(('row', 'chan'))
- up_grad: float32 [1024, 3072], P(('row', 'chan'))
- val_grad: float32 [1024, 512], P(('row', 'chan'))
- mix_grad: float32 [512, 3072], P(('row', 'chan'))
- down_grad: float32 [3072, 1024], P(('row', 'chan'))
- rate_grad: float32 [512, 512], P('chan', 'row')
- coef_grad: float32 [512, 512], P('chan', 'row')
All inputs are finite; a program needn't handle non-finite values. No bound on the sum of `starts` on one device may be relied on, other than what follows from the above.
Results may differ from a plain program's by a relative error of at most 0.007.
Values may be sent and summed in bfloat16 or wider, within the bound.
No kernel may reach another device: no remote copies, remote signals or barrier semaphores. Data moves between devices by JAX's collectives and lax.ppermute only.
A program may use at most 320 MiB of HBM per device.

v0:
```python
import jax
import jax.numpy as jnp
from jax import lax
from jax.experimental import pallas as pl
from jax.experimental.pallas import tpu as pltpu
from jax.sharding import PartitionSpec as P

T = 128
SUB = 8
GROUP = 16
SEG = 4
f32 = jnp.float32
bf16 = jnp.bfloat16
NT = (((1,), (1,)), ((), ()))
TN = (((0,), (0,)), ((), ()))
NN = (((1,), (0,)), ((), ()))


def mm(a, b, d=NN):
    return lax.dot_general(a, b, d, preferred_element_type=f32)


def iota(shape, d):
    return lax.broadcasted_iota(jnp.int32, shape, d)


def powers(rate_row, pt_ref, c):
    n = rate_row.shape[1]
    steps = iota((8, n), 0).astype(f32)
    r8 = jnp.broadcast_to(rate_row, (8, n))
    parts = [jnp.exp(-r8 * steps)]
    fade = jnp.exp(-8.0 * r8)
    while len(parts) < T // 8:
        parts = parts + [p * fade for p in parts]
        fade = fade * fade
    for i in range(0, len(parts), 2):
        pt_ref[c, i * 8 : i * 8 + 16, :] = jnp.concatenate(parts[i : i + 2], 0).astype(bf16)


def put(ref, c, val, rows):
    for q in range(val.shape[1] // T):
        ref[q, pl.ds(c, rows, stride=SUB), :] = val[:, q * T : (q + 1) * T]


def take(ref, c, rows):
    return jnp.concatenate(
        [ref[q, pl.ds(c, rows, stride=SUB), :] for q in range(ref.shape[0])], 1
    )


def tiles(v):
    return jnp.stack([v[:, q * T : (q + 1) * T] for q in range(v.shape[1] // T)])


def untile(v):
    return jnp.concatenate([v[q] for q in range(v.shape[0])], 1)


def flip_matrix():
    return (iota((T, T), 0) + iota((T, T), 1) == T - 1).astype(f32).astype(bf16)


def seg_masks(ins, g):
    return jnp.concatenate([(ins == g * SEG + k).astype(f32) for k in range(SEG)], 0)


def rep(x):
    return jnp.concatenate([x] * SEG, 0)


def fold(o, m, rows):
    o = o * m
    out = o[0:rows]
    for k in range(1, SEG):
        out = out + o[k * rows : (k + 1) * rows]
    return out


def far_part(a, p, rows):
    hi = a.astype(bf16)
    lo = (a - hi.astype(f32)).astype(bf16)
    o = mm(jnp.concatenate([hi, lo], 0), p, NT)
    return o[:rows] + o[rows:]


def lanes_of(ref, c, rows):
    return ref[pl.ds(c, rows, stride=GROUP), :]


def fwd_kernel(groups, keep, x, rate, coef, ins, insj, head, tailj, y, hs, toe, pt, ss, near, xs, kr):
    rows = ins.shape[0]
    n = rate.shape[1]
    flip = flip_matrix()
    xs[...] = x[...].astype(f32).reshape(rows * GROUP, T)
    tail = tailj[...]
    hd = head[...]
    m0 = seg_masks(ins[...], 0)
    m0b = m0.astype(bf16)
    tri = iota((T, T), 1) >= iota((T, T), 0)
    for sub in range(GROUP // SUB):
        lo = sub * SUB
        cf = coef[lo : lo + SUB, :]
        rt = rate[lo : lo + SUB, :]
        cfh = cf.astype(bf16)
        cfl = (cf - cfh.astype(f32)).astype(bf16)
        cf2 = jnp.concatenate([cfh, cfl], 0)
        xj = []
        for c in range(SUB):
            xc = lanes_of(xs, lo + c, rows).astype(bf16)
            xj.append(mm(xc, flip).astype(bf16) * tail)
        for c in range(SUB):
            powers(rt[c : c + 1], pt, c)
            p = pt[c]
            put(ss, c, mm(xj[c], p), rows)
            k2 = mm(cf2, p, NT)
            kr[c : c + 1, :] = k2[c : c + 1] + k2[SUB + c : SUB + c + 1]
        for c in range(SUB):
            k = jnp.broadcast_to(kr[c : c + 1, :], (T, T))
            kb = pltpu.roll(k, 0, 1, stride=1, stride_axis=0)
            tp = jnp.where(tri, kb, 0.0).astype(bf16)
            toe[lo + c] = tp
            xc = lanes_of(xs, lo + c, rows).astype(bf16)
            near[c] = fold(mm(rep(xc) * m0b, tp), m0, rows)
        fade = tiles(jnp.exp(-float(T) * rt))
        ce = tiles(cf * jnp.exp(-rt))
        h = jnp.zeros((n // T, SUB, T), f32)
        for b in range(rows):
            w = slice(b * SUB, (b + 1) * SUB)
            hs[sub, :, w, :] = h
            s = ss[:, w, :]
            ss[:, w, :] = h * ce
            h = h * (fade * keep[b]) + s

        @pl.loop(1, groups[0])
        def _(g):
            m = seg_masks(ins[...], g)
            for c in range(SUB):
                xc = lanes_of(xs, lo + c, rows).astype(bf16)
                near[c] += fold(mm(rep(xc) * m.astype(bf16), toe[lo + c]), m, rows)

        for c in range(SUB):
            far = far_part(take(ss, c, rows), pt[c], rows)
            xs[pl.ds(lo + c, rows, stride=GROUP), :] = near[c] + hd * far
    y[...] = xs[...].reshape(rows, GROUP, T).astype(bf16)


def bwd_kernel(
    groups, keep, x, dy, rate, coef, ins, insj, head, tailj, hs, toe,
    dv, drate, dcoef, pt, s1, e0, e1, near, gacc, nr, xs, ys,
):
    rows = ins.shape[0]
    n = rate.shape[1]
    flip = flip_matrix()
    xs[...] = x[...].astype(f32).reshape(rows * GROUP, T)
    ys[...] = dy[...].astype(f32).reshape(rows * GROUP, T)
    tail = tailj[...]
    hdb = head[...].astype(bf16)
    mn = seg_masks(ins[...], 0).astype(bf16)
    mj = seg_masks(insj[...], 0)
    mjb = mj.astype(bf16)
    lag = iota((rows, T), 1).astype(f32).astype(bf16)
    lag1 = (iota((rows, T), 1) + 1).astype(f32).astype(bf16)
    lagf = iota((1, T), 1).astype(f32)
    valid = iota((T, T), 0) + iota((T, T), 1) >= T - 1
    row16 = iota((16, T), 0)

    def lags(d, xx, md, mx):
        o = mm(rep(d) * md, rep(xx) * mx, TN)
        o = pltpu.roll(jnp.where(valid, o, 0.0), 1, 1, stride=1, stride_axis=0)
        return jnp.sum(o, axis=0, keepdims=True)

    for sub in range(GROUP // SUB):
        lo = sub * SUB
        rt = rate[lo : lo + SUB, :]
        cf = coef[lo : lo + SUB, :]
        xa = jnp.concatenate([lanes_of(xs, lo + c, rows) for c in range(SUB)], 0).astype(bf16)
        da = jnp.concatenate([lanes_of(ys, lo + c, rows) for c in range(SUB)], 0).astype(bf16)
        xja = mm(xa, flip).astype(bf16)
        dja = mm(da, flip).astype(bf16)
        for c in range(SUB):
            sl = slice(c * rows, (c + 1) * rows)
            near[c] = fold(mm(rep(dja[sl]) * mjb, toe[lo + c]), mj, rows)
            gacc[c : c + 1, :] = lags(da[sl], xja[sl], mn, mjb)

        @pl.loop(1, groups[0])
        def _(g):
            m = seg_masks(ins[...], g).astype(bf16)
            k = seg_masks(insj[...], g)
            kb = k.astype(bf16)
            for c in range(SUB):
                d = lanes_of(ys, lo + c, rows).astype(bf16)
                xx = lanes_of(xs, lo + c, rows).astype(bf16)
                dj = mm(d, flip).astype(bf16)
                xj = mm(xx, flip).astype(bf16)
                near[c] += fold(mm(rep(dj) * kb, toe[lo + c]), k, rows)
                gacc[c : c + 1, :] += lags(d, xj, m, kb)

        for c in range(SUB):
            sl = slice(c * rows, (c + 1) * rows)
            powers(rt[c : c + 1], pt, c)
            gr = gacc[c : c + 1, :]
            gl = gr * lagf
            gh = gr.astype(bf16).astype(f32)
            glh = gl.astype(bf16).astype(f32)
            gm = jnp.where(row16 == 2, glh, jnp.where(row16 == 3, gl - glh, 0.0))
            gm = jnp.where(row16 == 0, gh, jnp.where(row16 == 1, gr - gh, gm)).astype(bf16)
            dh = da[sl] * hdb
            o = mm(jnp.concatenate([xja[sl] * tail * lag, dh, dh * lag1, gm], 0), pt[c])
            put(s1, c, o[0:rows], rows)
            put(e0, c, o[rows : 2 * rows], rows)
            put(e1, c, o[2 * rows : 3 * rows], rows)
            k = 3 * rows
            nr[c : c + 1, :] = o[k : k + 1] + o[k + 1 : k + 2]
            nr[SUB + c : SUB + c + 1, :] = o[k + 2 : k + 3] + o[k + 3 : k + 4]
        fade = tiles(jnp.exp(-float(T) * rt))
        ee = tiles(jnp.exp(-rt))
        ce = tiles(cf) * ee
        zero = jnp.zeros((n // T, SUB, T), f32)
        dh, ac, ar, ae = zero, zero, zero, zero
        for b in range(rows - 1, -1, -1):
            w = slice(b * SUB, (b + 1) * SUB)
            h = hs[sub, :, w, :]
            e = e0[:, w, :]
            kf = fade * keep[b]
            ar = ar + dh * (kf * (float(T) * h) + s1[:, w, :])
            ae = ae + h * e1[:, w, :]
            ac = ac + h * e
            s1[:, w, :] = dh
            dh = ce * e + kf * dh
        for c in range(SUB):
            far = far_part(take(s1, c, rows), pt[c], rows)
            near[c] = near[c] + tail.astype(f32) * far
        dva = mm(near[...].reshape(SUB * rows, T).astype(bf16), flip)
        for c in range(SUB):
            xs[pl.ds(lo + c, rows, stride=GROUP), :] = dva[c * rows : (c + 1) * rows]
        dcoef[lo : lo + SUB, :] = nr[0:SUB, :] + untile(ee * ac)
        drate[lo : lo + SUB, :] = -(cf * nr[SUB : 2 * SUB, :] + untile(ar + ce * ae))
    dv[...] = xs[...].reshape(rows, GROUP, T).astype(bf16)


def ssm_masks(starts):
    seqs, length = starts.shape
    blocks = length // T
    rows = seqs * blocks
    st = starts.reshape(rows, T)
    tri = (iota((T, T), 0) <= iota((T, T), 1)).astype(bf16)
    ins = mm(st.astype(bf16), tri).astype(jnp.int32) - st[:, :1]
    cont = (st[:, :1] == 0) & (iota((rows, 1), 0) % blocks != 0)
    last = ins[:, -1:]
    head = ((ins == 0) & cont).astype(f32)
    back = (iota((T, T), 0) + iota((T, T), 1) == T - 1).astype(bf16)
    insj = mm(ins.astype(bf16), back).astype(jnp.int32)
    tailj = (insj == last).astype(bf16)
    keep = (cont & (last == 0)).astype(f32)[:, 0]
    groups = (jnp.max(last) // SEG + 1).reshape(1).astype(jnp.int32)
    return groups, keep, ins, insj, head, tailj


def ssm_specs(rows, n):
    full = pl.BlockSpec((rows, T), lambda i: (0, 0))
    return dict(
        sm=pl.BlockSpec(memory_space=pltpu.SMEM),
        full=full,
        ch=pl.BlockSpec((rows, GROUP, T), lambda i: (0, i, 0)),
        par=pl.BlockSpec((GROUP, n), lambda i: (i, 0)),
        hs=pl.BlockSpec((GROUP // SUB, n // T, rows * SUB, T), lambda i: (i, 0, 0, 0)),
        toe=pl.BlockSpec((GROUP, T, T), lambda i: (i, 0, 0)),
        big=pltpu.VMEM((n // T, rows * SUB, T), f32),
        pt=pltpu.VMEM((SUB, T, n), bf16),
        near=pltpu.VMEM((SUB, rows, T), f32),
        xs=pltpu.VMEM((rows * GROUP, T), f32),
        cost=pl.CostEstimate(flops=2 * 10**10, bytes_accessed=10**7, transcendentals=0),
    )


def ssm_fwd(x, rate, coef, masks):
    rows, chans, _ = x.shape
    n = rate.shape[1]
    s = ssm_specs(rows, n)
    return pl.pallas_call(
        fwd_kernel,
        grid=(chans // GROUP,),
        in_specs=[s["sm"], s["sm"], s["ch"], s["par"], s["par"]] + [s["full"]] * 4,
        out_specs=[s["ch"], s["hs"], s["toe"]],
        out_shape=[
            pltpu.HBM(x.shape, bf16),
            pltpu.HBM((chans // SUB, n // T, rows * SUB, T), f32),
            pltpu.HBM((chans, T, T), bf16),
        ],
        scratch_shapes=[s["pt"], s["big"], s["near"], s["xs"], pltpu.VMEM((SUB, T), f32)],
        compiler_params=pltpu.CompilerParams(vmem_limit_bytes=40 * 2**20),
        cost_estimate=s["cost"],
        name="ssm_fwd",
    )(masks[0], masks[1], x, rate, coef, *masks[2:])


def ssm_bwd(x, dy, rate, coef, masks, hs, toe):
    rows, chans, _ = x.shape
    n = rate.shape[1]
    s = ssm_specs(rows, n)
    return pl.pallas_call(
        bwd_kernel,
        grid=(chans // GROUP,),
        in_specs=[s["sm"], s["sm"], s["ch"], s["ch"], s["par"], s["par"]]
        + [s["full"]] * 4
        + [s["hs"], s["toe"]],
        out_specs=[s["ch"], s["par"], s["par"]],
        out_shape=[
            pltpu.HBM(x.shape, bf16),
            pltpu.HBM((chans, n), f32),
            pltpu.HBM((chans, n), f32),
        ],
        scratch_shapes=[
            s["pt"],
            s["big"],
            s["big"],
            s["big"],
            s["near"],
            pltpu.VMEM((SUB, T), f32),
            pltpu.VMEM((2 * SUB, n), f32),
            s["xs"],
            s["xs"],
        ],
        compiler_params=pltpu.CompilerParams(vmem_limit_bytes=40 * 2**20),
        cost_estimate=s["cost"],
        name="ssm_bwd",
    )(masks[0], masks[1], x, dy, rate, coef, *masks[2:], *from_hbm(hs, toe))


epsilon = 1e-05
TILE = 768


def gauss_cdf(a):
    return 0.5 * (1.0 + lax.erf(a * 0.7071067811865476))


def gauss_pdf(a):
    return jnp.exp(-0.5 * a * a) * 0.3989422804014327


def struct(shape, dtype):
    return jax.ShapeDtypeStruct(shape, dtype)


def in_hbm(shape, dtype):
    return pltpu.HBM(shape, dtype)


def from_hbm(*arrays):
    return tuple(pltpu.with_memory_space_constraint(a, pltpu.HBM) for a in arrays)


def whole(shape):
    return pl.BlockSpec(shape, lambda *_: (0,) * len(shape))


def call(kernel, name, grid, ins, outs, out_shape, args, scalars=None, scratch=(), aliases=None, vmem=24, cost=None):
    lead = [] if scalars is None else [scalars]
    return pl.pallas_call(
        kernel,
        grid_spec=pltpu.PrefetchScalarGridSpec(
            num_scalar_prefetch=len(lead),
            grid=grid,
            in_specs=ins,
            out_specs=outs,
            scratch_shapes=list(scratch),
        ),
        out_shape=out_shape,
        input_output_aliases=aliases or {},
        compiler_params=pltpu.CompilerParams(vmem_limit_bytes=vmem * 2**20),
        cost_estimate=cost and pl.CostEstimate(flops=cost, bytes_accessed=10**7, transcendentals=0),
        name=name,
    )(*lead, *args)


def normalise(x):
    centred = x - jnp.mean(x, axis=1, keepdims=True)
    inv_std = lax.rsqrt(jnp.mean(centred * centred, axis=1, keepdims=True) + epsilon)
    return centred * inv_std, inv_std


def norm_kernel(tok, gain, bias, w_val, normed, v_act, v_slope):
    x_hat, _ = normalise(tok[...].astype(f32))
    n = (x_hat * gain[...] + bias[...]).astype(bf16)
    normed[...] = n
    v = mm(n, w_val[...])
    cdf = gauss_cdf(v)
    v_act[...] = (v * cdf).T.astype(bf16).reshape(v_act.shape)
    v_slope[...] = (cdf + v * gauss_pdf(v)).T.reshape(v_slope.shape)


def norm_call(tokens, gain, bias, w_val, chan_n):
    own, width = tokens.shape
    inner = w_val.shape[1]
    quads = own // T
    spread = (chan_n, quads, inner // chan_n, T)
    block = pl.BlockSpec((chan_n, 1, inner // chan_n, T), lambda i: (0, i, 0, 0))
    rows = pl.BlockSpec((T, width), lambda i: (i, 0))
    return call(
        norm_kernel,
        "norm_val",
        (quads,),
        [rows, whole((1, width)), whole((1, width)), whole(w_val.shape)],
        [rows, block, block],
        [struct((own, width), bf16), struct(spread, bf16), struct(spread, f32)],
        from_hbm(tokens, gain[None], bias[None], w_val),
    )


def gate_kernel(
    core, n_own, n_oth, g_own, g_oth, w_up, w_mix, w_down,
    u_act, d_slope, d_yproj, normed_t, dy_own, dy_oth, ga, na, acc,
):
    j = pl.program_id(0)
    own = n_own.shape[0]

    @pl.when(j == 0)
    def _():
        for h, (n, g) in enumerate(((n_own, g_own), (n_oth, g_oth))):
            na[h * own : (h + 1) * own, :] = n[...]
            ga[h * own : (h + 1) * own, :] = g[...]
            normed_t[:, h * own : (h + 1) * own] = n[...].T

    u = mm(na[...], w_up[...])
    d = mm(ga[...], w_down[...], NT)
    cdf = gauss_cdf(u)
    act = u * cdf
    u_act[...] = act.astype(bf16)
    d_slope[...] = (d * (cdf + u * gauss_pdf(u))).astype(bf16)
    dyp = (d * act).astype(bf16)
    d_yproj[...] = dyp
    part = mm(dyp, w_mix[...], NT)

    @pl.when(j == 0)
    def _():
        acc[...] = part

    @pl.when(j > 0)
    def _():
        acc[...] += part

    @pl.when(j == pl.num_programs(0) - 1)
    def _():
        shape = (dy_own.shape[0], dy_own.shape[2], T)
        for q in range(dy_own.shape[1]):
            dy_own[:, q] = acc[q * T : (q + 1) * T, :].T.reshape(shape)
            dy_oth[:, q] = acc[own + q * T : own + (q + 1) * T, :].T.astype(bf16).reshape(shape)


def gate_call(core, normed, normed_oth, grad, grad_oth, w_up, w_mix, w_down, row_n, chan_n):
    own, width = normed.shape
    inner, ff = w_mix.shape
    per = ff // row_n // TILE
    half = ff // 2
    col = lambda j, s: (2 * (j // per) + s[0]) * per + j % per
    tok = whole((own, width))
    tile = pl.BlockSpec((2 * own, TILE), lambda j, s: (0, j))
    spread = (chan_n, own // T, inner // chan_n, T)
    return call(
        gate_kernel,
        "gate",
        (half // TILE,),
        [
            tok,
            tok,
            tok,
            tok,
            pl.BlockSpec((width, TILE), lambda j, s: (0, col(j, s))),
            pl.BlockSpec((inner, TILE), lambda j, s: (0, col(j, s))),
            pl.BlockSpec((TILE, width), lambda j, s: (col(j, s), 0)),
        ],
        [tile, tile, tile, whole((width, 2 * own)), whole(spread), whole(spread), whole((2 * own, width))],
        [in_hbm((2 * own, half), bf16)] * 3
        + [in_hbm((width, 2 * own), bf16), in_hbm(spread, f32), in_hbm(spread, bf16)]
        + [in_hbm((2 * own, width), bf16)],
        (normed, normed_oth, grad, grad_oth, w_up, w_mix, w_down),
        scalars=core,
        scratch=[
            pltpu.VMEM((2 * own, width), bf16),
            pltpu.VMEM((2 * own, inner), f32),
        ],
        vmem=56,
    )


def mine_a(s):
    return jnp.where(s[0] == 0, s[1], s[2])


def mine_b(s):
    return jnp.where(s[0] == 0, s[2], s[1])


def row_block(s, a, b, core, high, low):
    x = jnp.where(s[0] == 0, a, b)
    y = jnp.where(s[0] == 0, b, a)
    return x * 16 + core * 8 + high * 4 + low * 2 + y


def mid_kernel(
    s, y_own, y_oth, w_mix, u_act, d_slope, d_yproj, normed_t,
    gate, d_upre, u_give, u_keep, m_give, m_keep, yt, yn, us, ms,
):
    inner = yt.shape[0]

    own = yn.shape[0] // 2

    @pl.when(pl.program_id(0) == 0)
    def _():
        for h, y in enumerate((y_own, y_oth)):
            for q in range(y.shape[1]):
                part = y[:, q].reshape(inner, T)
                at = slice(h * own + q * T, h * own + (q + 1) * T)
                yt[:, at] = part
                yn[at, :] = part.T

    yp = mm(yn[...], w_mix[...])
    gate[...] = (u_act[...].astype(f32) * yp).astype(bf16)
    du = (d_slope[...].astype(f32) * yp).astype(bf16)
    d_upre[...] = du
    us[...] = mm(normed_t[...], du).astype(bf16)
    ms[...] = mm(yt[...], d_yproj[...]).astype(bf16)
    m = u_give.shape[1]
    for sel, out in ((1, u_give), (0, u_keep)):
        a = mine_a(s) ^ sel
        for b in (0, 1):
            for low in (0, 1):
                for high in (0, 1):
                    for core in (0, 1):
                        at = pl.multiple_of(row_block(s, a, b, core, high, low) * m, m)
                        out[b * 8 + low * 4 + high * 2 + core] = us[pl.ds(at, m), :]
    m = m_give.shape[1]
    for sel, out in ((1, m_give), (0, m_keep)):
        low = s[3] ^ sel
        for high in (0, 1):
            for a in (0, 1):
                for b in (0, 1):
                    for core in (0, 1):
                        at = pl.multiple_of(row_block(s, a, b, core, high, low) * m, m)
                        out[high * 8 + a * 4 + b * 2 + core] = ms[pl.ds(at, m), :]


def mid_call(scal, y_own, y_oth, w_mix, u_act, d_slope, d_yproj, normed_t, row_n):
    inner, ff = w_mix.shape
    half = u_act.shape[1]
    own = u_act.shape[0] // 2
    width = normed_t.shape[0]
    per = ff // row_n // TILE
    col = lambda j, s: (2 * (j // per) + s[0]) * per + j % per
    tile = pl.BlockSpec((2 * own, TILE), lambda j, s: (0, j))
    um, mx = width // 32, inner // 32
    ub = pl.BlockSpec((16, um, TILE), lambda j, s: (0, 0, j))
    mb = pl.BlockSpec((16, mx, TILE), lambda j, s: (0, 0, j))
    return call(
        mid_kernel,
        "mix_up",
        (half // TILE,),
        [
            whole(y_own.shape),
            whole(y_own.shape),
            pl.BlockSpec((inner, TILE), lambda j, s: (0, col(j, s))),
            tile,
            tile,
            tile,
            whole(normed_t.shape),
        ],
        [tile, tile, ub, ub, mb, mb],
        [in_hbm((2 * own, half), bf16)] * 2
        + [in_hbm((16, um, half), bf16)] * 2
        + [in_hbm((16, mx, half), bf16)] * 2,
        (y_own, y_oth, w_mix, u_act, d_slope, d_yproj, normed_t),
        scalars=scal,
        scratch=[
            pltpu.VMEM((inner, 2 * own), bf16),
            pltpu.VMEM((2 * own, inner), bf16),
            pltpu.VMEM((width, TILE), bf16),
            pltpu.VMEM((inner, TILE), bf16),
        ],
        vmem=56,
        cost=10**10,
    )


def block_kernel(s, gate, d_upre, w_down, w_up, block_own, dn_own, oth, acc):
    j = pl.program_id(0)
    own = block_own.shape[0]
    sums = (mm(gate[...], w_down[...]), mm(d_upre[...], w_up[...], NT))

    @pl.when(j == 0)
    def _():
        for k in (0, 1):
            acc[k] = sums[k]

    @pl.when(j > 0)
    def _():
        for k in (0, 1):
            acc[k] += sums[k]

    @pl.when(j == pl.num_programs(0) - 1)
    def _():
        block_own[...] = acc[0, :own]
        dn_own[...] = acc[1, :own]
        oth[...] = acc[:, own:].astype(bf16)


def block_call(scal, gate, d_upre, w_down, w_up, row_n):
    ff, width = w_down.shape
    own = gate.shape[0] // 2
    part = ff // row_n
    tile = pl.BlockSpec((2 * own, part), lambda j, s: (0, j))
    return call(
        block_kernel,
        "block",
        (row_n // 2,),
        [
            tile,
            tile,
            pl.BlockSpec((part, width), lambda j, s: (2 * j + s[0], 0)),
            pl.BlockSpec((width, part), lambda j, s: (0, 2 * j + s[0])),
        ],
        [whole((own, width)), whole((own, width)), whole((2, own, width))],
        [in_hbm((own, width), f32), in_hbm((own, width), f32), in_hbm((2, own, width), bf16)],
        (gate, d_upre, w_down, w_up),
        scalars=scal,
        scratch=[pltpu.VMEM((2, 2 * own, width), f32)],
        vmem=56,
    )


def down_val_kernel(s, down_g, down_k, v_own, v_oth, normed_t, d_give, d_keep, vs, vt):
    i = pl.program_id(0)
    inner, pair = vt.shape
    m = vs.shape[0] // 32
    rows = down_g.shape[0]

    @pl.when(i == 0)
    def _():
        for h, v in enumerate((v_own, v_oth)):
            for q in range(v.shape[1]):
                at = h * pair // 2 + q * T
                vt[:, at : at + T] = v[:, q].reshape(inner, T)
        vs[...] = mm(normed_t[...], vt[...], NT)

    b, low, high = i // 4, (i // 2) % 2, i % 2
    for sel, down, out in ((1, down_g, d_give), (0, down_k, d_keep)):
        out[0, 0:rows, :] = down[...]
        a = mine_a(s) ^ sel
        cut = []
        for core in (0, 1):
            at = pl.multiple_of(row_block(s, a, b, core, high, low) * m, m)
            cut.append(vs[pl.ds(at, m), :])
        parts = [jnp.concatenate([c[r * 8 : r * 8 + 8] for c in cut], 0) for r in range(m // 8)]
        out[0, rows : rows + 16, :] = jnp.concatenate(parts, 1).astype(bf16)


def down_val_call(scal, down, d_vpre, v_oth, normed_t):
    half = v_oth.shape
    inner = half[0] * half[2]
    width, pair = normed_t.shape
    rows = down.shape[0] // 16

    def block_of(sel):
        def at(i, s):
            a, b, low, high = mine_a(s) ^ sel, i // 4, (i // 2) % 2, i % 2
            x = jnp.where(s[0] == 0, a, b)
            y = jnp.where(s[0] == 0, b, a)
            return x * 8 + high * 4 + low * 2 + y, 0

        return pl.BlockSpec((rows, width), at)

    buf = (8, rows + 16, width)
    out = pl.BlockSpec((1, rows + 16, width), lambda i, s: (i, 0, 0))
    return call(
        down_val_kernel,
        "down_val",
        (8,),
        [
            block_of(1),
            block_of(0),
            pl.BlockSpec(half, lambda i, s: (s[0], 0, 0, 0)),
            whole(half),
            whole(normed_t.shape),
        ],
        [out, out],
        [struct(buf, bf16)] * 2,
        (down, down, d_vpre, v_oth, normed_t),
        scalars=scal,
        scratch=[pltpu.VMEM((width, inner), f32), pltpu.VMEM((inner, pair), bf16)],
    )


def step_kernel(bit, keep_g, got_g, keep_k, got_k, give, keep):
    give[...] = (keep_g[0].astype(f32) + got_g[0].astype(f32)).astype(bf16)
    keep[...] = (keep_k[0].astype(f32) + got_k[0].astype(f32)).astype(bf16)


def step_call(bit, keep, got):
    n, rows, cols = keep.shape
    n //= 2
    nb = max(1, n // 4)
    view = (2, n, rows, cols)
    other = pl.BlockSpec((1, nb, rows, cols), lambda i, b: (1 - b[0], i, 0, 0))
    same = pl.BlockSpec((1, nb, rows, cols), lambda i, b: (b[0], i, 0, 0))
    out = pl.BlockSpec((nb, rows, cols), lambda i, b: (i, 0, 0))
    keep, got = keep.reshape(view), got.reshape(view)
    return call(
        step_kernel,
        "halve",
        (n // nb,),
        [other, other, same, same],
        [out, out],
        [struct((n, rows, cols), bf16)] * 2,
        (keep, got, keep, got),
        scalars=bit,
    )


def tail_kernel(
    tok, grad, gain, block_own, got, dn_own, d_vpre, w_val, block_out, tokens_grad, norm_part, acc
):
    i = pl.program_id(0)
    x = tok[...].astype(f32)
    x_hat, inv_std = normalise(x)
    block_out[...] = (x + block_own[...] + got[0].astype(f32)).astype(bf16)
    dv = d_vpre[...].reshape(w_val.shape[1], T).T
    dn = dn_own[...] + got[1].astype(f32) + mm(dv, w_val[...], NT)
    dx = dn * gain[...]
    tokens_grad[...] = grad[...].astype(f32) + inv_std * (
        dx
        - jnp.mean(dx, axis=1, keepdims=True)
        - x_hat * jnp.mean(dx * x_hat, axis=1, keepdims=True)
    )
    sums = jnp.concatenate(
        [jnp.sum(dn * x_hat, axis=0, keepdims=True), jnp.sum(dn, axis=0, keepdims=True)], 0
    )

    @pl.when(i == 0)
    def _():
        acc[...] = sums

    @pl.when(i > 0)
    def _():
        acc[...] += sums

    @pl.when(i == pl.num_programs(0) - 1)
    def _():
        parts, lanes = norm_part.shape
        w = acc.shape[1] // parts
        for k in range(parts):
            cut = acc[:, k * w : (k + 1) * w]
            blank = jnp.zeros((1, lanes - 2 * w), f32)
            norm_part[k : k + 1, :] = jnp.concatenate([cut[0:1], cut[1:2], blank], 1)


def tail_call(tokens, grad, gain, block_own, got, dn_own, d_vpre, w_val, parts):
    own, width = tokens.shape
    rows = pl.BlockSpec((T, width), lambda i: (i, 0))
    chan_n, _, group, _ = d_vpre.shape
    return call(
        tail_kernel,
        "norm_back",
        (own // T,),
        [
            rows,
            rows,
            whole((1, width)),
            rows,
            pl.BlockSpec((2, T, width), lambda i: (0, i, 0)),
            rows,
            pl.BlockSpec((chan_n, 1, group, T), lambda i: (0, i, 0, 0)),
            whole(w_val.shape),
        ],
        [rows, rows, whole((parts, T))],
        [struct((own, width), bf16), struct((own, width), f32), struct((parts, T), f32)],
        from_hbm(tokens, grad, gain[None], block_own, got, dn_own, d_vpre, w_val),
        scratch=[pltpu.VMEM((2, width), f32)],
    )


def finish_kernel(s, u_keep, u_got, m_keep, m_got, d_keep, d_got, down, mine, other):
    d = d_keep[0].astype(f32) + d_got[0].astype(f32)
    rows = down.shape[0]
    down[...] = d[:rows]
    half = d.shape[1]
    um, mx = u_keep.shape[1], m_keep.shape[1]
    for out, core in ((mine, s[0]), (other, 1 - s[0])):
        out[0:um, :] = u_keep[core].astype(f32) + u_got[core].astype(f32)
        out[um : um + mx, :] = m_keep[core].astype(f32) + m_got[core].astype(f32)
        out[um + mx :, 0:half] = jnp.where(core == 0, d[rows : rows + 8], d[rows + 8 :])
        out[um + mx :, half:] = jnp.zeros((8, out.shape[1] - half), f32)


def finish_call(scal, up, mix, down):
    um, mx, half = up[0].shape[1], mix[0].shape[1], up[0].shape[2]
    rows, width = down[0].shape[1:]
    args = (*up, *mix, *down)
    pack = (um + mx + 8, half)
    return call(
        finish_kernel,
        "finish",
        (1,),
        [whole(a.shape) for a in args],
        [whole((rows - 16, width)), whole(pack), whole(pack)],
        [struct((rows - 16, width), f32), struct(pack, f32), struct(pack, f32)],
        args,
        scalars=scal,
    )


def join_kernel(s, mine, got, up, mix, val):
    um, mx = up.shape[0], mix.shape[0]
    first = s[0] == 0
    part = mine.shape[1] // 2
    for core in (0, 1):
        held = jnp.where(first, mine[...], got[...]) if core == 0 else jnp.where(first, got[...], mine[...])
        for x in (0, 1):
            to = slice((2 * x + core) * part, (2 * x + core + 1) * part)
            up[:, to] = held[0:um, x * part : (x + 1) * part]
            mix[:, to] = held[um : um + mx, x * part : (x + 1) * part]
        w = val.shape[1] // 2
        for r in range(val.shape[0] // 8):
            val[r * 8 : r * 8 + 8, core * w : (core + 1) * w] = held[um + mx :, r * w : (r + 1) * w]


def join_call(scal, mine, got, um, mx, inner):
    ff = mine.shape[1] * 2
    return call(
        join_kernel,
        "join",
        (1,),
        [whole(mine.shape)] * 2,
        [whole((um, ff)), whole((mx, ff)), whole((um, inner))],
        [struct((um, ff), f32), struct((mx, ff), f32), struct((um, inner), f32)],
        (mine, got),
        scalars=scal,
    )


def make_square(row_n, chan_n):
    def on_device(
        tokens, starts, layer_norm_gain, ln_bias, w_up, w_val, w_mix, w_down,
        decay_rate, mix_coef, out_grad,
    ):
        own, width = tokens.shape
        inner = w_val.shape[1]
        row, chan = lax.axis_index("row"), lax.axis_index("chan")
        core = row % 2
        scal = jnp.stack([core, row // 2, chan % 2, (chan // 2) % 2, chan // 4]).astype(jnp.int32)
        bit_x, bit_y = scal[1], scal[2]
        bit_a = jnp.where(core == 0, bit_x, bit_y).reshape(1)
        bit_b = jnp.where(core == 0, bit_y, bit_x).reshape(1)
        bit_low, bit_high = scal[3:4], scal[4:5]
        devices = [(r, c) for r in range(row_n) for c in range(chan_n)]
        flip_x = lambda r, c: (r ^ 2, c)
        flip_y = lambda r, c: (r, c ^ 1)
        moves = dict(
            core=lambda r, c: (r ^ 1, c),
            a=lambda r, c: flip_y(r, c) if r % 2 else flip_x(r, c),
            b=lambda r, c: flip_x(r, c) if r % 2 else flip_y(r, c),
            low=lambda r, c: (r, c ^ 2),
            high=lambda r, c: (r, c ^ 4),
            ab=lambda r, c: (r ^ 2, c ^ 1),
            z=lambda r, c: (r, c ^ 6),
        )

        def send(value, way):
            to = [moves[way](r, c) for r, c in devices]
            pairs = [(r * chan_n + c, t[0] * chan_n + t[1]) for (r, c), t in zip(devices, to)]
            return lax.ppermute(value, ("row", "chan"), pairs)

        after = lax.optimization_barrier
        trade = lambda v: lax.all_to_all(v, "chan", split_axis=0, concat_axis=0, tiled=True)
        rows = own * chan_n // T
        to_seq = lambda v: v.reshape(rows, inner // chan_n, T)
        to_tok = lambda v: v.reshape(chan_n, own // T, inner // chan_n, T)

        masks = ssm_masks(starts)
        grad_oth = send(out_grad, "core")
        normed, v_act, v_slope = norm_call(tokens, layer_norm_gain, ln_bias, w_val, chan_n)
        normed_oth = send(normed, "core")
        v_chan = to_seq(trade(v_act))
        u_act, d_slope, d_yproj, normed_t, dy_own, dy_oth, pair_grad = gate_call(
            scal, normed, normed_oth, out_grad, grad_oth, w_up, w_mix, w_down, row_n, chan_n
        )
        d_y = (dy_own + send(dy_oth, "core").astype(f32)).astype(bf16)
        v_chan, d_y = after((v_chan, d_y))
        d_y_chan = to_seq(trade(d_y))
        y_chan, states, toeplitz = ssm_fwd(v_chan, decay_rate, mix_coef, masks)
        y_chan, d_y_chan = after((y_chan, d_y_chan))
        y_own = trade(to_tok(y_chan))
        d_v_chan, d_rate, d_coef = ssm_bwd(
            v_chan, d_y_chan, decay_rate, mix_coef, masks, states, toeplitz
        )
        y_own, d_v_chan = after((y_own, d_v_chan))
        y_oth = send(y_own, "core")
        y_oth, d_v_chan = after((y_oth, d_v_chan))
        d_v = trade(to_tok(d_v_chan))
        gate_out, d_upre, u_give, u_keep, m_give, m_keep = mid_call(
            scal, y_own, y_oth, w_mix, u_act, d_slope, d_yproj, normed_t, row_n
        )
        u_give, m_give, gate_out, d_v, d_rate, d_coef = after(
            (u_give, m_give, gate_out, d_v, d_rate, d_coef)
        )

        u_got = send(u_give, "a")
        m_got = send(m_give, "low")
        rates = lax.psum_scatter(
            jnp.concatenate([d_rate, d_coef], 0), "row", scatter_dimension=1, tiled=True
        )
        half = chan_n // 2
        other_half = lambda v: lax.dynamic_slice_in_dim(v, (1 - core) * half, half, 0)
        v_give = (other_half(d_v).astype(f32) * other_half(v_slope)).astype(bf16)
        v_got = send(v_give, "core")
        d_vpre = (d_v.astype(f32) * v_slope).astype(bf16)
        down = mm(gate_out, pair_grad, TN).astype(bf16)
        d_give, d_keep = down_val_call(scal, down, d_vpre, v_got, normed_t)
        u_got, m_got, d_give, gate_out = after((u_got, m_got, d_give, gate_out))

        d_got = send(d_give, "a")
        m_give, m_keep = step_call(bit_high, m_keep, m_got)
        m_got = send(m_give, "high")
        u_give, u_keep = step_call(bit_b, u_keep, u_got)
        block_own, dn_own, bd_give = block_call(scal, gate_out, d_upre, w_down, w_up, row_n)
        d_got, m_got, u_give, bd_give = after((d_got, m_got, u_give, bd_give))

        u_got = send(u_give, "b")
        bd_got = send(bd_give, "core")
        d_give, d_keep = step_call(bit_b, d_keep, d_got)
        u_got, d_give, bd_got = after((u_got, d_give, bd_got))

        d_got = send(d_give, "b")
        u_give, u_keep = step_call(bit_low, u_keep, u_got)
        u_got = send(u_give, "low")
        m_give, m_keep = step_call(bit_a, m_keep, m_got)
        block_out, tokens_grad, norm_part = tail_call(
            tokens, out_grad, layer_norm_gain, block_own, bd_got, dn_own, d_vpre, w_val,
            row_n * chan_n,
        )
        d_got, u_got, m_give, norm_part = after((d_got, u_got, m_give, norm_part))

        d_give, d_keep = step_call(bit_low, d_keep, d_got)
        d_got = send(d_give, "low")
        u_give, u_keep = step_call(bit_high, u_keep, u_got)
        u_got = send(u_give, "high")
        m_got = send(m_give, "a")
        norm_part = norm_part + send(norm_part, "a") + send(norm_part, "b") + send(norm_part, "ab")
        d_got, m_got, u_got, norm_part = after((d_got, m_got, u_got, norm_part))

        d_give, d_keep = step_call(bit_high, d_keep, d_got)
        d_got = send(d_give, "high")
        m_give, m_keep = step_call(bit_b, m_keep, m_got)
        m_got = send(m_give, "b")
        norm_part = (
            norm_part + send(norm_part, "low") + send(norm_part, "high") + send(norm_part, "z")
        )
        d_got, m_got, norm_part = after((d_got, m_got, norm_part))

        down_grad, mine, other = finish_call(
            scal, (u_keep, u_got), (m_keep, m_got), (d_keep, d_got)
        )
        um, mx = u_keep.shape[1], m_keep.shape[1]
        other = send(other, "core")
        norm_part = norm_part + send(norm_part, "core")
        up_grad, mix_grad, val_grad = join_call(scal, mine, other, um, mx, inner)
        norm_sum = lax.dynamic_index_in_dim(norm_part, row * chan_n + chan, 0, keepdims=False)
        w = width // (row_n * chan_n)
        return (
            block_out,
            tokens_grad,
            norm_sum[:w],
            norm_sum[w : 2 * w],
            up_grad,
            val_grad,
            mix_grad,
            down_grad,
            rates[: decay_rate.shape[0]],
            rates[decay_rate.shape[0] :],
        )

    return on_device


def make_general(row_n, chan_n):
    row_hi = row_n // 2

    def swap(value, axis, bit):
        size = row_n if axis == "row" else chan_n
        return lax.ppermute(value, axis, [(i, i ^ (1 << bit)) for i in range(size)])

    def core_swap(value):
        return swap(value, "row", 0)

    def bits_of(size):
        return size.bit_length() - 1

    def scatter_sum(part, names, order, last_dtype):
        names = list(names)
        for step, name in enumerate(order):
            axis, bit = name
            dim = names.index(name)
            mine = (lax.axis_index(axis) >> bit) & 1
            keep = lax.dynamic_index_in_dim(part, mine, dim, keepdims=False)
            give = lax.dynamic_index_in_dim(part, 1 - mine, dim, keepdims=False)
            got = swap(give, axis, bit)
            part = keep.astype(jnp.float32) + got.astype(jnp.float32)
            if step < len(order) - 1:
                part = part.astype(give.dtype)
            else:
                part = part.astype(last_dtype)
            names.pop(dim)
        return part

    row_bits = [("row", k) for k in range(bits_of(row_n) - 1, 0, -1)]
    core_bit = ("row", 0)
    chan_bits = [("chan", k) for k in range(bits_of(chan_n) - 1, -1, -1)]
    near_y = chan_bits[2:]
    along_z = chan_bits[:2][::-1]

    def on_device(
        tokens,
        starts,
        layer_norm_gain,
        ln_bias,
        w_up,
        w_val,
        w_mix,
        w_down,
        decay_rate,
        mix_coef,
        out_grad,
    ):
        own, width = tokens.shape
        ff = w_up.shape[1]
        inner = w_val.shape[1]
        part_ff = ff // row_n
        core = lax.axis_index("row") % 2
        mm = lambda a, b, ca, cb: lax.dot_general(
            a, b, (((ca,), (cb,)), ((), ())), preferred_element_type=jnp.float32
        )
        masks = ssm_masks(starts)
        inputs_f = tokens.astype(jnp.float32)
        row_mean = jnp.mean(inputs_f, axis=1, keepdims=True)
        centred = inputs_f - row_mean
        inv_std = lax.rsqrt(jnp.mean(centred * centred, axis=1, keepdims=True) + epsilon)
        x_hat = centred * inv_std
        normed = (x_hat * layer_norm_gain + ln_bias).astype(jnp.bfloat16)
        v_pre = mm(w_val, normed, 0, 1)
        v_cdf = gauss_cdf(v_pre)
        v_act = (v_pre * v_cdf).astype(jnp.bfloat16)
        v_slope = v_cdf + v_pre * gauss_pdf(v_pre)
        v_chan = lax.all_to_all(
            v_act.reshape(inner, own // T, T), "chan", split_axis=0, concat_axis=1, tiled=True
        )
        v_chan = jnp.swapaxes(v_chan, 0, 1)
        pair_normed = jnp.concatenate([normed, core_swap(normed)], 0)
        pair_grad = jnp.concatenate([out_grad, core_swap(out_grad)], 0)
        halves = lambda w, d: lax.dynamic_index_in_dim(
            w.reshape(w.shape[:d] + (row_hi, 2, part_ff) + w.shape[d + 1 :]), core, d + 1, keepdims=False
        ).reshape(w.shape[:d] + (ff // 2,) + w.shape[d + 1 :])
        up_half = halves(w_up, 1)
        mix_half = halves(w_mix, 1)
        down_half = halves(w_down, 0)
        u_pre = mm(pair_normed, up_half, 1, 0)
        d_gate = mm(pair_grad, down_half, 1, 1)
        u_cdf = gauss_cdf(u_pre)
        u_act = u_pre * u_cdf
        d_yproj = (d_gate * u_act).astype(jnp.bfloat16)
        d_slope = d_gate * (u_cdf + u_pre * gauss_pdf(u_pre))
        d_y_part = mm(mix_half, d_yproj, 1, 1)
        d_y = (
            d_y_part[:, :own] + core_swap(d_y_part[:, own:].astype(jnp.bfloat16)).astype(jnp.float32)
        ).astype(jnp.bfloat16)
        d_y_chan = lax.all_to_all(
            d_y.reshape(inner, own // T, T), "chan", split_axis=0, concat_axis=1, tiled=True
        )
        d_y_chan = jnp.swapaxes(d_y_chan, 0, 1)
        y_chan, states, toeplitz = ssm_fwd(v_chan, decay_rate, mix_coef, masks)
        y_chan = jnp.swapaxes(y_chan, 0, 1)
        y_own = lax.all_to_all(y_chan, "chan", split_axis=1, concat_axis=0, tiled=True)
        y_own = y_own.reshape(inner, own)
        d_v_chan, d_rate, d_coef = ssm_bwd(
            v_chan, d_y_chan, decay_rate, mix_coef, masks, states, toeplitz
        )
        d_v_chan = jnp.swapaxes(d_v_chan, 0, 1)
        d_v = lax.all_to_all(d_v_chan, "chan", split_axis=1, concat_axis=0, tiled=True)
        pair_y = jnp.concatenate([y_own, core_swap(y_own)], 1)
        split_rows = lambda a, lead: a.reshape((2,) * lead + (-1,) + a.shape[1:])
        y_proj = mm(pair_y, mix_half, 0, 0)
        gate_out = (u_act * y_proj).astype(jnp.bfloat16)
        d_upre = (d_slope * y_proj).astype(jnp.bfloat16)
        mix_part = mm(pair_y, d_yproj, 1, 0).astype(jnp.bfloat16)
        down_part = mm(gate_out, pair_grad, 0, 0).astype(jnp.bfloat16)
        up_part = mm(pair_normed, d_upre, 0, 0).astype(jnp.bfloat16)
        all_names = row_bits + [core_bit] + chan_bits
        no_core = row_bits + chan_bits
        lead = len(all_names)
        mix_sum = scatter_sum(
            split_rows(mix_part, lead), all_names, along_z + row_bits + near_y, jnp.float32
        )
        up_sum = scatter_sum(
            split_rows(up_part, lead), all_names, row_bits + near_y + along_z, jnp.float32
        )
        down_grad = scatter_sum(
            split_rows(down_part, lead - 1), no_core, near_y + row_bits + along_z, jnp.float32
        )

        def join_cores(halfsum):
            mine = lax.dynamic_index_in_dim(halfsum, core, 0, keepdims=False)
            other = core_swap(lax.dynamic_index_in_dim(halfsum, 1 - core, 0, keepdims=False))
            shape = (mine.shape[0], row_hi, part_ff)
            low = jnp.where(core == 0, mine, other).reshape(shape)
            high = jnp.where(core == 0, other, mine).reshape(shape)
            return jnp.stack([low, high], 2).reshape(mine.shape[0], ff)

        block_part = mm(gate_out, down_half, 1, 0)
        block_out = (
            inputs_f
            + block_part[:own]
            + core_swap(block_part[own:].astype(jnp.bfloat16)).astype(jnp.float32)
        ).astype(jnp.bfloat16)
        d_normed_part = mm(d_upre, up_half, 1, 1)
        d_normed_got = core_swap(d_normed_part[own:].astype(jnp.bfloat16)).astype(jnp.float32)
        d_vpre = (d_v.reshape(inner, own).astype(jnp.float32) * v_slope).astype(jnp.bfloat16)
        val_part = mm(normed, d_vpre, 0, 1).astype(jnp.bfloat16)
        val_grad = scatter_sum(
            split_rows(val_part, lead),
            all_names,
            [core_bit] + along_z + near_y + row_bits,
            jnp.float32,
        )
        d_normed = d_normed_part[:own] + d_normed_got + mm(d_vpre, w_val, 0, 1)
        norm_part = jnp.stack([jnp.sum(d_normed * x_hat, axis=0), jnp.sum(d_normed, axis=0)], 1)
        norm_sum = scatter_sum(
            split_rows(norm_part, lead), all_names, [core_bit] + row_bits + chan_bits, jnp.float32
        )
        d_xh = d_normed * layer_norm_gain
        tokens_grad = out_grad.astype(jnp.float32) + inv_std * (
            d_xh
            - jnp.mean(d_xh, axis=1, keepdims=True)
            - x_hat * jnp.mean(d_xh * x_hat, axis=1, keepdims=True)
        )
        row_all = row_bits + [core_bit]
        states_n = decay_rate.shape[1]
        rates = jnp.stack([d_rate, d_coef]).reshape(
            (2 * d_rate.shape[0],) + (2,) * len(row_all) + (states_n // row_n,)
        )
        rates = jnp.moveaxis(rates, 0, len(row_all))
        rates = scatter_sum(rates, row_all, [core_bit] + row_bits, jnp.float32)
        rates = rates.reshape(2, d_rate.shape[0], states_n // row_n)
        return (
            block_out,
            tokens_grad,
            norm_sum[:, 0],
            norm_sum[:, 1],
            join_cores(up_sum),
            val_grad,
            join_cores(mix_sum),
            down_grad,
            rates[0],
            rates[1],
        )

    return on_device


def solution(mesh):
    spread = P(("row", "chan"), None)
    row_n, chan_n = mesh.shape["row"], mesh.shape["chan"]
    make = make_square if (row_n, chan_n) == (4, 8) else make_general
    return jax.shard_map(
        make(row_n, chan_n),
        mesh=mesh,
        in_specs=(
            spread,
            P("row", None),
            P(),
            P(),
            P(),
            P(),
            P(),
            P(),
            P("chan", None),
            P("chan", None),
            spread,
        ),
        out_specs=(
            spread,
            spread,
            P(("row", "chan")),
            P(("row", "chan")),
            spread,
            spread,
            spread,
            spread,
            P("chan", "row"),
            P("chan", "row"),
        ),
        check_vma=False,
    )
```

profile of v0, /device:TPU:0, one launch (start us, length us, event | category | flops | bytes accessed | tf_op | source)
XLA Modules:
  0.0 228.0 jit_solution(13141883482259154525)
XLA Ops:
  7.7 5.1 %norm_val.1 = (bf16[512,1024]{1,0:T(8,128)(2,1)S(1)}, bf16[8,4,64,128]{3,2,1,0:T(8,128)(2,1)}, f32[8,4,64,128]{3,2,1,0:T(8,128)S(1)}) custom-call(bf16[512,1024]{1,0:T(8,128)(2,1)} %tok.3, f32[1,1024]{1,0:T(1,128)} %bitcast.81, f32[1,1024]{1,0:T(1,128)} %bitcast.83, bf16[1024,512]{1,0:T(8,128)(2,1)} %w_val.3), custom_call_target="tpu_custom_call" | custom-call | tf_op jit(solution)/shard_map/norm_val/pallas_call | solution.py:360
  12.9 7.3 %all-to-all-start = ((bf16[8,4,64,128]{3,2,1,0:T(8,128)(2,1)}), bf16[8,4,64,128]{3,2,1,0:T(8,128)(2,1)S(1)}, u32[]{:S(2)}, u32[]{:S(2)}) async-start(bf16[8,4,64,128]{3,2,1,0:T(8,128)(2,1)} %get-tuple-element.100), calls=%async_computation | async-start | bytes 1048576 | tf_op jit(solution)/shard_map/all_to_all | solution.py:873
  21.1 18.6 %gate.1 = (bf16[1024,1536]{1,0:T(8,128)(2,1)}, bf16[1024,1536]{1,0:T(8,128)(2,1)}, bf16[1024,1536]{1,0:T(8,128)(2,1)}, bf16[1024,1024]{1,0:T(8,128)(2,1)}, f32[8...) custom-call(s32[5]{0:T(128)} %stack.23.core.s, bf16[512,1024]{1,0:T(8,128)(2,1)} %copy-done.6, ...), custom_call_target="tpu_custom_call" | custom-call | tf_op jit(solution)/shard_map/gate/pallas_call | solution.py:360
  43.6 2.2 add_convert_fusion
  45.8 6.0 %all-to-all-start.1 = ((bf16[8,4,64,128]{3,2,1,0:T(8,128)(2,1)}), bf16[8,4,64,128]{3,2,1,0:T(8,128)(2,1)S(1)}, u32[]{:S(2)}, u32[]{:S(2)}) async-start(bf16[8,4,64,128]{3,2,1,0:T(8,128)(2,1)} %add_convert_fusion), calls=%async_computation.1 | async-start | bytes 1048576 | tf_op jit(solution)/shard_map/all_to_all | solution.py:873
  51.8 13.7 %ssm_fwd.1 = (bf16[32,64,128]{2,1,0:T(8,128)(2,1)}, f32[8,4,256,128]{3,2,1,0:T(8,128)}, bf16[64,128,128]{2,1,0:T(8,128)(2,1)}) custom-call(s32[1]{0:T(128)} %bitcast.8.groups, f32[32]{0:T(128)S(1)} %convert_reduce_fusion.keep, bf16[32,64,128]{2,1,0:T(8,128)(2,1)S(1)} %bitcast.73, f32[64,512]{1,0:T(8,128)S(1)} %copy-done.9, f32[64,512]{1,0:T(8,128)S(1)} %copy-done.10, ...), custom_call_target="tpu_custom_call" | custom-call | flops 20000000000 | bytes 10000000 | tf_op jit(solution)/shard_map/ssm_fwd/pallas_call | solution.py:280
  67.0 4.6 %all-to-all-start.2 = ((bf16[8,4,64,128]{3,2,1,0:T(8,128)(2,1)}), bf16[8,4,64,128]{3,2,1,0:T(8,128)(2,1)S(1)}, u32[]{:S(2)}, u32[]{:S(2)}) async-start(bf16[8,4,64,128]{3,2,1,0:T(8,128)(2,1)} %bitcast.77), calls=%async_computation.2 | async-start | bytes 1048576 | tf_op jit(solution)/shard_map/all_to_all | solution.py:873
  71.5 18.6 %ssm_bwd.1 = (bf16[32,64,128]{2,1,0:T(8,128)(2,1)}, f32[64,512]{1,0:T(8,128)}, f32[64,512]{1,0:T(8,128)}) custom-call(s32[1]{0:T(128)} %bitcast.8.groups, f32[32]{0:T(128)S(1)} %convert_reduce_fusion.keep, bf16[32,64,128]{2,1,0:T(8,128)(2,1)S(1)} %bitcast.74, bf16[32,64,128]{2,1,0:T(8,128)(2,1)S(1)} %bitcast.75, f32[64,512]{1,0:T(8,128)S(1)} %copy-done.9, ...), custom_call_target="tpu_custom_call" | custom-call | flops 20000000000 | bytes 10000000 | tf_op jit(solution)/shard_map/ssm_bwd/pallas_call | solution.py:301
  90.2 1.9 collective-permute-done.3.y_oth
  92.1 6.0 %all-to-all-start.3 = ((bf16[8,4,64,128]{3,2,1,0:T(8,128)(2,1)}), bf16[8,4,64,128]{3,2,1,0:T(8,128)(2,1)S(1)}, u32[]{:S(2)}, u32[]{:S(2)}) async-start(bf16[8,4,64,128]{3,2,1,0:T(8,128)(2,1)} %bitcast.76), calls=%async_computation.3 | async-start | bytes 1048576 | tf_op jit(solution)/shard_map/all_to_all | solution.py:873
  98.2 14.6 %mix_up.1 = (bf16[1024,1536]{1,0:T(8,128)(2,1)}, bf16[1024,1536]{1,0:T(8,128)(2,1)}, bf16[16,32,1536]{2,1,0:T(8,128)(2,1)}, bf16[16,32,1536]{2,1,0:T(8,128)(2,1)...) custom-call(s32[5]{0:T(128)} %stack.23.core.s, bf16[8,4,64,128]{3,2,1,0:T(8,128)(2,1)} %copy-done.12, ...), custom_call_target="tpu_custom_call" | custom-call | flops 10000000000 | bytes 10000000 | tf_op jit(solution)/shard_map/mix_up/pallas_call | solution.py:360
  112.9 1.5 collective-permute-start.4
  114.6 2.0 collective-permute-start.5
  116.5 6.0 %convolution_convert_fusion.down_g.down_k = bf16[1536,1024]{1,0:T(8,128)(2,1)S(1)} fusion(bf16[1024,1536]{1,0:T(8,128)(2,1)} %get-tuple-element.132.gate, bf16[1024,1024]{1,0:T(8,128)(2,1)} %get-tuple-element.128), kind=kOutput, calls=%fused_computation | convolution fusion | flops 3222798336 | bytes 8388608 | tf_op jit(solution)/shard_map/dot_general | solution.py:20
  122.7 1.6 copy-done.3
  124.3 4.4 %down_val.1 = (bf16[8,112,1024]{2,1,0:T(8,128)(2,1)}, bf16[8,112,1024]{2,1,0:T(8,128)(2,1)S(1)}) custom-call(s32[5]{0:T(128)S(1)} %copy-done.7, bf16[1536,1024]{1,0:T(8,128)(2,1)S(1)} %convolution_convert_fusion.down_g.down_k, bf16[1536,1024]{1,0:T(8,128)(2,1)S(1)} %convolution_convert_fusion.down_g.down_k, ...), custom_call_target="tpu_custom_call" | custom-call | tf_op jit(solution)/shard_map/down_val/pallas_call | solution.py:360
  128.8 6.1 %collective-permute-done.5 = bf16[16,16,1536]{2,1,0:T(8,128)(2,1)S(1)} collective-permute-done((bf16[16,16,1536]{2,1,0:T(8,128)(2,1)}, bf16[16,16,1536]{2,1,0:T(8,128)(2,1)S(1)}, u32[]{:S(2)}, u32[]{:S(2)}) %collective-permute-start.5) | collective-permute-done | bytes 786464 | tf_op jit(solution)/shard_map/ppermute | solution.py:870
  137.6 2.6 %collective-permute-start.8 = (bf16[8,16,1536]{2,1,0:T(8,128)(2,1)}, bf16[8,16,1536]{2,1,0:T(8,128)(2,1)}, u32[]{:S(2)}, u32[]{:S(2)}) collective-permute-start(bf16[8,16,1536]{2,1,0:T(8,128)(2,1)} %get-tuple-element.138), channel_id=1, source_target_pairs={{0,4},{1,5},{2,6},{3,7},{4,0},{5,1},{6,2},{7,3},{8,12},{9,13},{10,... | collective-permute-start | bytes 1179656 | tf_op jit(solution)/shard_map/ppermute | solution.py:870
  140.2 14.7 %block.1 = (f32[512,1024]{1,0:T(8,128)}, f32[512,1024]{1,0:T(8,128)}, bf16[2,512,1024]{2,1,0:T(8,128)(2,1)}) custom-call(s32[5]{0:T(128)} %stack.23.core.s, bf16[1024,1536]{1,0:T(8,128)(2,1)} %get-tuple-element.132.gate, bf16[1024,1536]{1,0:T(8,128)(2,1)} %get-tuple-element.133.d_upre, bf16[3072,1024]{1,0:T(8,128)(2,1)} %w_down.3, bf16[1024,3072]{1,0:T(8,128)(2,1)} %w_up.3), custom_call_target="tpu_custom_call" | custom-call | tf_op jit(solution)/shard_map/block/pallas_call | solution.py:360
  155.3 3.5 %collective-permute-done.8 = bf16[8,16,1536]{2,1,0:T(8,128)(2,1)} collective-permute-done((bf16[8,16,1536]{2,1,0:T(8,128)(2,1)}, bf16[8,16,1536]{2,1,0:T(8,128)(2,1)}, u32[]{:S(2)}, u32[]{:S(2)}) %collective-permute-start.8) | collective-permute-done | bytes 393248 | tf_op jit(solution)/shard_map/ppermute | solution.py:870
  160.2 3.7 %halve.11 = (bf16[4,112,1024]{2,1,0:T(8,128)(2,1)}, bf16[4,112,1024]{2,1,0:T(8,128)(2,1)S(1)}) custom-call(s32[1]{0:T(128)} %bitcast.16.bit, bf16[2,4,112,1024]{3,2,1,0:T(8,128)(2,1)S(1)} %bitcast.41, bf16[2,4,112,1024]{3,2,1,0:T(8,128)(2,1)} %bitcast.20.got_g.got_k, bf16[2,4,112,1024]{3,2,1,0:T(8,128)(2,1)S(1)} %bitcast.42, ...), custom_call_target="tpu_custom_call" | custom-call | tf_op jit(solution)/shard_map/halve/pallas_call | solution.py:360
  163.8 7.0 %collective-permute-done.9 = bf16[8,32,1536]{2,1,0:T(8,128)(2,1)S(1)} collective-permute-done((bf16[8,32,1536]{2,1,0:T(8,128)(2,1)S(1)}, bf16[8,32,1536]{2,1,0:T(8,128)(2,1)S(1)}, u32[]{:S(2)}, u32[]{:S(2)}) %collective-permute-start.9) | collective-permute-done | bytes 786464 | tf_op jit(solution)/shard_map/ppermute | solution.py:870
  175.0 1.8 halve.13
  176.8 7.3 %norm_back.1 = (bf16[512,1024]{1,0:T(8,128)(2,1)}, f32[512,1024]{1,0:T(8,128)}, f32[32,128]{1,0:T(8,128)S(1)}) custom-call(bf16[512,1024]{1,0:T(8,128)(2,1)} %tok.3, bf16[512,1024]{1,0:T(8,128)(2,1)} %grad.1, f32[1,1024]{1,0:T(1,128)} %bitcast.82, f32[512,1024]{1,0:T(8,128)} %get-tuple-element.134.block_own, bf16[2,512,1024]{2,1,0:T(8,128)(2,1)} %copy-done.11, ...), custom_call_target="tpu_custom_call" | custom-call | tf_op jit(solution)/shard_map/norm_back/pallas_call | solution.py:360
  187.4 1.5 collective-permute-start.18
  189.4 1.5 collective-permute-start.16
  191.1 2.6 %collective-permute-start.15 = (bf16[2,32,1536]{2,1,0:T(8,128)(2,1)S(1)}, bf16[2,32,1536]{2,1,0:T(8,128)(2,1)S(1)}, u32[]{:S(2)}, u32[]{:S(2)}) collective-permute-start(bf16[2,32,1536]{2,1,0:T(8,128)(2,1)S(1)} %get-tuple-element.167), channel_id=1, source_target_pairs={{0,4},{1,5},{2,6},{3,7},{4,0},{5,1},{6,2},{7,3},{8,12},{9,13},{10,... | collective-permute-start | bytes 589832 | tf_op jit(solution)/shard_map/ppermute | solution.py:870
  194.2 5.6 %collective-permute-done.15.u_got = bf16[2,32,1536]{2,1,0:T(8,128)(2,1)S(1)} collective-permute-done((bf16[2,32,1536]{2,1,0:T(8,128)(2,1)S(1)}, bf16[2,32,1536]{2,1,0:T(8,128)(2,1)S(1)}, u32[]{:S(2)}, u32[]{:S(2)}) %collective-permute-start.15) | collective-permute-done | bytes 196640 | tf_op jit(solution)/shard_map/ppermute | solution.py:870
  200.9 3.3 %collective-permute-start.23 = (f32[32,128]{1,0:T(8,128)S(1)}, f32[32,128]{1,0:T(8,128)S(1)}, u32[]{:S(2)}, u32[]{:S(2)}) collective-permute-start(f32[32,128]{1,0:T(8,128)S(1)} %add_add_fusion.1), channel_id=1, source_target_pairs={{0,6},{1,7},{2,4},{3,5},{4,2},{5,3},{6,0},{7,1},{8,14},{9,15},{10,... | collective-permute-start | bytes 49160 | tf_op jit(solution)/shard_map/ppermute | solution.py:870
  205.4 1.9 collective-permute-start.19
  209.7 2.4 %collective-permute-done.20.m_got = bf16[2,16,1536]{2,1,0:T(8,128)(2,1)S(1)} collective-permute-done((bf16[2,16,1536]{2,1,0:T(8,128)(2,1)S(1)}, bf16[2,16,1536]{2,1,0:T(8,128)(2,1)S(1)}, u32[]{:S(2)}, u32[]{:S(2)}) %collective-permute-start.20) | collective-permute-done | bytes 98336 | tf_op jit(solution)/shard_map/ppermute | solution.py:870
  212.1 3.8 %collective-permute-done.19.d_got = bf16[1,112,1024]{2,1,0:T(8,128)(2,1)S(1)} collective-permute-done((bf16[1,112,1024]{2,1,0:T(8,128)(2,1)S(1)}, bf16[1,112,1024]{2,1,0:T(8,128)(2,1)S(1)}, u32[]{:S(2)}, u32[]{:S(2)}) %collective-permute-start.19) | collective-permute-done | bytes 229408 | tf_op jit(solution)/shard_map/ppermute | solution.py:870
  (103 shorter events, 28.0 us)
Async XLA Ops:
  7.2 13.9 %collective-permute-start.1 = (bf16[512,1024]{1,0:T(8,128)(2,1)}, bf16[512,1024]{1,0:T(8,128)(2,1)}, u32[]{:S(2)}, u32[]{:S(2)}) collective-permute-start(bf16[512,1024]{1,0:T(8,128)(2,1)} %grad.1), channel_id=1, source_target_pairs={{0,8},{1,9},{2,10},{3,11},{4,12},{5,13},{6,14},{7,15},{8,0},{9,1},... | collective-permute-start | bytes 3145736 | tf_op jit(solution)/shard_map/ppermute | solution.py:870
  12.9 8.3 %collective-permute-start = (bf16[512,1024]{1,0:T(8,128)(2,1)S(1)}, bf16[512,1024]{1,0:T(8,128)(2,1)}, u32[]{:S(2)}, u32[]{:S(2)}) collective-permute-start(bf16[512,1024]{1,0:T(8,128)(2,1)S(1)} %get-tuple-element.101.n_own), channel_id=1, source_target_pairs={{0,8},{1,9},{2,10},{3,11},{4,12},{5,13},{6,14},{7,15},{8,0},{9,1},... | collective-permute-start | bytes 3145736 | tf_op jit(solution)/shard_map/ppermute | solution.py:870
  12.9 32.9 %all-to-all-start = ((bf16[8,4,64,128]{3,2,1,0:T(8,128)(2,1)}), bf16[8,4,64,128]{3,2,1,0:T(8,128)(2,1)S(1)}, u32[]{:S(2)}, u32[]{:S(2)}) async-start(bf16[8,4,64,128]{3,2,1,0:T(8,128)(2,1)} %get-tuple-element.100), calls=%async_computation | async-start | bytes 1048576 | tf_op jit(solution)/shard_map/all_to_all | solution.py:873
  39.8 3.9 %collective-permute-start.2 = (bf16[8,4,64,128]{3,2,1,0:T(8,128)(2,1)}, bf16[8,4,64,128]{3,2,1,0:T(8,128)(2,1)S(1)}, u32[]{:S(2)}, u32[]{:S(2)}) collective-permute-start(bf16[8,4,64,128]{3,2,1,0:T(8,128)(2,1)} %get-tuple-element.103), channel_id=1, source_target_pairs={{0,8},{1,9},{2,10},{3,11},{4,12},{5,13},{6,14},{7,15},{8,0},{9,1},... | collective-permute-start | bytes 1572872 | tf_op jit(solution)/shard_map/ppermute | solution.py:870
  45.8 21.1 %all-to-all-start.1 = ((bf16[8,4,64,128]{3,2,1,0:T(8,128)(2,1)}), bf16[8,4,64,128]{3,2,1,0:T(8,128)(2,1)S(1)}, u32[]{:S(2)}, u32[]{:S(2)}) async-start(bf16[8,4,64,128]{3,2,1,0:T(8,128)(2,1)} %add_convert_fusion), calls=%async_computation.1 | async-start | bytes 1048576 | tf_op jit(solution)/shard_map/all_to_all | solution.py:873
  67.0 23.2 %all-to-all-start.2 = ((bf16[8,4,64,128]{3,2,1,0:T(8,128)(2,1)}), bf16[8,4,64,128]{3,2,1,0:T(8,128)(2,1)S(1)}, u32[]{:S(2)}, u32[]{:S(2)}) async-start(bf16[8,4,64,128]{3,2,1,0:T(8,128)(2,1)} %bitcast.77), calls=%async_computation.2 | async-start | bytes 1048576 | tf_op jit(solution)/shard_map/all_to_all | solution.py:873
  90.1 2.0 collective-permute-start.3
  92.1 20.8 %all-to-all-start.3 = ((bf16[8,4,64,128]{3,2,1,0:T(8,128)(2,1)}), bf16[8,4,64,128]{3,2,1,0:T(8,128)(2,1)S(1)}, u32[]{:S(2)}, u32[]{:S(2)}) async-start(bf16[8,4,64,128]{3,2,1,0:T(8,128)(2,1)} %bitcast.76), calls=%async_computation.3 | async-start | bytes 1048576 | tf_op jit(solution)/shard_map/all_to_all | solution.py:873
  98.1 119.6 %reduce-scatter.2.cloned.1.call-start = ((), (), s32[]{:S(2)}) async-start(), calls=%async_computation.5 | async-start | bytes 327680 | tf_op jit(solution)/shard_map/reduce_scatter | solution.py:908
  112.9 21.9 %collective-permute-start.4 = (bf16[16,32,1536]{2,1,0:T(8,128)(2,1)}, bf16[16,32,1536]{2,1,0:T(8,128)(2,1)S(1)}, u32[]{:S(2)}, u32[]{:S(2)}) collective-permute-start(bf16[16,32,1536]{2,1,0:T(8,128)(2,1)} %get-tuple-element.125), channel_id=1, source_target_pairs={{0,16},{1,17},{2,18},{3,19},{4,20},{5,21},{6,22},{7,23},{8,9},{9,8... | collective-permute-start | bytes 4718600 | tf_op jit(solution)/shard_map/ppermute | solution.py:870
  114.5 8.2 %collective-permute-start.6 = (bf16[4,4,64,128]{3,2,1,0:T(8,128)(2,1)S(1)}, bf16[4,4,64,128]{3,2,1,0:T(8,128)(2,1)S(1)}, u32[]{:S(2)}, u32[]{:S(2)}) collective-permute-start(bf16[4,4,64,128]{3,2,1,0:T(8,128)(2,1)S(1)} %multiply_convert_fusion.1), channel_id=1, source_target_pairs={{0,8},{1,9},{2,10},{3,11},{4,12},{5,13},{6,14},{7,15},{8,0},{9,1},... | collective-permute-start | bytes 786440 | tf_op jit(solution)/shard_map/ppermute | solution.py:870
  114.6 20.3 %collective-permute-start.5 = (bf16[16,16,1536]{2,1,0:T(8,128)(2,1)}, bf16[16,16,1536]{2,1,0:T(8,128)(2,1)S(1)}, u32[]{:S(2)}, u32[]{:S(2)}) collective-permute-start(bf16[16,16,1536]{2,1,0:T(8,128)(2,1)} %get-tuple-element.126), channel_id=1, source_target_pairs={{0,2},{1,3},{2,0},{3,1},{4,6},{5,7},{6,4},{7,5},{8,10},{9,11},{10,... | collective-permute-start | bytes 2359304 | tf_op jit(solution)/shard_map/ppermute | solution.py:870
  134.9 23.9 %collective-permute-start.7 = (bf16[8,112,1024]{2,1,0:T(8,128)(2,1)}, bf16[8,112,1024]{2,1,0:T(8,128)(2,1)}, u32[]{:S(2)}, u32[]{:S(2)}) collective-permute-start(bf16[8,112,1024]{2,1,0:T(8,128)(2,1)} %get-tuple-element.135), channel_id=1, source_target_pairs={{0,16},{1,17},{2,18},{3,19},{4,20},{5,21},{6,22},{7,23},{8,9},{9,8... | collective-permute-start | bytes 5505032 | tf_op jit(solution)/shard_map/ppermute | solution.py:870
  137.6 21.2 %collective-permute-start.8 = (bf16[8,16,1536]{2,1,0:T(8,128)(2,1)}, bf16[8,16,1536]{2,1,0:T(8,128)(2,1)}, u32[]{:S(2)}, u32[]{:S(2)}) collective-permute-start(bf16[8,16,1536]{2,1,0:T(8,128)(2,1)} %get-tuple-element.138), channel_id=1, source_target_pairs={{0,4},{1,5},{2,6},{3,7},{4,0},{5,1},{6,2},{7,3},{8,12},{9,13},{10,... | collective-permute-start | bytes 1179656 | tf_op jit(solution)/shard_map/ppermute | solution.py:870
  158.8 12.1 %collective-permute-start.10 = (bf16[2,512,1024]{2,1,0:T(8,128)(2,1)S(1)}, bf16[2,512,1024]{2,1,0:T(8,128)(2,1)S(1)}, u32[]{:S(2)}, u32[]{:S(2)}) collective-permute-start(bf16[2,512,1024]{2,1,0:T(8,128)(2,1)S(1)} %copy-done.16), channel_id=1, source_target_pairs={{0,8},{1,9},{2,10},{3,11},{4,12},{5,13},{6,14},{7,15},{8,0},{9,1},... | collective-permute-start | bytes 6291464 | tf_op jit(solution)/shard_map/ppermute | solution.py:870
  158.8 12.1 %collective-permute-start.9 = (bf16[8,32,1536]{2,1,0:T(8,128)(2,1)S(1)}, bf16[8,32,1536]{2,1,0:T(8,128)(2,1)S(1)}, u32[]{:S(2)}, u32[]{:S(2)}) collective-permute-start(bf16[8,32,1536]{2,1,0:T(8,128)(2,1)S(1)} %get-tuple-element.143), channel_id=1, source_target_pairs={{0,1},{1,0},{2,3},{3,2},{4,5},{5,4},{6,7},{7,6},{8,24},{9,25},{10,... | collective-permute-start | bytes 2359304 | tf_op jit(solution)/shard_map/ppermute | solution.py:870
  170.9 13.6 %collective-permute-start.11 = (bf16[4,112,1024]{2,1,0:T(8,128)(2,1)}, bf16[4,112,1024]{2,1,0:T(8,128)(2,1)S(1)}, u32[]{:S(2)}, u32[]{:S(2)}) collective-permute-start(bf16[4,112,1024]{2,1,0:T(8,128)(2,1)} %get-tuple-element.153), channel_id=1, source_target_pairs={{0,1},{1,0},{2,3},{3,2},{4,5},{5,4},{6,7},{7,6},{8,24},{9,25},{10,... | collective-permute-start | bytes 2752520 | tf_op jit(solution)/shard_map/ppermute | solution.py:870
  173.6 10.5 %collective-permute-start.12 = (bf16[4,32,1536]{2,1,0:T(8,128)(2,1)}, bf16[4,32,1536]{2,1,0:T(8,128)(2,1)S(1)}, u32[]{:S(2)}, u32[]{:S(2)}) collective-permute-start(bf16[4,32,1536]{2,1,0:T(8,128)(2,1)} %get-tuple-element.156), channel_id=1, source_target_pairs={{0,2},{1,3},{2,0},{3,1},{4,6},{5,7},{6,4},{7,5},{8,10},{9,11},{10,... | collective-permute-start | bytes 1179656 | tf_op jit(solution)/shard_map/ppermute | solution.py:870
  185.4 15.6 %collective-permute-start.13 = (bf16[2,112,1024]{2,1,0:T(8,128)(2,1)}, bf16[2,112,1024]{2,1,0:T(8,128)(2,1)S(1)}, u32[]{:S(2)}, u32[]{:S(2)}) collective-permute-start(bf16[2,112,1024]{2,1,0:T(8,128)(2,1)} %get-tuple-element.163), channel_id=1, source_target_pairs={{0,2},{1,3},{2,0},{3,1},{4,6},{5,7},{6,4},{7,5},{8,10},{9,11},{10,... | collective-permute-start | bytes 1376264 | tf_op jit(solution)/shard_map/ppermute | solution.py:870
  187.4 6.3 %collective-permute-start.18 = (f32[32,128]{1,0:T(8,128)S(1)}, f32[32,128]{1,0:T(8,128)S(1)}, u32[]{:S(2)}, u32[]{:S(2)}) collective-permute-start(f32[32,128]{1,0:T(8,128)S(1)} %get-tuple-element.168), channel_id=1, source_target_pairs={{0,17},{1,16},{2,19},{3,18},{4,21},{5,20},{6,23},{7,22},{8,25},{9,... | collective-permute-start | bytes 49160 | tf_op jit(solution)/shard_map/ppermute | solution.py:870
  188.9 5.3 %collective-permute-start.17 = (f32[32,128]{1,0:T(8,128)S(1)}, f32[32,128]{1,0:T(8,128)S(1)}, u32[]{:S(2)}, u32[]{:S(2)}) collective-permute-start(f32[32,128]{1,0:T(8,128)S(1)} %get-tuple-element.168), channel_id=1, source_target_pairs={{0,1},{1,0},{2,3},{3,2},{4,5},{5,4},{6,7},{7,6},{8,24},{9,25},{10,... | collective-permute-start | bytes 49160 | tf_op jit(solution)/shard_map/ppermute | solution.py:870
  189.4 4.8 %collective-permute-start.16 = (f32[32,128]{1,0:T(8,128)S(1)}, f32[32,128]{1,0:T(8,128)S(1)}, u32[]{:S(2)}, u32[]{:S(2)}) collective-permute-start(f32[32,128]{1,0:T(8,128)S(1)} %get-tuple-element.168), channel_id=1, source_target_pairs={{0,16},{1,17},{2,18},{3,19},{4,20},{5,21},{6,22},{7,23},{8,9},{9,8... | collective-permute-start | bytes 49160 | tf_op jit(solution)/shard_map/ppermute | solution.py:870
  191.0 25.0 %copy-start.8 = (s32[5]{0:T(128)S(1)}, s32[5]{0:T(128)}, u32[]{:S(2)}) copy-start(s32[5]{0:T(128)} %stack.23.core.s) | copy-start | bytes 64
  191.1 8.7 %collective-permute-start.15 = (bf16[2,32,1536]{2,1,0:T(8,128)(2,1)S(1)}, bf16[2,32,1536]{2,1,0:T(8,128)(2,1)S(1)}, u32[]{:S(2)}, u32[]{:S(2)}) collective-permute-start(bf16[2,32,1536]{2,1,0:T(8,128)(2,1)S(1)} %get-tuple-element.167), channel_id=1, source_target_pairs={{0,4},{1,5},{2,6},{3,7},{4,0},{5,1},{6,2},{7,3},{8,12},{9,13},{10,... | collective-permute-start | bytes 589832 | tf_op jit(solution)/shard_map/ppermute | solution.py:870
  193.7 6.1 %collective-permute-start.14 = (bf16[4,16,1536]{2,1,0:T(8,128)(2,1)S(1)}, bf16[4,16,1536]{2,1,0:T(8,128)(2,1)S(1)}, u32[]{:S(2)}, u32[]{:S(2)}) collective-permute-start(bf16[4,16,1536]{2,1,0:T(8,128)(2,1)S(1)} %get-tuple-element.164), channel_id=1, source_target_pairs={{0,16},{1,17},{2,18},{3,19},{4,20},{5,21},{6,22},{7,23},{8,9},{9,8... | collective-permute-start | bytes 589832 | tf_op jit(solution)/shard_map/ppermute | solution.py:870
  200.9 7.9 %collective-permute-start.23 = (f32[32,128]{1,0:T(8,128)S(1)}, f32[32,128]{1,0:T(8,128)S(1)}, u32[]{:S(2)}, u32[]{:S(2)}) collective-permute-start(f32[32,128]{1,0:T(8,128)S(1)} %add_add_fusion.1), channel_id=1, source_target_pairs={{0,6},{1,7},{2,4},{3,5},{4,2},{5,3},{6,0},{7,1},{8,14},{9,15},{10,... | collective-permute-start | bytes 49160 | tf_op jit(solution)/shard_map/ppermute | solution.py:870
  204.2 5.5 %collective-permute-start.22 = (f32[32,128]{1,0:T(8,128)S(1)}, f32[32,128]{1,0:T(8,128)S(1)}, u32[]{:S(2)}, u32[]{:S(2)}) collective-permute-start(f32[32,128]{1,0:T(8,128)S(1)} %add_add_fusion.1), channel_id=1, source_target_pairs={{0,4},{1,5},{2,6},{3,7},{4,0},{5,1},{6,2},{7,3},{8,12},{9,13},{10,... | collective-permute-start | bytes 49160 | tf_op jit(solution)/shard_map/ppermute | solution.py:870
  204.7 5.0 %collective-permute-start.21 = (f32[32,128]{1,0:T(8,128)S(1)}, f32[32,128]{1,0:T(8,128)S(1)}, u32[]{:S(2)}, u32[]{:S(2)}) collective-permute-start(f32[32,128]{1,0:T(8,128)S(1)} %add_add_fusion.1), channel_id=1, source_target_pairs={{0,2},{1,3},{2,0},{3,1},{4,6},{5,7},{6,4},{7,5},{8,10},{9,11},{10,... | collective-permute-start | bytes 49160 | tf_op jit(solution)/shard_map/ppermute | solution.py:870
  205.4 10.5 %collective-permute-start.19 = (bf16[1,112,1024]{2,1,0:T(8,128)(2,1)S(1)}, bf16[1,112,1024]{2,1,0:T(8,128)(2,1)S(1)}, u32[]{:S(2)}, u32[]{:S(2)}) collective-permute-start(bf16[1,112,1024]{2,1,0:T(8,128)(2,1)S(1)} %get-tuple-element.170), channel_id=1, source_target_pairs={{0,4},{1,5},{2,6},{3,7},{4,0},{5,1},{6,2},{7,3},{8,12},{9,13},{10,... | collective-permute-start | bytes 688136 | tf_op jit(solution)/shard_map/ppermute | solution.py:870
  207.4 4.7 %collective-permute-start.20 = (bf16[2,16,1536]{2,1,0:T(8,128)(2,1)S(1)}, bf16[2,16,1536]{2,1,0:T(8,128)(2,1)S(1)}, u32[]{:S(2)}, u32[]{:S(2)}) collective-permute-start(bf16[2,16,1536]{2,1,0:T(8,128)(2,1)S(1)} %get-tuple-element.173), channel_id=1, source_target_pairs={{0,1},{1,0},{2,3},{3,2},{4,5},{5,4},{6,7},{7,6},{8,24},{9,25},{10,... | collective-permute-start | bytes 294920 | tf_op jit(solution)/shard_map/ppermute | solution.py:870
  215.9 3.3 %collective-permute-start.24 = (f32[32,128]{1,0:T(8,128)S(1)}, f32[32,128]{1,0:T(8,128)S(1)}, u32[]{:S(2)}, u32[]{:S(2)}) collective-permute-start(f32[32,128]{1,0:T(8,128)S(1)} %add_add_fusion), channel_id=1, source_target_pairs={{0,8},{1,9},{2,10},{3,11},{4,12},{5,13},{6,14},{7,15},{8,0},{9,1},... | collective-permute-start | bytes 49160 | tf_op jit(solution)/shard_map/ppermute | solution.py:870
  217.2 2.5 %collective-permute-start.25 = (f32[56,1536]{1,0:T(8,128)S(1)}, f32[56,1536]{1,0:T(8,128)S(1)}, u32[]{:S(2)}, u32[]{:S(2)}) collective-permute-start(f32[56,1536]{1,0:T(8,128)S(1)} %get-tuple-element.183), channel_id=1, source_target_pairs={{0,8},{1,9},{2,10},{3,11},{4,12},{5,13},{6,14},{7,15},{8,0},{9,1},... | collective-permute-start | bytes 1032200 | tf_op jit(solution)/shard_map/ppermute | solution.py:870
  (17 other events, 125.4 us)
Sparse Core Ops, SparseCore 0:
  187.5 19.0 reduce-scatter.1
where the time goes:
time: 229 us; the launch traced here: 228 us
  Pallas kernels  110 us (48%)
  starting transfers between devices  51.6 us (23%)
  waiting for transfers between devices  34.4 us (15%)
  between operations  16.9 us (7%)
  matrix products  6.19 us (3%)
  local copies, waits for them, and re-layouts  5.16 us (2%)
  other arithmetic  4.19 us (2%)
    pallas_call x17, Pallas kernels, call(): pl.pallas_call(kernel, grid_spec=pltpu.PrefetchScalarGridSpec(num_scalar_...  77.3 us
    ppermute x26, waiting for transfers between devices, send(): return lax.ppermute(value, ('row', 'chan'), pairs)  32.8 us
    ppermute x26, starting transfers between devices, send(): return lax.ppermute(value, ('row', 'chan'), pairs)  27.7 us
    all_to_all x4, starting transfers between devices, on_device(): lax.all_to_all(v, 'chan', split_axis=0, concat_axis=0, tiled=True)  23.8 us
    pallas_call x1, Pallas kernels, ssm_bwd(): pl.pallas_call(bwd_kernel, grid=(chans // GROUP,), in_specs=[s['sm'], s['...  18.6 us
    pallas_call x1, Pallas kernels, ssm_fwd(): pl.pallas_call(fwd_kernel, grid=(chans // GROUP,), in_specs=[s['sm'], s['...  13.7 us
    dot_general x3, matrix products, mm(): return lax.dot_general(a, b, d, preferred_element_type=f32)  6.19 us
  transfers between devices with their start and end apart: 31, of which 12 were waited for; matrix products, arithmetic and copies ran while one was open for 6% of the time, Pallas kernels for 47%

commit v1 on v0

--- a/solution.py
+++ b/solution.py
@@ -146,7 +146,7 @@
 
 def bwd_kernel(
     groups, keep, x, dy, rate, coef, ins, insj, head, tailj, hs, toe,
-    dv, drate, dcoef, pt, s1, e0, e1, near, gacc, nr, xs, ys,
+    dv, rates, pt, s1, e0, e1, near, gacc, nr, xs, ys,
 ):
     rows = ins.shape[0]
     n = rate.shape[1]
@@ -233,8 +233,14 @@
         dva = mm(near[...].reshape(SUB * rows, T).astype(bf16), flip)
         for c in range(SUB):
             xs[pl.ds(lo + c, rows, stride=GROUP), :] = dva[c * rows : (c + 1) * rows]
-        dcoef[lo : lo + SUB, :] = nr[0:SUB, :] + untile(ee * ac)
-        drate[lo : lo + SUB, :] = -(cf * nr[SUB : 2 * SUB, :] + untile(ar + ce * ae))
+        cut = (lo, lo + SUB)
+        dcoef = nr[0:SUB, :] + untile(ee * ac)
+        drate = -(cf * nr[SUB : 2 * SUB, :] + untile(ar + ce * ae))
+        lanes = rates.shape[-1]
+        for row in range(n // lanes):
+            at = slice(row * lanes, (row + 1) * lanes)
+            rates[row % 2, row // 2, 0, cut[0] : cut[1], :] = drate[:, at]
+            rates[row % 2, row // 2, 1, cut[0] : cut[1], :] = dcoef[:, at]
     dv[...] = xs[...].reshape(rows, GROUP, T).astype(bf16)
 
 
@@ -288,13 +294,13 @@
             pltpu.HBM((chans, T, T), bf16),
         ],
         scratch_shapes=[s["pt"], s["big"], s["near"], s["xs"], pltpu.VMEM((SUB, T), f32)],
-        compiler_params=pltpu.CompilerParams(vmem_limit_bytes=40 * 2**20),
+        compiler_params=pltpu.CompilerParams(vmem_limit_bytes=16 * 2**20),
         cost_estimate=s["cost"],
         name="ssm_fwd",
     )(masks[0], masks[1], x, rate, coef, *masks[2:])
 
 
-def ssm_bwd(x, dy, rate, coef, masks, hs, toe):
+def ssm_bwd(x, dy, rate, coef, masks, hs, toe, row_n):
     rows, chans, _ = x.shape
     n = rate.shape[1]
     s = ssm_specs(rows, n)
@@ -304,11 +310,13 @@
         in_specs=[s["sm"], s["sm"], s["ch"], s["ch"], s["par"], s["par"]]
         + [s["full"]] * 4
         + [s["hs"], s["toe"]],
-        out_specs=[s["ch"], s["par"], s["par"]],
+        out_specs=[
+            s["ch"],
+            pl.BlockSpec((2, row_n // 2, 2, GROUP, n // row_n), lambda i: (0, 0, 0, i, 0)),
+        ],
         out_shape=[
             pltpu.HBM(x.shape, bf16),
-            pltpu.HBM((chans, n), f32),
-            pltpu.HBM((chans, n), f32),
+            jax.ShapeDtypeStruct((2, row_n // 2, 2, chans, n // row_n), f32),
         ],
         scratch_shapes=[
             s["pt"],
@@ -321,7 +329,7 @@
             s["xs"],
             s["xs"],
         ],
-        compiler_params=pltpu.CompilerParams(vmem_limit_bytes=40 * 2**20),
+        compiler_params=pltpu.CompilerParams(vmem_limit_bytes=16 * 2**20),
         cost_estimate=s["cost"],
         name="ssm_bwd",
     )(masks[0], masks[1], x, dy, rate, coef, *masks[2:], *from_hbm(hs, toe))
@@ -474,7 +482,7 @@
         [in_hbm((2 * own, half), bf16)] * 3
         + [in_hbm((width, 2 * own), bf16), in_hbm(spread, f32), in_hbm(spread, bf16)]
         + [in_hbm((2 * own, width), bf16)],
-        (normed, normed_oth, grad, grad_oth, w_up, w_mix, w_down),
+        from_hbm(normed, normed_oth, grad, grad_oth, w_up, w_mix, w_down),
         scalars=core,
         scratch=[
             pltpu.VMEM((2 * own, width), bf16),
@@ -569,7 +577,7 @@
         [in_hbm((2 * own, half), bf16)] * 2
         + [in_hbm((16, um, half), bf16)] * 2
         + [in_hbm((16, mx, half), bf16)] * 2,
-        (y_own, y_oth, w_mix, u_act, d_slope, d_yproj, normed_t),
+        from_hbm(y_own, y_oth, w_mix, u_act, d_slope, d_yproj, normed_t),
         scalars=scal,
         scratch=[
             pltpu.VMEM((inner, 2 * own), bf16),
@@ -621,7 +629,7 @@
         ],
         [whole((own, width)), whole((own, width)), whole((2, own, width))],
         [in_hbm((own, width), f32), in_hbm((own, width), f32), in_hbm((2, own, width), bf16)],
-        (gate, d_upre, w_down, w_up),
+        from_hbm(gate, d_upre, w_down, w_up),
         scalars=scal,
         scratch=[pltpu.VMEM((2, 2 * own, width), f32)],
         vmem=56,
@@ -778,24 +786,27 @@
     )
 
 
-def finish_kernel(s, u_keep, u_got, m_keep, m_got, d_keep, d_got, down, mine, other):
+def finish_kernel(s, u_keep, u_got, m_keep, m_got, d_keep, d_got, norm, down, mine, other):
     d = d_keep[0].astype(f32) + d_got[0].astype(f32)
     rows = down.shape[0]
     down[...] = d[:rows]
     half = d.shape[1]
     um, mx = u_keep.shape[1], m_keep.shape[1]
-    for out, core in ((mine, s[0]), (other, 1 - s[0])):
+    tail = um + mx + 8
+    for out, core, owner in ((mine, s[0], s[5]), (other, 1 - s[0], s[6])):
         out[0:um, :] = u_keep[core].astype(f32) + u_got[core].astype(f32)
         out[um : um + mx, :] = m_keep[core].astype(f32) + m_got[core].astype(f32)
-        out[um + mx :, 0:half] = jnp.where(core == 0, d[rows : rows + 8], d[rows + 8 :])
-        out[um + mx :, half:] = jnp.zeros((8, out.shape[1] - half), f32)
-
-
-def finish_call(scal, up, mix, down):
+        out[um + mx : tail, 0:half] = jnp.where(core == 0, d[rows : rows + 8], d[rows + 8 :])
+        out[um + mx : tail, half:] = jnp.zeros((8, out.shape[1] - half), f32)
+        out[tail:, :] = jnp.zeros((8, out.shape[1]), f32)
+        out[tail : tail + 1, 0:T] = norm[pl.ds(owner, 1), :]
+
+
+def finish_call(scal, up, mix, down, norm):
     um, mx, half = up[0].shape[1], mix[0].shape[1], up[0].shape[2]
     rows, width = down[0].shape[1:]
-    args = (*up, *mix, *down)
-    pack = (um + mx + 8, half)
+    args = (*up, *mix, *down, norm)
+    pack = (um + mx + 16, half)
     return call(
         finish_kernel,
         "finish",
@@ -808,7 +819,7 @@
     )
 
 
-def join_kernel(s, mine, got, up, mix, val):
+def join_kernel(s, mine, got, up, mix, val, norm):
     um, mx = up.shape[0], mix.shape[0]
     first = s[0] == 0
     part = mine.shape[1] // 2
@@ -820,7 +831,9 @@
             mix[:, to] = held[um : um + mx, x * part : (x + 1) * part]
         w = val.shape[1] // 2
         for r in range(val.shape[0] // 8):
-            val[r * 8 : r * 8 + 8, core * w : (core + 1) * w] = held[um + mx :, r * w : (r + 1) * w]
+            at = slice(r * w, (r + 1) * w)
+            val[r * 8 : r * 8 + 8, core * w : (core + 1) * w] = held[um + mx : um + mx + 8, at]
+    norm[...] = mine[um + mx + 8 :, 0:T] + got[um + mx + 8 :, 0:T]
 
 
 def join_call(scal, mine, got, um, mx, inner):
@@ -830,8 +843,13 @@
         "join",
         (1,),
         [whole(mine.shape)] * 2,
-        [whole((um, ff)), whole((mx, ff)), whole((um, inner))],
-        [struct((um, ff), f32), struct((mx, ff), f32), struct((um, inner), f32)],
+        [whole((um, ff)), whole((mx, ff)), whole((um, inner)), whole((8, T))],
+        [
+            struct((um, ff), f32),
+            struct((mx, ff), f32),
+            struct((um, inner), f32),
+            struct((8, T), f32),
+        ],
         (mine, got),
         scalars=scal,
     )
@@ -846,7 +864,10 @@
         inner = w_val.shape[1]
         row, chan = lax.axis_index("row"), lax.axis_index("chan")
         core = row % 2
-        scal = jnp.stack([core, row // 2, chan % 2, (chan // 2) % 2, chan // 4]).astype(jnp.int32)
+        me = row * chan_n + chan
+        there = (row ^ 1) * chan_n + chan
+        scal = jnp.stack([core, row // 2, chan % 2, (chan // 2) % 2, chan // 4, me, there])
+        scal = scal.astype(jnp.int32)
         bit_x, bit_y = scal[1], scal[2]
         bit_a = jnp.where(core == 0, bit_x, bit_y).reshape(1)
         bit_b = jnp.where(core == 0, bit_y, bit_x).reshape(1)
@@ -860,6 +881,7 @@
             b=lambda r, c: flip_x(r, c) if r % 2 else flip_y(r, c),
             low=lambda r, c: (r, c ^ 2),
             high=lambda r, c: (r, c ^ 4),
+            x=lambda r, c: (r ^ 2, c),
             ab=lambda r, c: (r ^ 2, c ^ 1),
             z=lambda r, c: (r, c ^ 6),
         )
@@ -889,8 +911,8 @@
         y_chan, states, toeplitz = ssm_fwd(v_chan, decay_rate, mix_coef, masks)
         y_chan, d_y_chan = after((y_chan, d_y_chan))
         y_own = trade(to_tok(y_chan))
-        d_v_chan, d_rate, d_coef = ssm_bwd(
-            v_chan, d_y_chan, decay_rate, mix_coef, masks, states, toeplitz
+        d_v_chan, rates = ssm_bwd(
+            v_chan, d_y_chan, decay_rate, mix_coef, masks, states, toeplitz, row_n
         )
         y_own, d_v_chan = after((y_own, d_v_chan))
         y_oth = send(y_own, "core")
@@ -899,15 +921,12 @@
         gate_out, d_upre, u_give, u_keep, m_give, m_keep = mid_call(
             scal, y_own, y_oth, w_mix, u_act, d_slope, d_yproj, normed_t, row_n
         )
-        u_give, m_give, gate_out, d_v, d_rate, d_coef = after(
-            (u_give, m_give, gate_out, d_v, d_rate, d_coef)
-        )
+        u_give, m_give, gate_out, d_v, rates = after((u_give, m_give, gate_out, d_v, rates))
 
         u_got = send(u_give, "a")
         m_got = send(m_give, "low")
-        rates = lax.psum_scatter(
-            jnp.concatenate([d_rate, d_coef], 0), "row", scatter_dimension=1, tiled=True
-        )
+        rates_give = lax.dynamic_index_in_dim(rates, 1 - core, 0, keepdims=False)
+        rates_got = send(rates_give, "core")
         half = chan_n // 2
         other_half = lambda v: lax.dynamic_slice_in_dim(v, (1 - core) * half, half, 0)
         v_give = (other_half(d_v).astype(f32) * other_half(v_slope)).astype(bf16)
@@ -915,7 +934,9 @@
         d_vpre = (d_v.astype(f32) * v_slope).astype(bf16)
         down = mm(gate_out, pair_grad, TN).astype(bf16)
         d_give, d_keep = down_val_call(scal, down, d_vpre, v_got, normed_t)
-        u_got, m_got, d_give, gate_out = after((u_got, m_got, d_give, gate_out))
+        u_got, m_got, d_give, gate_out, rates_got = after(
+            (u_got, m_got, d_give, gate_out, rates_got)
+        )
 
         d_got = send(d_give, "a")
         m_give, m_keep = step_call(bit_high, m_keep, m_got)
@@ -927,43 +948,48 @@
         u_got = send(u_give, "b")
         bd_got = send(bd_give, "core")
         d_give, d_keep = step_call(bit_b, d_keep, d_got)
-        u_got, d_give, bd_got = after((u_got, d_give, bd_got))
-
+        rates = lax.dynamic_index_in_dim(rates, core, 0, keepdims=False) + rates_got
+        rates_give = lax.dynamic_index_in_dim(rates, 1 - bit_x, 0, keepdims=False)
+        block_out, tokens_grad, norm_part = tail_call(
+            tokens, out_grad, layer_norm_gain, block_own, bd_got, dn_own, d_vpre, w_val,
+            row_n * chan_n,
+        )
+        u_got, d_give, norm_part, rates_give = after((u_got, d_give, norm_part, rates_give))
+
+        rates_got = send(rates_give, "x")
         d_got = send(d_give, "b")
         u_give, u_keep = step_call(bit_low, u_keep, u_got)
         u_got = send(u_give, "low")
         m_give, m_keep = step_call(bit_a, m_keep, m_got)
-        block_out, tokens_grad, norm_part = tail_call(
-            tokens, out_grad, layer_norm_gain, block_own, bd_got, dn_own, d_vpre, w_val,
-            row_n * chan_n,
-        )
-        d_got, u_got, m_give, norm_part = after((d_got, u_got, m_give, norm_part))
+        norm_part = norm_part + send(norm_part, "low")
+        d_got, u_got, m_give, norm_part, rates_got = after(
+            (d_got, u_got, m_give, norm_part, rates_got)
+        )
+        rates = lax.dynamic_index_in_dim(rates, bit_x, 0, keepdims=False) + rates_got
 
         d_give, d_keep = step_call(bit_low, d_keep, d_got)
         d_got = send(d_give, "low")
         u_give, u_keep = step_call(bit_high, u_keep, u_got)
         u_got = send(u_give, "high")
         m_got = send(m_give, "a")
-        norm_part = norm_part + send(norm_part, "a") + send(norm_part, "b") + send(norm_part, "ab")
+        norm_part = norm_part + send(norm_part, "a")
+        norm_part = norm_part + send(norm_part, "b")
         d_got, m_got, u_got, norm_part = after((d_got, m_got, u_got, norm_part))
 
         d_give, d_keep = step_call(bit_high, d_keep, d_got)
         d_got = send(d_give, "high")
         m_give, m_keep = step_call(bit_b, m_keep, m_got)
         m_got = send(m_give, "b")
-        norm_part = (
-            norm_part + send(norm_part, "low") + send(norm_part, "high") + send(norm_part, "z")
-        )
+        norm_part = norm_part + send(norm_part, "high")
         d_got, m_got, norm_part = after((d_got, m_got, norm_part))
 
         down_grad, mine, other = finish_call(
-            scal, (u_keep, u_got), (m_keep, m_got), (d_keep, d_got)
+            scal, (u_keep, u_got), (m_keep, m_got), (d_keep, d_got), norm_part
         )
         um, mx = u_keep.shape[1], m_keep.shape[1]
         other = send(other, "core")
-        norm_part = norm_part + send(norm_part, "core")
-        up_grad, mix_grad, val_grad = join_call(scal, mine, other, um, mx, inner)
-        norm_sum = lax.dynamic_index_in_dim(norm_part, row * chan_n + chan, 0, keepdims=False)
+        up_grad, mix_grad, val_grad, norm_sum = join_call(scal, mine, other, um, mx, inner)
+        norm_sum = norm_sum[0]
         w = width // (row_n * chan_n)
         return (
             block_out,
@@ -974,8 +1000,8 @@
             val_grad,
             mix_grad,
             down_grad,
-            rates[: decay_rate.shape[0]],
-            rates[decay_rate.shape[0] :],
+            rates[0],
+            rates[1],
         )
 
     return on_device
@@ -1079,8 +1105,8 @@
         y_chan = jnp.swapaxes(y_chan, 0, 1)
         y_own = lax.all_to_all(y_chan, "chan", split_axis=1, concat_axis=0, tiled=True)
         y_own = y_own.reshape(inner, own)
-        d_v_chan, d_rate, d_coef = ssm_bwd(
-            v_chan, d_y_chan, decay_rate, mix_coef, masks, states, toeplitz
+        d_v_chan, rates = ssm_bwd(
+            v_chan, d_y_chan, decay_rate, mix_coef, masks, states, toeplitz, row_n
         )
         d_v_chan = jnp.swapaxes(d_v_chan, 0, 1)
         d_v = lax.all_to_all(d_v_chan, "chan", split_axis=1, concat_axis=0, tiled=True)
@@ -1140,14 +1166,10 @@
             - jnp.mean(d_xh, axis=1, keepdims=True)
             - x_hat * jnp.mean(d_xh * x_hat, axis=1, keepdims=True)
         )
-        row_all = row_bits + [core_bit]
-        states_n = decay_rate.shape[1]
-        rates = jnp.stack([d_rate, d_coef]).reshape(
-            (2 * d_rate.shape[0],) + (2,) * len(row_all) + (states_n // row_n,)
-        )
-        rates = jnp.moveaxis(rates, 0, len(row_all))
-        rates = scatter_sum(rates, row_all, [core_bit] + row_bits, jnp.float32)
-        rates = rates.reshape(2, d_rate.shape[0], states_n // row_n)
+        row_all = [core_bit] + row_bits
+        chans, lanes = rates.shape[-2:]
+        rates = rates.reshape((2,) * len(row_all) + (2 * chans, lanes))
+        rates = scatter_sum(rates, row_all, row_all, jnp.float32).reshape(2, chans, lanes)
         return (
             block_out,
             tokens_grad,

time: 229 us -> 215 us (0.939)
  between operations: 16.9 us -> 3.59 us
  starting transfers between devices: 51.6 us -> 47.8 us
  local copies, waits for them, and re-layouts: 5.16 us -> 7.7 us
    ppermute x26 -> x25, starting transfers between devices: 27.7 us -> 23.9 us  [send(): return lax.ppermute(value, ('row', 'chan'), pairs)]
    unnamed x36 -> x44, local copies, waits for them, and re-layouts: 2.39 us -> 5.08 us
    ppermute x26 -> x25, waiting for transfers between devices: 32.8 us -> 32.8 us  [send(): return lax.ppermute(value, ('row', 'chan'), pairs)]
  transfers between devices with their start and end apart: 31 -> 29, of which waited for: 12 -> 12; matrix products, arithmetic and copies ran while one was open for 6% -> 6% of each run, Pallas kernels for 47% -> 48%
where the time goes in v1:
time: 215 us; the launch traced here: 214 us
  Pallas kernels  110 us (51%)
  starting transfers between devices  47.8 us (22%)
  waiting for transfers between devices  34.4 us (16%)
  local copies, waits for them, and re-layouts  7.7 us (4%)
  matrix products  6.19 us (3%)
  other arithmetic  4.46 us (2%)
  between operations  3.59 us (2%)
    pallas_call x17, Pallas kernels, call(): pl.pallas_call(kernel, grid_spec=pltpu.PrefetchScalarGridSpec(num_scalar_...  77.9 us
    ppermute x25, waiting for transfers between devices, send(): return lax.ppermute(value, ('row', 'chan'), pairs)  32.8 us
    ppermute x25, starting transfers between devices, send(): return lax.ppermute(value, ('row', 'chan'), pairs)  23.9 us
    all_to_all x4, starting transfers between devices, on_device(): lax.all_to_all(v, 'chan', split_axis=0, concat_axis=0, tiled=True)  23.8 us
    pallas_call x1, Pallas kernels, ssm_bwd(): pl.pallas_call(bwd_kernel, grid=(chans // GROUP,), in_specs=[s['sm'], s['...  18.6 us
    pallas_call x1, Pallas kernels, ssm_fwd(): pl.pallas_call(fwd_kernel, grid=(chans // GROUP,), in_specs=[s['sm'], s['...  13.7 us
    dot_general x3, matrix products, mm(): return lax.dot_general(a, b, d, preferred_element_type=f32)  6.19 us
    unnamed x44, local copies, waits for them, and re-layouts  5.08 us
  transfers between devices with their start and end apart: 29, of which 12 were waited for; matrix products, arithmetic and copies ran while one was open for 6% of the time, Pallas kernels for 48%

profile of v1, /device:TPU:0, one launch (start us, length us, event | category | flops | bytes accessed | tf_op | source)
XLA Modules:
  0.0 214.2 jit_solution(6732836623164415463)
XLA Ops:
  0.7 5.2 %norm_val.1 = (bf16[512,1024]{1,0:T(8,128)(2,1)S(1)}, bf16[8,4,64,128]{3,2,1,0:T(8,128)(2,1)}, f32[8,4,64,128]{3,2,1,0:T(8,128)S(1)}) custom-call(bf16[512,1024]{1,0:T(8,128)(2,1)} %tok.3, f32[1,1024]{1,0:T(1,128)} %bitcast.95, f32[1,1024]{1,0:T(1,128)} %bitcast.97, bf16[1024,512]{1,0:T(8,128)(2,1)} %w_val.3), custom_call_target="tpu_custom_call" | custom-call | tf_op jit(solution)/shard_map/norm_val/pallas_call | solution.py:368
  6.3 7.3 %all-to-all-start = ((bf16[8,4,64,128]{3,2,1,0:T(8,128)(2,1)}), bf16[8,4,64,128]{3,2,1,0:T(8,128)(2,1)S(1)}, u32[]{:S(2)}, u32[]{:S(2)}) async-start(bf16[8,4,64,128]{3,2,1,0:T(8,128)(2,1)} %get-tuple-element.102), calls=%async_computation | async-start | bytes 1048576 | tf_op jit(solution)/shard_map/all_to_all | solution.py:895
  14.5 18.6 %gate.1 = (bf16[1024,1536]{1,0:T(8,128)(2,1)}, bf16[1024,1536]{1,0:T(8,128)(2,1)}, bf16[1024,1536]{1,0:T(8,128)(2,1)}, bf16[1024,1024]{1,0:T(8,128)(2,1)}, f32[8...) custom-call(s32[7]{0:T(128)} %stack.31.core.s, bf16[512,1024]{1,0:T(8,128)(2,1)} %copy-done.10, ...), custom_call_target="tpu_custom_call" | custom-call | tf_op jit(solution)/shard_map/gate/pallas_call | solution.py:368
  37.0 2.2 %add_convert_fusion = bf16[8,4,64,128]{3,2,1,0:T(8,128)(2,1)} fusion(f32[8,4,64,128]{3,2,1,0:T(8,128)} %get-tuple-element.104, bf16[8,4,64,128]{3,2,1,0:T(8,128)(2,1)S(1)} %collective-permute-done.2), kind=kLoop, calls=%fused_computation.6 | loop fusion | flops 786432 | bytes 2097152 | tf_op jit(solution)/shard_map/convert_element_type | solution.py:908
  39.2 6.0 %all-to-all-start.1 = ((bf16[8,4,64,128]{3,2,1,0:T(8,128)(2,1)}), bf16[8,4,64,128]{3,2,1,0:T(8,128)(2,1)S(1)}, u32[]{:S(2)}, u32[]{:S(2)}) async-start(bf16[8,4,64,128]{3,2,1,0:T(8,128)(2,1)} %add_convert_fusion), calls=%async_computation.1 | async-start | bytes 1048576 | tf_op jit(solution)/shard_map/all_to_all | solution.py:895
  45.2 13.7 %ssm_fwd.1 = (bf16[32,64,128]{2,1,0:T(8,128)(2,1)}, f32[8,4,256,128]{3,2,1,0:T(8,128)}, bf16[64,128,128]{2,1,0:T(8,128)(2,1)}) custom-call(s32[1]{0:T(128)} %bitcast.10.groups, f32[32]{0:T(128)S(1)} %convert_reduce_fusion.keep, bf16[32,64,128]{2,1,0:T(8,128)(2,1)S(1)} %bitcast.87, f32[64,512]{1,0:T(8,128)S(1)} %copy-done.14, f32[64,512]{1,0:T(8,128)S(1)} %copy-done.15, ...), custom_call_target="tpu_custom_call" | custom-call | flops 20000000000 | bytes 10000000 | tf_op jit(solution)/shard_map/ssm_fwd/pallas_call | solution.py:286
  60.3 4.6 %all-to-all-start.2 = ((bf16[8,4,64,128]{3,2,1,0:T(8,128)(2,1)}), bf16[8,4,64,128]{3,2,1,0:T(8,128)(2,1)S(1)}, u32[]{:S(2)}, u32[]{:S(2)}) async-start(bf16[8,4,64,128]{3,2,1,0:T(8,128)(2,1)} %bitcast.91), calls=%async_computation.2 | async-start | bytes 1048576 | tf_op jit(solution)/shard_map/all_to_all | solution.py:895
  64.9 18.6 %ssm_bwd.1 = (bf16[32,64,128]{2,1,0:T(8,128)(2,1)}, f32[2,2,2,64,128]{4,3,2,1,0:T(8,128)S(1)}) custom-call(s32[1]{0:T(128)} %bitcast.10.groups, f32[32]{0:T(128)S(1)} %convert_reduce_fusion.keep, bf16[32,64,128]{2,1,0:T(8,128)(2,1)S(1)} %bitcast.88, bf16[32,64,128]{2,1,0:T(8,128)(2,1)S(1)} %bitcast.89, f32[64,512]{1,0:T(8,128)S(1)} %copy-done.14, ...), custom_call_target="tpu_custom_call" | custom-call | flops 20000000000 | bytes 10000000 | tf_op jit(solution)/shard_map/ssm_bwd/pallas_call | solution.py:307
  83.6 1.9 collective-permute-done.3.y_oth
  85.5 6.0 %all-to-all-start.3 = ((bf16[8,4,64,128]{3,2,1,0:T(8,128)(2,1)}), bf16[8,4,64,128]{3,2,1,0:T(8,128)(2,1)S(1)}, u32[]{:S(2)}, u32[]{:S(2)}) async-start(bf16[8,4,64,128]{3,2,1,0:T(8,128)(2,1)} %bitcast.90), calls=%async_computation.3 | async-start | bytes 1048576 | tf_op jit(solution)/shard_map/all_to_all | solution.py:895
  91.5 14.6 %mix_up.1 = (bf16[1024,1536]{1,0:T(8,128)(2,1)}, bf16[1024,1536]{1,0:T(8,128)(2,1)}, bf16[16,32,1536]{2,1,0:T(8,128)(2,1)}, bf16[16,32,1536]{2,1,0:T(8,128)(2,1)...) custom-call(s32[7]{0:T(128)} %stack.31.core.s, bf16[8,4,64,128]{3,2,1,0:T(8,128)(2,1)} %copy-done.18, ...), custom_call_target="tpu_custom_call" | custom-call | flops 10000000000 | bytes 10000000 | tf_op jit(solution)/shard_map/mix_up/pallas_call | solution.py:368
  106.2 1.5 collective-permute-start.4
  107.9 2.0 collective-permute-start.5
  110.1 6.0 %convolution_convert_fusion.down_g.down_k = bf16[1536,1024]{1,0:T(8,128)(2,1)S(1)} fusion(bf16[1024,1536]{1,0:T(8,128)(2,1)} %get-tuple-element.134.gate, bf16[1024,1024]{1,0:T(8,128)(2,1)} %get-tuple-element.129), kind=kOutput, calls=%fused_computation | convolution fusion | flops 3222798336 | bytes 8388608 | tf_op jit(solution)/shard_map/dot_general | solution.py:20
  116.3 1.6 copy-done.5
  117.9 4.4 %down_val.1 = (bf16[8,112,1024]{2,1,0:T(8,128)(2,1)}, bf16[8,112,1024]{2,1,0:T(8,128)(2,1)S(1)}) custom-call(s32[7]{0:T(128)S(1)} %copy-done.12, bf16[1536,1024]{1,0:T(8,128)(2,1)S(1)} %convolution_convert_fusion.down_g.down_k, bf16[1536,1024]{1,0:T(8,128)(2,1)S(1)} %convolution_convert_fusion.down_g.down_k, ...), custom_call_target="tpu_custom_call" | custom-call | tf_op jit(solution)/shard_map/down_val/pallas_call | solution.py:368
  122.3 5.9 %collective-permute-done.5 = bf16[16,16,1536]{2,1,0:T(8,128)(2,1)S(1)} collective-permute-done((bf16[16,16,1536]{2,1,0:T(8,128)(2,1)}, bf16[16,16,1536]{2,1,0:T(8,128)(2,1)S(1)}, u32[]{:S(2)}, u32[]{:S(2)}) %collective-permute-start.5) | collective-permute-done | bytes 786464 | tf_op jit(solution)/shard_map/ppermute | solution.py:892
  131.0 2.6 %collective-permute-start.9 = (bf16[8,16,1536]{2,1,0:T(8,128)(2,1)}, bf16[8,16,1536]{2,1,0:T(8,128)(2,1)}, u32[]{:S(2)}, u32[]{:S(2)}) collective-permute-start(bf16[8,16,1536]{2,1,0:T(8,128)(2,1)} %get-tuple-element.140), channel_id=1, source_target_pairs={{0,4},{1,5},{2,6},{3,7},{4,0},{5,1},{6,2},{7,3},{8,12},{9,13},{10,... | collective-permute-start | bytes 1179656 | tf_op jit(solution)/shard_map/ppermute | solution.py:892
  133.5 14.7 %block.1 = (f32[512,1024]{1,0:T(8,128)}, f32[512,1024]{1,0:T(8,128)}, bf16[2,512,1024]{2,1,0:T(8,128)(2,1)}) custom-call(s32[7]{0:T(128)} %stack.31.core.s, bf16[1024,1536]{1,0:T(8,128)(2,1)} %get-tuple-element.134.gate, bf16[1024,1536]{1,0:T(8,128)(2,1)} %get-tuple-element.135.d_upre, bf16[3072,1024]{1,0:T(8,128)(2,1)} %w_down.3, bf16[1024,3072]{1,0:T(8,128)(2,1)} %w_up.3), custom_call_target="tpu_custom_call" | custom-call | tf_op jit(solution)/shard_map/block/pallas_call | solution.py:368
  148.2 1.6 halve.10
  150.7 1.4 collective-permute-done.9
  155.1 3.6 %halve.11 = (bf16[4,112,1024]{2,1,0:T(8,128)(2,1)}, bf16[4,112,1024]{2,1,0:T(8,128)(2,1)S(1)}) custom-call(s32[1]{0:T(128)} %bitcast.19.bit, bf16[2,4,112,1024]{3,2,1,0:T(8,128)(2,1)S(1)} %bitcast.55, bf16[2,4,112,1024]{3,2,1,0:T(8,128)(2,1)} %bitcast.24.got_g.got_k, bf16[2,4,112,1024]{3,2,1,0:T(8,128)(2,1)S(1)} %bitcast.56, ...), custom_call_target="tpu_custom_call" | custom-call | tf_op jit(solution)/shard_map/halve/pallas_call | solution.py:368
  158.8 7.3 %norm_back.1 = (bf16[512,1024]{1,0:T(8,128)(2,1)}, f32[512,1024]{1,0:T(8,128)}, f32[32,128]{1,0:T(8,128)S(1)}) custom-call(bf16[512,1024]{1,0:T(8,128)(2,1)} %tok.3, bf16[512,1024]{1,0:T(8,128)(2,1)} %grad.1, f32[1,1024]{1,0:T(1,128)} %bitcast.96, f32[512,1024]{1,0:T(8,128)} %get-tuple-element.136.block_own, ...), custom_call_target="tpu_custom_call" | custom-call | tf_op jit(solution)/shard_map/norm_back/pallas_call | solution.py:368
  172.5 1.8 halve.13
  174.4 6.1 %collective-permute-done.14 = f32[32,128]{1,0:T(8,128)S(1)} collective-permute-done((f32[32,128]{1,0:T(8,128)S(1)}, f32[32,128]{1,0:T(8,128)S(1)}, u32[]{:S(2)}, u32[]{:S(2)}) %collective-permute-start.14) | collective-permute-done | bytes 16416 | tf_op jit(solution)/shard_map/ppermute | solution.py:892
  182.4 2.6 %collective-permute-start.18 = (bf16[2,32,1536]{2,1,0:T(8,128)(2,1)S(1)}, bf16[2,32,1536]{2,1,0:T(8,128)(2,1)S(1)}, u32[]{:S(2)}, u32[]{:S(2)}) collective-permute-start(bf16[2,32,1536]{2,1,0:T(8,128)(2,1)S(1)} %get-tuple-element.171), channel_id=1, source_target_pairs={{0,4},{1,5},{2,6},{3,7},{4,0},{5,1},{6,2},{7,3},{8,12},{9,13},{10,... | collective-permute-start | bytes 589832 | tf_op jit(solution)/shard_map/ppermute | solution.py:892
  185.5 1.5 collective-permute-start.19
  187.0 3.8 %collective-permute-done.19 = f32[32,128]{1,0:T(8,128)S(1)} collective-permute-done((f32[32,128]{1,0:T(8,128)S(1)}, f32[32,128]{1,0:T(8,128)S(1)}, u32[]{:S(2)}, u32[]{:S(2)}) %collective-permute-start.19) | collective-permute-done | bytes 16416 | tf_op jit(solution)/shard_map/ppermute | solution.py:892
  192.1 2.4 %collective-permute-done.20 = f32[32,128]{1,0:T(8,128)S(1)} collective-permute-done((f32[32,128]{1,0:T(8,128)S(1)}, f32[32,128]{1,0:T(8,128)S(1)}, u32[]{:S(2)}, u32[]{:S(2)}) %collective-permute-start.20) | collective-permute-done | bytes 16416 | tf_op jit(solution)/shard_map/ppermute | solution.py:892
  196.8 2.3 %collective-permute-start.21 = (bf16[1,112,1024]{2,1,0:T(8,128)(2,1)S(1)}, bf16[1,112,1024]{2,1,0:T(8,128)(2,1)S(1)}, u32[]{:S(2)}, u32[]{:S(2)}) collective-permute-start(bf16[1,112,1024]{2,1,0:T(8,128)(2,1)S(1)} %get-tuple-element.179), channel_id=1, source_target_pairs={{0,4},{1,5},{2,6},{3,7},{4,0},{5,1},{6,2},{7,3},{8,12},{9,13},{10,... | collective-permute-start | bytes 688136 | tf_op jit(solution)/shard_map/ppermute | solution.py:892
  199.2 1.5 collective-permute-start.22
  201.3 7.9 %collective-permute-done.23 = f32[32,128]{1,0:T(8,128)S(1)} collective-permute-done((f32[32,128]{1,0:T(8,128)S(1)}, f32[32,128]{1,0:T(8,128)S(1)}, u32[]{:S(2)}, u32[]{:S(2)}) %collective-permute-start.23) | collective-permute-done | bytes 16416 | tf_op jit(solution)/shard_map/ppermute | solution.py:892
  (110 shorter events, 29.7 us)
Async XLA Ops:
  5.8 8.6 %collective-permute-start = (bf16[512,1024]{1,0:T(8,128)(2,1)S(1)}, bf16[512,1024]{1,0:T(8,128)(2,1)}, u32[]{:S(2)}, u32[]{:S(2)}) collective-permute-start(bf16[512,1024]{1,0:T(8,128)(2,1)S(1)} %get-tuple-element.103.n_own), channel_id=1, source_target_pairs={{0,8},{1,9},{2,10},{3,11},{4,12},{5,13},{6,14},{7,15},{8,0},{9,1},... | collective-permute-start | bytes 3145736 | tf_op jit(solution)/shard_map/ppermute | solution.py:892
  6.3 8.2 %collective-permute-start.1 = (bf16[512,1024]{1,0:T(8,128)(2,1)}, bf16[512,1024]{1,0:T(8,128)(2,1)}, u32[]{:S(2)}, u32[]{:S(2)}) collective-permute-start(bf16[512,1024]{1,0:T(8,128)(2,1)} %grad.1), channel_id=1, source_target_pairs={{0,8},{1,9},{2,10},{3,11},{4,12},{5,13},{6,14},{7,15},{8,0},{9,1},... | collective-permute-start | bytes 3145736 | tf_op jit(solution)/shard_map/ppermute | solution.py:892
  6.3 32.9 %all-to-all-start = ((bf16[8,4,64,128]{3,2,1,0:T(8,128)(2,1)}), bf16[8,4,64,128]{3,2,1,0:T(8,128)(2,1)S(1)}, u32[]{:S(2)}, u32[]{:S(2)}) async-start(bf16[8,4,64,128]{3,2,1,0:T(8,128)(2,1)} %get-tuple-element.102), calls=%async_computation | async-start | bytes 1048576 | tf_op jit(solution)/shard_map/all_to_all | solution.py:895
  33.1 3.9 %collective-permute-start.2 = (bf16[8,4,64,128]{3,2,1,0:T(8,128)(2,1)}, bf16[8,4,64,128]{3,2,1,0:T(8,128)(2,1)S(1)}, u32[]{:S(2)}, u32[]{:S(2)}) collective-permute-start(bf16[8,4,64,128]{3,2,1,0:T(8,128)(2,1)} %get-tuple-element.105), channel_id=1, source_target_pairs={{0,8},{1,9},{2,10},{3,11},{4,12},{5,13},{6,14},{7,15},{8,0},{9,1},... | collective-permute-start | bytes 1572872 | tf_op jit(solution)/shard_map/ppermute | solution.py:892
  39.2 21.1 %all-to-all-start.1 = ((bf16[8,4,64,128]{3,2,1,0:T(8,128)(2,1)}), bf16[8,4,64,128]{3,2,1,0:T(8,128)(2,1)S(1)}, u32[]{:S(2)}, u32[]{:S(2)}) async-start(bf16[8,4,64,128]{3,2,1,0:T(8,128)(2,1)} %add_convert_fusion), calls=%async_computation.1 | async-start | bytes 1048576 | tf_op jit(solution)/shard_map/all_to_all | solution.py:895
  60.3 23.1 %all-to-all-start.2 = ((bf16[8,4,64,128]{3,2,1,0:T(8,128)(2,1)}), bf16[8,4,64,128]{3,2,1,0:T(8,128)(2,1)S(1)}, u32[]{:S(2)}, u32[]{:S(2)}) async-start(bf16[8,4,64,128]{3,2,1,0:T(8,128)(2,1)} %bitcast.91), calls=%async_computation.2 | async-start | bytes 1048576 | tf_op jit(solution)/shard_map/all_to_all | solution.py:895
  83.5 26.4 %copy-start.11 = (f32[2,2,2,64,128]{4,3,2,1,0:T(8,128)}, f32[2,2,2,64,128]{4,3,2,1,0:T(8,128)S(1)}, u32[]{:S(2)}) copy-start(f32[2,2,2,64,128]{4,3,2,1,0:T(8,128)S(1)} %get-tuple-element.133) | copy-start | bytes 786436
  83.5 2.0 collective-permute-start.3
  85.5 20.8 %all-to-all-start.3 = ((bf16[8,4,64,128]{3,2,1,0:T(8,128)(2,1)}), bf16[8,4,64,128]{3,2,1,0:T(8,128)(2,1)S(1)}, u32[]{:S(2)}, u32[]{:S(2)}) async-start(bf16[8,4,64,128]{3,2,1,0:T(8,128)(2,1)} %bitcast.90), calls=%async_computation.3 | async-start | bytes 1048576 | tf_op jit(solution)/shard_map/all_to_all | solution.py:895
  106.2 21.9 %collective-permute-start.4 = (bf16[16,32,1536]{2,1,0:T(8,128)(2,1)}, bf16[16,32,1536]{2,1,0:T(8,128)(2,1)S(1)}, u32[]{:S(2)}, u32[]{:S(2)}) collective-permute-start(bf16[16,32,1536]{2,1,0:T(8,128)(2,1)} %get-tuple-element.126), channel_id=1, source_target_pairs={{0,16},{1,17},{2,18},{3,19},{4,20},{5,21},{6,22},{7,23},{8,9},{9,8... | collective-permute-start | bytes 4718600 | tf_op jit(solution)/shard_map/ppermute | solution.py:892
  107.8 8.5 %collective-permute-start.6 = (bf16[4,4,64,128]{3,2,1,0:T(8,128)(2,1)S(1)}, bf16[4,4,64,128]{3,2,1,0:T(8,128)(2,1)S(1)}, u32[]{:S(2)}, u32[]{:S(2)}) collective-permute-start(bf16[4,4,64,128]{3,2,1,0:T(8,128)(2,1)S(1)} %multiply_convert_fusion.1), channel_id=1, source_target_pairs={{0,8},{1,9},{2,10},{3,11},{4,12},{5,13},{6,14},{7,15},{8,0},{9,1},... | collective-permute-start | bytes 786440 | tf_op jit(solution)/shard_map/ppermute | solution.py:892
  107.9 20.3 %collective-permute-start.5 = (bf16[16,16,1536]{2,1,0:T(8,128)(2,1)}, bf16[16,16,1536]{2,1,0:T(8,128)(2,1)S(1)}, u32[]{:S(2)}, u32[]{:S(2)}) collective-permute-start(bf16[16,16,1536]{2,1,0:T(8,128)(2,1)} %get-tuple-element.127), channel_id=1, source_target_pairs={{0,2},{1,3},{2,0},{3,1},{4,6},{5,7},{6,4},{7,5},{8,10},{9,11},{10,... | collective-permute-start | bytes 2359304 | tf_op jit(solution)/shard_map/ppermute | solution.py:892
  109.8 12.5 %collective-permute-start.7 = (f32[2,2,64,128]{3,2,1,0:T(8,128)S(1)}, f32[2,2,64,128]{3,2,1,0:T(8,128)S(1)}, u32[]{:S(2)}, u32[]{:S(2)}) collective-permute-start(f32[2,2,64,128]{3,2,1,0:T(8,128)S(1)} %dynamic-slice_bitcast_fusion), channel_id=1, source_target_pairs={{0,8},{1,9},{2,10},{3,11},{4,12},{5,13},{6,14},{7,15},{8,0},{9,1},... | collective-permute-start | bytes 393224 | tf_op jit(solution)/shard_map/ppermute | solution.py:892
  128.2 24.0 %collective-permute-start.8 = (bf16[8,112,1024]{2,1,0:T(8,128)(2,1)}, bf16[8,112,1024]{2,1,0:T(8,128)(2,1)}, u32[]{:S(2)}, u32[]{:S(2)}) collective-permute-start(bf16[8,112,1024]{2,1,0:T(8,128)(2,1)} %get-tuple-element.137), channel_id=1, source_target_pairs={{0,16},{1,17},{2,18},{3,19},{4,20},{5,21},{6,22},{7,23},{8,9},{9,8... | collective-permute-start | bytes 5505032 | tf_op jit(solution)/shard_map/ppermute | solution.py:892
  131.0 21.2 %collective-permute-start.9 = (bf16[8,16,1536]{2,1,0:T(8,128)(2,1)}, bf16[8,16,1536]{2,1,0:T(8,128)(2,1)}, u32[]{:S(2)}, u32[]{:S(2)}) collective-permute-start(bf16[8,16,1536]{2,1,0:T(8,128)(2,1)} %get-tuple-element.140), channel_id=1, source_target_pairs={{0,4},{1,5},{2,6},{3,7},{4,0},{5,1},{6,2},{7,3},{8,12},{9,13},{10,... | collective-permute-start | bytes 1179656 | tf_op jit(solution)/shard_map/ppermute | solution.py:892
  152.1 6.6 %collective-permute-start.10 = (bf16[2,512,1024]{2,1,0:T(8,128)(2,1)}, bf16[2,512,1024]{2,1,0:T(8,128)(2,1)}, u32[]{:S(2)}, u32[]{:S(2)}) collective-permute-start(bf16[2,512,1024]{2,1,0:T(8,128)(2,1)} %get-tuple-element.145), channel_id=1, source_target_pairs={{0,8},{1,9},{2,10},{3,11},{4,12},{5,13},{6,14},{7,15},{8,0},{9,1},... | collective-permute-start | bytes 6291464 | tf_op jit(solution)/shard_map/ppermute | solution.py:892
  152.2 13.9 %collective-permute-start.11 = (bf16[8,32,1536]{2,1,0:T(8,128)(2,1)}, bf16[8,32,1536]{2,1,0:T(8,128)(2,1)S(1)}, u32[]{:S(2)}, u32[]{:S(2)}) collective-permute-start(bf16[8,32,1536]{2,1,0:T(8,128)(2,1)} %get-tuple-element.150), channel_id=1, source_target_pairs={{0,1},{1,0},{2,3},{3,2},{4,5},{5,4},{6,7},{7,6},{8,24},{9,25},{10,... | collective-permute-start | bytes 2359304 | tf_op jit(solution)/shard_map/ppermute | solution.py:892
  166.1 14.5 %collective-permute-start.12 = (bf16[4,112,1024]{2,1,0:T(8,128)(2,1)}, bf16[4,112,1024]{2,1,0:T(8,128)(2,1)S(1)}, u32[]{:S(2)}, u32[]{:S(2)}) collective-permute-start(bf16[4,112,1024]{2,1,0:T(8,128)(2,1)} %get-tuple-element.158), channel_id=1, source_target_pairs={{0,1},{1,0},{2,3},{3,2},{4,5},{5,4},{6,7},{7,6},{8,24},{9,25},{10,... | collective-permute-start | bytes 2752520 | tf_op jit(solution)/shard_map/ppermute | solution.py:892
  169.0 11.5 %collective-permute-start.13 = (bf16[4,32,1536]{2,1,0:T(8,128)(2,1)}, bf16[4,32,1536]{2,1,0:T(8,128)(2,1)S(1)}, u32[]{:S(2)}, u32[]{:S(2)}) collective-permute-start(bf16[4,32,1536]{2,1,0:T(8,128)(2,1)} %get-tuple-element.159), channel_id=1, source_target_pairs={{0,2},{1,3},{2,0},{3,1},{4,6},{5,7},{6,4},{7,5},{8,10},{9,11},{10,... | collective-permute-start | bytes 1179656 | tf_op jit(solution)/shard_map/ppermute | solution.py:892
  170.3 10.2 %collective-permute-start.15 = (f32[2,64,128]{2,1,0:T(8,128)}, f32[2,64,128]{2,1,0:T(8,128)S(1)}, u32[]{:S(2)}, u32[]{:S(2)}) collective-permute-start(f32[2,64,128]{2,1,0:T(8,128)} %dynamic-slice_bitcast_fusion.1), channel_id=1, source_target_pairs={{0,16},{1,17},{2,18},{3,19},{4,20},{5,21},{6,22},{7,23},{8,24},{9,... | collective-permute-start | bytes 196616 | tf_op jit(solution)/shard_map/ppermute | solution.py:892
  170.8 9.7 %collective-permute-start.14 = (f32[32,128]{1,0:T(8,128)S(1)}, f32[32,128]{1,0:T(8,128)S(1)}, u32[]{:S(2)}, u32[]{:S(2)}) collective-permute-start(f32[32,128]{1,0:T(8,128)S(1)} %get-tuple-element.163), channel_id=1, source_target_pairs={{0,2},{1,3},{2,0},{3,1},{4,6},{5,7},{6,4},{7,5},{8,10},{9,11},{10,... | collective-permute-start | bytes 49160 | tf_op jit(solution)/shard_map/ppermute | solution.py:892
  180.8 15.9 %collective-permute-start.16 = (bf16[2,112,1024]{2,1,0:T(8,128)(2,1)S(1)}, bf16[2,112,1024]{2,1,0:T(8,128)(2,1)S(1)}, u32[]{:S(2)}, u32[]{:S(2)}) collective-permute-start(bf16[2,112,1024]{2,1,0:T(8,128)(2,1)S(1)} %get-tuple-element.169), channel_id=1, source_target_pairs={{0,2},{1,3},{2,0},{3,1},{4,6},{5,7},{6,4},{7,5},{8,10},{9,11},{10,... | collective-permute-start | bytes 1376264 | tf_op jit(solution)/shard_map/ppermute | solution.py:892
  182.2 26.9 %copy-start.13 = (s32[7]{0:T(128)S(1)}, s32[7]{0:T(128)}, u32[]{:S(2)}) copy-start(s32[7]{0:T(128)} %stack.31.core.s) | copy-start | bytes 88
  182.4 28.2 %copy-start.17 = (f32[2,2,64,128]{3,2,1,0:T(8,128)S(1)}, f32[2,2,64,128]{3,2,1,0:T(8,128)}, u32[]{:S(2)}) copy-start(f32[2,2,64,128]{3,2,1,0:T(8,128)} %copy-done.16) | copy-start | bytes 393220
  182.4 13.2 %collective-permute-start.18 = (bf16[2,32,1536]{2,1,0:T(8,128)(2,1)S(1)}, bf16[2,32,1536]{2,1,0:T(8,128)(2,1)S(1)}, u32[]{:S(2)}, u32[]{:S(2)}) collective-permute-start(bf16[2,32,1536]{2,1,0:T(8,128)(2,1)S(1)} %get-tuple-element.171), channel_id=1, source_target_pairs={{0,4},{1,5},{2,6},{3,7},{4,0},{5,1},{6,2},{7,3},{8,12},{9,13},{10,... | collective-permute-start | bytes 589832 | tf_op jit(solution)/shard_map/ppermute | solution.py:892
  184.9 10.6 %collective-permute-start.17 = (bf16[4,16,1536]{2,1,0:T(8,128)(2,1)S(1)}, bf16[4,16,1536]{2,1,0:T(8,128)(2,1)S(1)}, u32[]{:S(2)}, u32[]{:S(2)}) collective-permute-start(bf16[4,16,1536]{2,1,0:T(8,128)(2,1)S(1)} %get-tuple-element.170), channel_id=1, source_target_pairs={{0,16},{1,17},{2,18},{3,19},{4,20},{5,21},{6,22},{7,23},{8,9},{9,8... | collective-permute-start | bytes 589832 | tf_op jit(solution)/shard_map/ppermute | solution.py:892
  185.5 5.3 %collective-permute-start.19 = (f32[32,128]{1,0:T(8,128)S(1)}, f32[32,128]{1,0:T(8,128)S(1)}, u32[]{:S(2)}, u32[]{:S(2)}) collective-permute-start(f32[32,128]{1,0:T(8,128)S(1)} %add.95), channel_id=1, source_target_pairs={{0,16},{1,17},{2,18},{3,19},{4,20},{5,21},{6,22},{7,23},{8,9},{9,8... | collective-permute-start | bytes 49160 | tf_op jit(solution)/shard_map/ppermute | solution.py:892
  190.8 3.7 %collective-permute-start.20 = (f32[32,128]{1,0:T(8,128)S(1)}, f32[32,128]{1,0:T(8,128)S(1)}, u32[]{:S(2)}, u32[]{:S(2)}) collective-permute-start(f32[32,128]{1,0:T(8,128)S(1)} %add.96), channel_id=1, source_target_pairs={{0,1},{1,0},{2,3},{3,2},{4,5},{5,4},{6,7},{7,6},{8,24},{9,25},{10,... | collective-permute-start | bytes 49160 | tf_op jit(solution)/shard_map/ppermute | solution.py:892
  196.8 12.3 %collective-permute-start.21 = (bf16[1,112,1024]{2,1,0:T(8,128)(2,1)S(1)}, bf16[1,112,1024]{2,1,0:T(8,128)(2,1)S(1)}, u32[]{:S(2)}, u32[]{:S(2)}) collective-permute-start(bf16[1,112,1024]{2,1,0:T(8,128)(2,1)S(1)} %get-tuple-element.179), channel_id=1, source_target_pairs={{0,4},{1,5},{2,6},{3,7},{4,0},{5,1},{6,2},{7,3},{8,12},{9,13},{10,... | collective-permute-start | bytes 688136 | tf_op jit(solution)/shard_map/ppermute | solution.py:892
  199.2 10.0 %collective-permute-start.22 = (bf16[2,16,1536]{2,1,0:T(8,128)(2,1)S(1)}, bf16[2,16,1536]{2,1,0:T(8,128)(2,1)S(1)}, u32[]{:S(2)}, u32[]{:S(2)}) collective-permute-start(bf16[2,16,1536]{2,1,0:T(8,128)(2,1)S(1)} %get-tuple-element.180), channel_id=1, source_target_pairs={{0,1},{1,0},{2,3},{3,2},{4,5},{5,4},{6,7},{7,6},{8,24},{9,25},{10,... | collective-permute-start | bytes 294920 | tf_op jit(solution)/shard_map/ppermute | solution.py:892
  200.7 8.4 %collective-permute-start.23 = (f32[32,128]{1,0:T(8,128)S(1)}, f32[32,128]{1,0:T(8,128)S(1)}, u32[]{:S(2)}, u32[]{:S(2)}) collective-permute-start(f32[32,128]{1,0:T(8,128)S(1)} %add.97), channel_id=1, source_target_pairs={{0,4},{1,5},{2,6},{3,7},{4,0},{5,1},{6,2},{7,3},{8,12},{9,13},{10,... | collective-permute-start | bytes 49160 | tf_op jit(solution)/shard_map/ppermute | solution.py:892
  210.5 1.7 collective-permute-start.24
  (19 other events, 147.5 us)

commit v2 on v1

--- a/solution.py
+++ b/solution.py
@@ -110,10 +110,10 @@
             xj.append(mm(xc, flip).astype(bf16) * tail)
         for c in range(SUB):
             powers(rt[c : c + 1], pt, c)
-            p = pt[c]
-            put(ss, c, mm(xj[c], p), rows)
-            k2 = mm(cf2, p, NT)
+            k2 = mm(cf2, pt[c], NT)
             kr[c : c + 1, :] = k2[c : c + 1] + k2[SUB + c : SUB + c + 1]
+        for c in range(SUB):
+            put(ss, c, mm(xj[c], pt[c]), rows)
         for c in range(SUB):
             k = jnp.broadcast_to(kr[c : c + 1, :], (T, T))
             kb = pltpu.roll(k, 0, 1, stride=1, stride_axis=0)
@@ -145,9 +145,9 @@
 
 
 def bwd_kernel(
-    groups, keep, x, dy, rate, coef, ins, insj, head, tailj, hs, toe,
-    dv, rates, pt, s1, e0, e1, near, gacc, nr, xs, ys,
+    groups, keep, x, dy, rate, coef, ins, insj, head, tailj, hs, toe, *rest
 ):
+    dv, rates, pt, s1, e0, e1, near, gacc, nr, xs, ys = rest[-11:]
     rows = ins.shape[0]
     n = rate.shape[1]
     flip = flip_matrix()
@@ -262,15 +262,15 @@
     return groups, keep, ins, insj, head, tailj
 
 
-def ssm_specs(rows, n):
+def ssm_specs(rows, n, first=0):
     full = pl.BlockSpec((rows, T), lambda i: (0, 0))
     return dict(
         sm=pl.BlockSpec(memory_space=pltpu.SMEM),
         full=full,
-        ch=pl.BlockSpec((rows, GROUP, T), lambda i: (0, i, 0)),
-        par=pl.BlockSpec((GROUP, n), lambda i: (i, 0)),
-        hs=pl.BlockSpec((GROUP // SUB, n // T, rows * SUB, T), lambda i: (i, 0, 0, 0)),
-        toe=pl.BlockSpec((GROUP, T, T), lambda i: (i, 0, 0)),
+        ch=pl.BlockSpec((rows, GROUP, T), lambda i: (0, i + first, 0)),
+        par=pl.BlockSpec((GROUP, n), lambda i: (i + first, 0)),
+        hs=pl.BlockSpec((GROUP // SUB, n // T, rows * SUB, T), lambda i: (i + first, 0, 0, 0)),
+        toe=pl.BlockSpec((GROUP, T, T), lambda i: (i + first, 0, 0)),
         big=pltpu.VMEM((n // T, rows * SUB, T), f32),
         pt=pltpu.VMEM((SUB, T, n), bf16),
         near=pltpu.VMEM((SUB, rows, T), f32),
@@ -300,19 +300,22 @@
     )(masks[0], masks[1], x, rate, coef, *masks[2:])
 
 
-def ssm_bwd(x, dy, rate, coef, masks, hs, toe, row_n):
+def ssm_bwd(x, dy, rate, coef, masks, hs, toe, row_n, part=0, parts=1, held=()):
     rows, chans, _ = x.shape
     n = rate.shape[1]
-    s = ssm_specs(rows, n)
+    steps = chans // GROUP // parts
+    s = ssm_specs(rows, n, part * steps)
+    raw = pl.BlockSpec(memory_space=pl.ANY)
     return pl.pallas_call(
         bwd_kernel,
-        grid=(chans // GROUP,),
+        grid=(steps,),
         in_specs=[s["sm"], s["sm"], s["ch"], s["ch"], s["par"], s["par"]]
         + [s["full"]] * 4
-        + [s["hs"], s["toe"]],
+        + [s["hs"], s["toe"]]
+        + [raw] * len(held),
         out_specs=[
             s["ch"],
-            pl.BlockSpec((2, row_n // 2, 2, GROUP, n // row_n), lambda i: (0, 0, 0, i, 0)),
+            pl.BlockSpec((2, row_n // 2, 2, GROUP, n // row_n), lambda i: (0, 0, 0, i + part * steps, 0)),
         ],
         out_shape=[
             pltpu.HBM(x.shape, bf16),
@@ -331,12 +334,14 @@
         ],
         compiler_params=pltpu.CompilerParams(vmem_limit_bytes=16 * 2**20),
         cost_estimate=s["cost"],
+        input_output_aliases={12 + i: i for i in range(len(held))},
         name="ssm_bwd",
-    )(masks[0], masks[1], x, dy, rate, coef, *masks[2:], *from_hbm(hs, toe))
+    )(masks[0], masks[1], x, dy, rate, coef, *masks[2:], *from_hbm(hs, toe), *held)
 
 
 epsilon = 1e-05
 TILE = 768
+BLOCK_COLS = 256
 
 
 def gauss_cdf(a):
@@ -416,79 +421,103 @@
     )
 
 
-def gate_kernel(
-    core, n_own, n_oth, g_own, g_oth, w_up, w_mix, w_down,
-    u_act, d_slope, d_yproj, normed_t, dy_own, dy_oth, ga, na, acc,
-):
-    j = pl.program_id(0)
-    own = n_own.shape[0]
-
-    @pl.when(j == 0)
-    def _():
-        for h, (n, g) in enumerate(((n_own, g_own), (n_oth, g_oth))):
-            na[h * own : (h + 1) * own, :] = n[...]
-            ga[h * own : (h + 1) * own, :] = g[...]
-            normed_t[:, h * own : (h + 1) * own] = n[...].T
-
-    u = mm(na[...], w_up[...])
-    d = mm(ga[...], w_down[...], NT)
+def gate_tile(normed, grad, w_up, w_mix, w_down, u_act, d_slope, d_yproj):
+    u = mm(normed, w_up[...])
+    d = mm(grad, w_down[...], NT)
     cdf = gauss_cdf(u)
     act = u * cdf
     u_act[...] = act.astype(bf16)
     d_slope[...] = (d * (cdf + u * gauss_pdf(u))).astype(bf16)
     dyp = (d * act).astype(bf16)
     d_yproj[...] = dyp
-    part = mm(dyp, w_mix[...], NT)
+    return mm(dyp, w_mix[...], NT)
+
+
+def gate_first_kernel(
+    core, n_own, n_oth, g_own, g_oth, w_up, w_mix, w_down,
+    u_act, d_slope, d_yproj, na, ga, acc,
+):
+    own = n_own.shape[0]
+    for h, (n, g) in enumerate(((n_own, g_own), (n_oth, g_oth))):
+        na[h * own : (h + 1) * own, :] = n[...]
+        ga[h * own : (h + 1) * own, :] = g[...]
+    acc[...] = gate_tile(na[...], ga[...], w_up, w_mix, w_down, u_act, d_slope, d_yproj)
+
+
+def gate_last_kernel(
+    core, na, ga, acc, w_up, w_mix, w_down, _u, _s, _d,
+    u_act, d_slope, d_yproj, normed_t, dy_own, dy_oth, sums,
+):
+    j = pl.program_id(0)
+    own = na.shape[0] // 2
 
     @pl.when(j == 0)
     def _():
-        acc[...] = part
-
-    @pl.when(j > 0)
-    def _():
-        acc[...] += part
+        sums[...] = acc[...]
+        normed_t[...] = na[...].T
+
+    sums[...] += gate_tile(na[...], ga[...], w_up, w_mix, w_down, u_act, d_slope, d_yproj)
 
     @pl.when(j == pl.num_programs(0) - 1)
     def _():
         shape = (dy_own.shape[0], dy_own.shape[2], T)
         for q in range(dy_own.shape[1]):
-            dy_own[:, q] = acc[q * T : (q + 1) * T, :].T.reshape(shape)
-            dy_oth[:, q] = acc[own + q * T : own + (q + 1) * T, :].T.astype(bf16).reshape(shape)
-
-
-def gate_call(core, normed, normed_oth, grad, grad_oth, w_up, w_mix, w_down, row_n, chan_n):
+            dy_own[:, q] = sums[q * T : (q + 1) * T, :].T.reshape(shape)
+            dy_oth[:, q] = sums[own + q * T : own + (q + 1) * T, :].T.astype(bf16).reshape(shape)
+
+
+def gate_specs(own, w_mix, row_n, first):
+    inner, ff = w_mix.shape
+    part = ff // row_n
+    col = lambda j, s: 2 * (j + first) + s[0]
+    return [
+        lambda width: pl.BlockSpec((width, part), lambda j, s: (0, col(j, s))),
+        pl.BlockSpec((inner, part), lambda j, s: (0, col(j, s))),
+        lambda width: pl.BlockSpec((part, width), lambda j, s: (col(j, s), 0)),
+        pl.BlockSpec((2 * own, part), lambda j, s: (0, j + first)),
+    ]
+
+
+def gate_first(core, normed, normed_oth, grad, grad_oth, w_up, w_mix, w_down, row_n):
     own, width = normed.shape
     inner, ff = w_mix.shape
-    per = ff // row_n // TILE
-    half = ff // 2
-    col = lambda j, s: (2 * (j // per) + s[0]) * per + j % per
+    up, mix, down, tile = gate_specs(own, w_mix, row_n, 0)
     tok = whole((own, width))
-    tile = pl.BlockSpec((2 * own, TILE), lambda j, s: (0, j))
+    pair = (2 * own, width)
+    return call(
+        gate_first_kernel,
+        "gate_first",
+        (1,),
+        [tok, tok, tok, tok, up(width), mix, down(width)],
+        [tile, tile, tile, whole(pair), whole(pair), whole((2 * own, inner))],
+        [in_hbm((2 * own, ff // 2), bf16)] * 3
+        + [in_hbm(pair, bf16), in_hbm(pair, bf16), in_hbm((2 * own, inner), f32)],
+        from_hbm(normed, normed_oth, grad, grad_oth, w_up, w_mix, w_down),
+        scalars=core,
+        vmem=44,
+    )
+
+
+def gate_last(core, pair_normed, pair_grad, acc, w_up, w_mix, w_down, held, row_n, chan_n):
+    own, width = pair_normed.shape[0] // 2, pair_normed.shape[1]
+    inner, ff = w_mix.shape
+    up, mix, down, tile = gate_specs(own, w_mix, row_n, 1)
+    pair = (2 * own, width)
+    raw = pl.BlockSpec(memory_space=pl.ANY)
     spread = (chan_n, own // T, inner // chan_n, T)
     return call(
-        gate_kernel,
-        "gate",
-        (half // TILE,),
-        [
-            tok,
-            tok,
-            tok,
-            tok,
-            pl.BlockSpec((width, TILE), lambda j, s: (0, col(j, s))),
-            pl.BlockSpec((inner, TILE), lambda j, s: (0, col(j, s))),
-            pl.BlockSpec((TILE, width), lambda j, s: (col(j, s), 0)),
-        ],
-        [tile, tile, tile, whole((width, 2 * own)), whole(spread), whole(spread), whole((2 * own, width))],
-        [in_hbm((2 * own, half), bf16)] * 3
-        + [in_hbm((width, 2 * own), bf16), in_hbm(spread, f32), in_hbm(spread, bf16)]
-        + [in_hbm((2 * own, width), bf16)],
-        from_hbm(normed, normed_oth, grad, grad_oth, w_up, w_mix, w_down),
+        gate_last_kernel,
+        "gate_last",
+        (row_n // 2 - 1,),
+        [whole(pair), whole(pair), whole(acc.shape), up(width), mix, down(width), raw, raw, raw],
+        [tile, tile, tile, whole((width, 2 * own)), whole(spread), whole(spread)],
+        [in_hbm((2 * own, ff // 2), bf16)] * 3
+        + [in_hbm((width, 2 * own), bf16), in_hbm(spread, f32), in_hbm(spread, bf16)],
+        from_hbm(pair_normed, pair_grad, acc, w_up, w_mix, w_down, *held),
         scalars=core,
-        scratch=[
-            pltpu.VMEM((2 * own, width), bf16),
-            pltpu.VMEM((2 * own, inner), f32),
-        ],
-        vmem=56,
+        scratch=[pltpu.VMEM(acc.shape, f32)],
+        aliases={7: 0, 8: 1, 9: 2},
+        vmem=48,
     )
 
 
@@ -585,88 +614,54 @@
             pltpu.VMEM((width, TILE), bf16),
             pltpu.VMEM((inner, TILE), bf16),
         ],
-        vmem=56,
+        vmem=32,
         cost=10**10,
     )
 
 
-def block_kernel(s, gate, d_upre, w_down, w_up, block_own, dn_own, oth, acc):
-    j = pl.program_id(0)
+def block_kernel(s, gate, d_upre, *refs):
+    half = (len(refs) - 3) // 2
+    downs, ups, (block_own, dn_own, oth) = refs[:half], refs[half : 2 * half], refs[2 * half :]
     own = block_own.shape[0]
-    sums = (mm(gate[...], w_down[...]), mm(d_upre[...], w_up[...], NT))
-
-    @pl.when(j == 0)
-    def _():
-        for k in (0, 1):
-            acc[k] = sums[k]
-
-    @pl.when(j > 0)
-    def _():
-        for k in (0, 1):
-            acc[k] += sums[k]
-
-    @pl.when(j == pl.num_programs(0) - 1)
-    def _():
-        block_own[...] = acc[0, :own]
-        dn_own[...] = acc[1, :own]
-        oth[...] = acc[:, own:].astype(bf16)
+    part = downs[0].shape[0]
+    cut = lambda ref, k: ref[:, k * part : (k + 1) * part]
+    block = sum(mm(cut(gate, k), w[...]) for k, w in enumerate(downs))
+    dn = sum(mm(cut(d_upre, k), w[...], NT) for k, w in enumerate(ups))
+    block_own[...] = block[:own]
+    dn_own[...] = dn[:own]
+    oth[0] = block[own:].astype(bf16)
+    oth[1] = dn[own:].astype(bf16)
 
 
 def block_call(scal, gate, d_upre, w_down, w_up, row_n):
     ff, width = w_down.shape
     own = gate.shape[0] // 2
     part = ff // row_n
-    tile = pl.BlockSpec((2 * own, part), lambda j, s: (0, j))
+    cols = BLOCK_COLS
+    out = pl.BlockSpec((own, cols), lambda j, s: (0, j))
+    ks = range(row_n // 2)
     return call(
         block_kernel,
         "block",
-        (row_n // 2,),
-        [
-            tile,
-            tile,
-            pl.BlockSpec((part, width), lambda j, s: (2 * j + s[0], 0)),
-            pl.BlockSpec((width, part), lambda j, s: (0, 2 * j + s[0])),
-        ],
-        [whole((own, width)), whole((own, width)), whole((2, own, width))],
+        (width // cols,),
+        [whole(gate.shape), whole(d_upre.shape)]
+        + [pl.BlockSpec((part, cols), lambda j, s, k=k: (2 * k + s[0], j)) for k in ks]
+        + [pl.BlockSpec((cols, part), lambda j, s, k=k: (j, 2 * k + s[0])) for k in ks],
+        [out, out, pl.BlockSpec((2, own, cols), lambda j, s: (0, 0, j))],
         [in_hbm((own, width), f32), in_hbm((own, width), f32), in_hbm((2, own, width), bf16)],
-        from_hbm(gate, d_upre, w_down, w_up),
+        from_hbm(gate, d_upre, *[w_down for _ in ks], *[w_up for _ in ks]),
         scalars=scal,
-        scratch=[pltpu.VMEM((2, 2 * own, width), f32)],
-        vmem=56,
-    )
-
-
-def down_val_kernel(s, down_g, down_k, v_own, v_oth, normed_t, d_give, d_keep, vs, vt):
-    i = pl.program_id(0)
-    inner, pair = vt.shape
-    m = vs.shape[0] // 32
-    rows = down_g.shape[0]
-
-    @pl.when(i == 0)
-    def _():
-        for h, v in enumerate((v_own, v_oth)):
-            for q in range(v.shape[1]):
-                at = h * pair // 2 + q * T
-                vt[:, at : at + T] = v[:, q].reshape(inner, T)
-        vs[...] = mm(normed_t[...], vt[...], NT)
-
-    b, low, high = i // 4, (i // 2) % 2, i % 2
-    for sel, down, out in ((1, down_g, d_give), (0, down_k, d_keep)):
-        out[0, 0:rows, :] = down[...]
-        a = mine_a(s) ^ sel
-        cut = []
-        for core in (0, 1):
-            at = pl.multiple_of(row_block(s, a, b, core, high, low) * m, m)
-            cut.append(vs[pl.ds(at, m), :])
-        parts = [jnp.concatenate([c[r * 8 : r * 8 + 8] for c in cut], 0) for r in range(m // 8)]
-        out[0, rows : rows + 16, :] = jnp.concatenate(parts, 1).astype(bf16)
-
-
-def down_val_call(scal, down, d_vpre, v_oth, normed_t):
-    half = v_oth.shape
-    inner = half[0] * half[2]
-    width, pair = normed_t.shape
-    rows = down.shape[0] // 16
+        vmem=36,
+    )
+
+
+def split_kernel(s, down_g, down_k, d_give, d_keep):
+    d_give[0] = down_g[...]
+    d_keep[0] = down_k[...]
+
+
+def split_call(scal, down):
+    rows, width = down.shape[0] // 16, down.shape[1]
 
     def block_of(sel):
         def at(i, s):
@@ -677,22 +672,60 @@
 
         return pl.BlockSpec((rows, width), at)
 
-    buf = (8, rows + 16, width)
-    out = pl.BlockSpec((1, rows + 16, width), lambda i, s: (i, 0, 0))
+    out = pl.BlockSpec((1, rows, width), lambda i, s: (i, 0, 0))
     return call(
-        down_val_kernel,
-        "down_val",
+        split_kernel,
+        "split",
         (8,),
+        [block_of(1), block_of(0)],
+        [out, out],
+        [struct((8, rows, width), bf16)] * 2,
+        (down, down),
+        scalars=scal,
+    )
+
+
+def val_kernel(s, v_own, v_oth, normed_t, v_give, v_keep, vs, vt):
+    inner, pair = vt.shape
+    for h, v in enumerate((v_own, v_oth)):
+        for q in range(v.shape[1]):
+            at = h * pair // 2 + q * T
+            vt[:, at : at + T] = v[:, q].reshape(inner, T)
+    vs[...] = mm(normed_t[...], vt[...], NT)
+    m = vs.shape[0] // 32
+    for sel, out in ((1, v_give), (0, v_keep)):
+        a = mine_a(s) ^ sel
+        for b in (0, 1):
+            for low in (0, 1):
+                for high in (0, 1):
+                    cut = []
+                    for core in (0, 1):
+                        at = pl.multiple_of(row_block(s, a, b, core, high, low) * m, m)
+                        cut.append(vs[pl.ds(at, m), :])
+                    parts = [
+                        jnp.concatenate([c[r * 8 : r * 8 + 8] for c in cut], 0)
+                        for r in range(m // 8)
+                    ]
+                    out[b * 4 + low * 2 + high] = jnp.concatenate(parts, 1).astype(bf16)
+
+
+def val_call(scal, d_vpre, v_oth, normed_t):
+    half = v_oth.shape
+    inner = half[0] * half[2]
+    width, pair = normed_t.shape
+    buf = (8, 16, width)
+    return call(
+        val_kernel,
+        "val",
+        (1,),
         [
-            block_of(1),
-            block_of(0),
             pl.BlockSpec(half, lambda i, s: (s[0], 0, 0, 0)),
             whole(half),
             whole(normed_t.shape),
         ],
-        [out, out],
+        [whole(buf), whole(buf)],
         [struct(buf, bf16)] * 2,
-        (down, down, d_vpre, v_oth, normed_t),
+        (d_vpre, v_oth, normed_t),
         scalars=scal,
         scratch=[pltpu.VMEM((width, inner), f32), pltpu.VMEM((inner, pair), bf16)],
     )
@@ -786,34 +819,33 @@
     )
 
 
-def finish_kernel(s, u_keep, u_got, m_keep, m_got, d_keep, d_got, norm, down, mine, other):
-    d = d_keep[0].astype(f32) + d_got[0].astype(f32)
-    rows = down.shape[0]
-    down[...] = d[:rows]
-    half = d.shape[1]
+def finish_kernel(s, u_keep, u_got, m_keep, m_got, d_keep, d_got, v_keep, v_got, norm, down, mine, other):
+    down[...] = d_keep[0].astype(f32) + d_got[0].astype(f32)
+    v = v_keep[0].astype(f32) + v_got[0].astype(f32)
+    half = v.shape[1]
     um, mx = u_keep.shape[1], m_keep.shape[1]
     tail = um + mx + 8
     for out, core, owner in ((mine, s[0], s[5]), (other, 1 - s[0], s[6])):
         out[0:um, :] = u_keep[core].astype(f32) + u_got[core].astype(f32)
         out[um : um + mx, :] = m_keep[core].astype(f32) + m_got[core].astype(f32)
-        out[um + mx : tail, 0:half] = jnp.where(core == 0, d[rows : rows + 8], d[rows + 8 :])
+        out[um + mx : tail, 0:half] = jnp.where(core == 0, v[:8], v[8:])
         out[um + mx : tail, half:] = jnp.zeros((8, out.shape[1] - half), f32)
         out[tail:, :] = jnp.zeros((8, out.shape[1]), f32)
         out[tail : tail + 1, 0:T] = norm[pl.ds(owner, 1), :]
 
 
-def finish_call(scal, up, mix, down, norm):
+def finish_call(scal, up, mix, down, val, norm):
     um, mx, half = up[0].shape[1], mix[0].shape[1], up[0].shape[2]
     rows, width = down[0].shape[1:]
-    args = (*up, *mix, *down, norm)
+    args = (*up, *mix, *down, *val, norm)
     pack = (um + mx + 16, half)
     return call(
         finish_kernel,
         "finish",
         (1,),
         [whole(a.shape) for a in args],
-        [whole((rows - 16, width)), whole(pack), whole(pack)],
-        [struct((rows - 16, width), f32), struct(pack, f32), struct(pack, f32)],
+        [whole((rows, width)), whole(pack), whole(pack)],
+        [struct((rows, width), f32), struct(pack, f32), struct(pack, f32)],
         args,
         scalars=scal,
     )
@@ -902,89 +934,103 @@
         normed, v_act, v_slope = norm_call(tokens, layer_norm_gain, ln_bias, w_val, chan_n)
         normed_oth = send(normed, "core")
         v_chan = to_seq(trade(v_act))
-        u_act, d_slope, d_yproj, normed_t, dy_own, dy_oth, pair_grad = gate_call(
-            scal, normed, normed_oth, out_grad, grad_oth, w_up, w_mix, w_down, row_n, chan_n
+        *gated, pair_normed, pair_grad, acc = gate_first(
+            scal, normed, normed_oth, out_grad, grad_oth, w_up, w_mix, w_down, row_n
+        )
+        v_chan, acc = after((v_chan, acc))
+        y_chan, states, toeplitz = ssm_fwd(v_chan, decay_rate, mix_coef, masks)
+        y_chan, acc = after((y_chan, acc))
+        y_own = trade(to_tok(y_chan))
+        u_act, d_slope, d_yproj, normed_t, dy_own, dy_oth = gate_last(
+            scal, pair_normed, pair_grad, acc, w_up, w_mix, w_down, gated, row_n, chan_n
         )
         d_y = (dy_own + send(dy_oth, "core").astype(f32)).astype(bf16)
-        v_chan, d_y = after((v_chan, d_y))
+        y_own, d_y = after((y_own, d_y))
+        y_oth = send(y_own, "core")
         d_y_chan = to_seq(trade(d_y))
-        y_chan, states, toeplitz = ssm_fwd(v_chan, decay_rate, mix_coef, masks)
-        y_chan, d_y_chan = after((y_chan, d_y_chan))
-        y_own = trade(to_tok(y_chan))
-        d_v_chan, rates = ssm_bwd(
-            v_chan, d_y_chan, decay_rate, mix_coef, masks, states, toeplitz, row_n
-        )
-        y_own, d_v_chan = after((y_own, d_v_chan))
-        y_oth = send(y_own, "core")
-        y_oth, d_v_chan = after((y_oth, d_v_chan))
-        d_v = trade(to_tok(d_v_chan))
         gate_out, d_upre, u_give, u_keep, m_give, m_keep = mid_call(
             scal, y_own, y_oth, w_mix, u_act, d_slope, d_yproj, normed_t, row_n
         )
-        u_give, m_give, gate_out, d_v, rates = after((u_give, m_give, gate_out, d_v, rates))
+        u_give, m_give, gate_out, d_y_chan = after((u_give, m_give, gate_out, d_y_chan))
+        back = lambda part, held, d_y_chan: ssm_bwd(
+            v_chan, d_y_chan, decay_rate, mix_coef, masks, states, toeplitz, row_n, part, 2, held
+        )
 
         u_got = send(u_give, "a")
         m_got = send(m_give, "low")
+        down = mm(gate_out, pair_grad, TN).astype(bf16)
+        d_give, d_keep = split_call(scal, down)
+        held = back(0, (), d_y_chan)
+        u_got, m_got, d_give, gate_out, d_y_chan, *held = after(
+            (u_got, m_got, d_give, gate_out, d_y_chan, *held)
+        )
+
+        d_got = send(d_give, "a")
+        m_give, m_keep = step_call(bit_high, m_keep, m_got)
+        m_got = send(m_give, "high")
+        d_v_chan, rates = back(1, tuple(held), d_y_chan)
+        u_give, u_keep = step_call(bit_b, u_keep, u_got)
+        d_v_chan, u_give, gate_out, rates = after((d_v_chan, u_give, gate_out, rates))
+        d_v = trade(to_tok(d_v_chan))
+        d_got, m_got, u_give = after((d_got, m_got, u_give))
+        u_got = send(u_give, "b")
+        block_own, dn_own, bd_give = block_call(scal, gate_out, d_upre, w_down, w_up, row_n)
+        d_give, d_keep = step_call(bit_b, d_keep, d_got)
         rates_give = lax.dynamic_index_in_dim(rates, 1 - core, 0, keepdims=False)
         rates_got = send(rates_give, "core")
+        u_got, d_give, bd_give, d_v, rates_got = after((u_got, d_give, bd_give, d_v, rates_got))
+
+        d_got = send(d_give, "b")
+        u_give, u_keep = step_call(bit_low, u_keep, u_got)
+        u_give, d_v, m_got = after((u_give, d_v, m_got))
+        u_got = send(u_give, "low")
         half = chan_n // 2
         other_half = lambda v: lax.dynamic_slice_in_dim(v, (1 - core) * half, half, 0)
         v_give = (other_half(d_v).astype(f32) * other_half(v_slope)).astype(bf16)
         v_got = send(v_give, "core")
+        bd_got = send(bd_give, "core")
         d_vpre = (d_v.astype(f32) * v_slope).astype(bf16)
-        down = mm(gate_out, pair_grad, TN).astype(bf16)
-        d_give, d_keep = down_val_call(scal, down, d_vpre, v_got, normed_t)
-        u_got, m_got, d_give, gate_out, rates_got = after(
-            (u_got, m_got, d_give, gate_out, rates_got)
-        )
-
-        d_got = send(d_give, "a")
-        m_give, m_keep = step_call(bit_high, m_keep, m_got)
-        m_got = send(m_give, "high")
-        u_give, u_keep = step_call(bit_b, u_keep, u_got)
-        block_own, dn_own, bd_give = block_call(scal, gate_out, d_upre, w_down, w_up, row_n)
-        d_got, m_got, u_give, bd_give = after((d_got, m_got, u_give, bd_give))
-
-        u_got = send(u_give, "b")
-        bd_got = send(bd_give, "core")
-        d_give, d_keep = step_call(bit_b, d_keep, d_got)
+        v_give, v_keep = val_call(scal, d_vpre, v_got, normed_t)
+        v_got = send(v_give, "a")
+        m_give, m_keep = step_call(bit_a, m_keep, m_got)
         rates = lax.dynamic_index_in_dim(rates, core, 0, keepdims=False) + rates_got
         rates_give = lax.dynamic_index_in_dim(rates, 1 - bit_x, 0, keepdims=False)
-        block_out, tokens_grad, norm_part = tail_call(
-            tokens, out_grad, layer_norm_gain, block_own, bd_got, dn_own, d_vpre, w_val,
-            row_n * chan_n,
-        )
-        u_got, d_give, norm_part, rates_give = after((u_got, d_give, norm_part, rates_give))
+        d_got, u_got, m_give, v_got, rates_give, d_vpre, bd_got = after(
+            (d_got, u_got, m_give, v_got, rates_give, d_vpre, bd_got)
+        )
 
         rates_got = send(rates_give, "x")
-        d_got = send(d_give, "b")
-        u_give, u_keep = step_call(bit_low, u_keep, u_got)
-        u_got = send(u_give, "low")
-        m_give, m_keep = step_call(bit_a, m_keep, m_got)
-        norm_part = norm_part + send(norm_part, "low")
-        d_got, u_got, m_give, norm_part, rates_got = after(
-            (d_got, u_got, m_give, norm_part, rates_got)
-        )
-        rates = lax.dynamic_index_in_dim(rates, bit_x, 0, keepdims=False) + rates_got
-
         d_give, d_keep = step_call(bit_low, d_keep, d_got)
         d_got = send(d_give, "low")
         u_give, u_keep = step_call(bit_high, u_keep, u_got)
         u_got = send(u_give, "high")
         m_got = send(m_give, "a")
-        norm_part = norm_part + send(norm_part, "a")
-        norm_part = norm_part + send(norm_part, "b")
-        d_got, m_got, u_got, norm_part = after((d_got, m_got, u_got, norm_part))
+        v_give, v_keep = step_call(bit_b, v_keep, v_got)
+        v_got = send(v_give, "b")
+        block_out, tokens_grad, norm_part = tail_call(
+            tokens, out_grad, layer_norm_gain, block_own, bd_got, dn_own, d_vpre, w_val,
+            row_n * chan_n,
+        )
+        d_got, m_got, u_got, v_got, norm_part, rates_got = after(
+            (d_got, m_got, u_got, v_got, norm_part, rates_got)
+        )
+        rates = lax.dynamic_index_in_dim(rates, bit_x, 0, keepdims=False) + rates_got
 
         d_give, d_keep = step_call(bit_high, d_keep, d_got)
         d_got = send(d_give, "high")
         m_give, m_keep = step_call(bit_b, m_keep, m_got)
         m_got = send(m_give, "b")
+        v_give, v_keep = step_call(bit_low, v_keep, v_got)
+        v_got = send(v_give, "low")
+        norm_part = norm_part + send(norm_part, "a") + send(norm_part, "b") + send(norm_part, "ab")
+        norm_part = norm_part + send(norm_part, "low")
+        d_got, m_got, v_got, norm_part = after((d_got, m_got, v_got, norm_part))
+
+        v_give, v_keep = step_call(bit_high, v_keep, v_got)
+        v_got = send(v_give, "high")
         norm_part = norm_part + send(norm_part, "high")
-        d_got, m_got, norm_part = after((d_got, m_got, norm_part))
-
         down_grad, mine, other = finish_call(
-            scal, (u_keep, u_got), (m_keep, m_got), (d_keep, d_got), norm_part
+            scal, (u_keep, u_got), (m_keep, m_got), (d_keep, d_got), (v_keep, v_got), norm_part
         )
         um, mx = u_keep.shape[1], m_keep.shape[1]
         other = send(other, "core")

time: 215 us -> 206 us (0.958)
  waiting for transfers between devices: 34.4 us -> 15.6 us
  starting transfers between devices: 47.8 us -> 55.5 us
  matrix products: 6.19 us -> 3.92 us
  other arithmetic: 4.46 us -> 6.61 us
    ppermute x25 -> x30, waiting for transfers between devices: 32.8 us -> 15.6 us  [send(): return lax.ppermute(value, ('row', 'chan'), pairs)]
    ppermute x25 -> x30, starting transfers between devices: 23.9 us -> 32.1 us  [send(): return lax.ppermute(value, ('row', 'chan'), pairs)]
    pallas_call x1 -> x2, Pallas kernels: 18.6 us -> 20.9 us  [ssm_bwd(): pl.pallas_call(bwd_kernel, grid=(steps,), in_specs=[s['sm'], s['sm'], s['...]
    dot_general x3, matrix products: 6.19 us -> 3.92 us  [mm(): return lax.dot_general(a, b, d, preferred_element_type=f32)]
    unnamed x44 -> x78, local copies, waits for them, and re-layouts: 5.08 us -> 6.98 us
    pallas_call x17 -> x22, Pallas kernels: 77.9 us -> 76.6 us  [call(): pl.pallas_call(kernel, grid_spec=pltpu.PrefetchScalarGridSpec(num_scalar_...]
  transfers between devices with their start and end apart: 29 -> 34, of which waited for: 12 -> 8; matrix products, arithmetic and copies ran while one was open for 6% -> 6% of each run, Pallas kernels for 48% -> 44%
where the time goes in v2:
time: 206 us; the launch traced here: 205 us
  Pallas kernels  110 us (53%)
  starting transfers between devices  55.5 us (27%)
  waiting for transfers between devices  15.6 us (8%)
  local copies, waits for them, and re-layouts  9.32 us (5%)
  other arithmetic  6.61 us (3%)
  between operations  3.97 us (2%)
  matrix products  3.92 us (2%)
    pallas_call x22, Pallas kernels, call(): pl.pallas_call(kernel, grid_spec=pltpu.PrefetchScalarGridSpec(num_scalar_...  76.6 us
    ppermute x30, starting transfers between devices, send(): return lax.ppermute(value, ('row', 'chan'), pairs)  32.1 us
    all_to_all x4, starting transfers between devices, on_device(): lax.all_to_all(v, 'chan', split_axis=0, concat_axis=0, tiled=True)  23.4 us
    pallas_call x2, Pallas kernels, ssm_bwd(): pl.pallas_call(bwd_kernel, grid=(steps,), in_specs=[s['sm'], s['sm'], s['...  20.9 us
    ppermute x30, waiting for transfers between devices, send(): return lax.ppermute(value, ('row', 'chan'), pairs)  15.6 us
    pallas_call x1, Pallas kernels, ssm_fwd(): pl.pallas_call(fwd_kernel, grid=(chans // GROUP,), in_specs=[s['sm'], s['...  12.3 us
    unnamed x78, local copies, waits for them, and re-layouts  6.98 us
  transfers between devices with their start and end apart: 34, of which 8 were waited for; matrix products, arithmetic and copies ran while one was open for 6% of the time, Pallas kernels for 44%

profile of v2, /device:TPU:0, one launch (start us, length us, event | category | flops | bytes accessed | tf_op | source)
XLA Modules:
  0.0 204.7 jit_solution(6158884410194056662)
XLA Ops:
  0.7 5.2 %norm_val.1 = (bf16[512,1024]{1,0:T(8,128)(2,1)S(1)}, bf16[8,4,64,128]{3,2,1,0:T(8,128)(2,1)}, f32[8,4,64,128]{3,2,1,0:T(8,128)S(1)}) custom-call(bf16[512,1024]{1,0:T(8,128)(2,1)} %tok.3, f32[1,1024]{1,0:T(1,128)} %bitcast.115, f32[1,1024]{1,0:T(1,128)} %bitcast.117, bf16[1024,512]{1,0:T(8,128)(2,1)} %w_val.3), custom_call_target="tpu_custom_call" | custom-call | tf_op jit(solution)/shard_map/norm_val/pallas_call | solution.py:373
  7.4 7.3 %all-to-all-start = ((bf16[8,4,64,128]{3,2,1,0:T(8,128)(2,1)}), bf16[8,4,64,128]{3,2,1,0:T(8,128)(2,1)S(1)}, u32[]{:S(2)}, u32[]{:S(2)}) async-start(bf16[8,4,64,128]{3,2,1,0:T(8,128)(2,1)} %get-tuple-element.128), calls=%async_computation | async-start | bytes 1048576 | tf_op jit(solution)/shard_map/all_to_all | solution.py:927
  19.0 10.9 %gate_first.1 = (bf16[1024,1536]{1,0:T(8,128)(2,1)}, bf16[1024,1536]{1,0:T(8,128)(2,1)}, bf16[1024,1536]{1,0:T(8,128)(2,1)}, bf16[1024,1024]{1,0:T(8,128)(2,1)},...) custom-call(s32[7]{0:T(128)S(1)} %stack.31.core.s, bf16[512,1024]{1,0:T(8,128)(2,1)} %copy-done.10, ...), custom_call_target="tpu_custom_call" | custom-call | tf_op jit(solution)/shard_map/gate_first/pallas_call | solution.py:373
  29.9 12.3 %ssm_fwd.1 = (bf16[32,64,128]{2,1,0:T(8,128)(2,1)}, f32[8,4,256,128]{3,2,1,0:T(8,128)}, bf16[64,128,128]{2,1,0:T(8,128)(2,1)}) custom-call(s32[1]{0:T(128)} %bitcast.10.groups, f32[32]{0:T(128)S(1)} %convert_reduce_fusion.keep, bf16[32,64,128]{2,1,0:T(8,128)(2,1)S(1)} %bitcast.101, f32[64,512]{1,0:T(8,128)S(1)} %copy-done.23, f32[64,512]{1,0:T(8,128)S(1)} %copy-done.25, ...), custom_call_target="tpu_custom_call" | custom-call | flops 20000000000 | bytes 10000000 | tf_op jit(solution)/shard_map/ssm_fwd/pallas_call | solution.py:286
  42.2 6.0 %all-to-all-start.1 = ((bf16[8,4,64,128]{3,2,1,0:T(8,128)(2,1)}), bf16[8,4,64,128]{3,2,1,0:T(8,128)(2,1)S(1)}, u32[]{:S(2)}, u32[]{:S(2)}) async-start(bf16[8,4,64,128]{3,2,1,0:T(8,128)(2,1)} %bitcast.111), calls=%async_computation.1 | async-start | bytes 1048576 | tf_op jit(solution)/shard_map/all_to_all | solution.py:927
  48.2 11.5 %gate_last.1 = (bf16[1024,1536]{1,0:T(8,128)(2,1)}, bf16[1024,1536]{1,0:T(8,128)(2,1)}, bf16[1024,1536]{1,0:T(8,128)(2,1)}, bf16[1024,1024]{1,0:T(8,128)(2,1)}, ...) custom-call(s32[7]{0:T(128)S(1)} %stack.31.core.s, ...), custom_call_target="tpu_custom_call", output_to_operand_aliasing={{0}: (7, {}), {1}: (8, {}), {2}: (9, {})} | custom-call | tf_op jit(solution)/shard_map/gate_last/pallas_call | solution.py:373
  59.7 2.1 %collective-permute-done.2 = bf16[8,4,64,128]{3,2,1,0:T(8,128)(2,1)S(1)} collective-permute-done((bf16[8,4,64,128]{3,2,1,0:T(8,128)(2,1)}, bf16[8,4,64,128]{3,2,1,0:T(8,128)(2,1)S(1)}, u32[]{:S(2)}, u32[]{:S(2)}) %collective-permute-start.2) | collective-permute-done | bytes 524320 | tf_op jit(solution)/shard_map/ppermute | solution.py:924
  61.8 2.2 %add_convert_fusion = bf16[8,4,64,128]{3,2,1,0:T(8,128)(2,1)} fusion(f32[8,4,64,128]{3,2,1,0:T(8,128)} %get-tuple-element.141, bf16[8,4,64,128]{3,2,1,0:T(8,128)(2,1)S(1)} %collective-permute-done.2), kind=kLoop, calls=%fused_computation.6 | loop fusion | flops 786432 | bytes 2097152 | tf_op jit(solution)/shard_map/convert_element_type | solution.py:947
  64.1 6.0 %all-to-all-start.2 = ((bf16[8,4,64,128]{3,2,1,0:T(8,128)(2,1)}), bf16[8,4,64,128]{3,2,1,0:T(8,128)(2,1)S(1)}, u32[]{:S(2)}, u32[]{:S(2)}) async-start(bf16[8,4,64,128]{3,2,1,0:T(8,128)(2,1)} %add_convert_fusion), calls=%async_computation.2 | async-start | bytes 1048576 | tf_op jit(solution)/shard_map/all_to_all | solution.py:927
  70.9 14.4 %mix_up.1 = (bf16[1024,1536]{1,0:T(8,128)(2,1)}, bf16[1024,1536]{1,0:T(8,128)(2,1)}, bf16[16,32,1536]{2,1,0:T(8,128)(2,1)}, bf16[16,32,1536]{2,1,0:T(8,128)(2,1)...) custom-call(s32[7]{0:T(128)S(1)} %stack.31.core.s, bf16[8,4,64,128]{3,2,1,0:T(8,128)(2,1)} %copy-done.36, ...), custom_call_target="tpu_custom_call" | custom-call | flops 10000000000 | bytes 10000000 | tf_op jit(solution)/shard_map/mix_up/pallas_call | solution.py:373
  85.4 1.6 collective-permute-start.4
  86.9 2.0 collective-permute-start.5
  89.0 10.4 %ssm_bwd.2 = (bf16[32,64,128]{2,1,0:T(8,128)(2,1)}, f32[2,2,2,64,128]{4,3,2,1,0:T(8,128)S(1)}) custom-call(s32[1]{0:T(128)} %bitcast.10.groups, f32[32]{0:T(128)S(1)} %convert_reduce_fusion.keep, bf16[32,64,128]{2,1,0:T(8,128)(2,1)S(1)} %bitcast.102, bf16[32,64,128]{2,1,0:T(8,128)(2,1)S(1)} %bitcast.104, f32[64,512]{1,0:T(8,128)S(1)} %copy-done.23, ...), custom_call_target="tpu_custom_call" | custom-call | flops 20000000000 | bytes 10000000 | tf_op jit(solution)/shard_map/ssm_bwd/pallas_call | solution.py:309
  99.4 3.7 %convolution_convert_fusion.down_g.down_k = bf16[1536,1024]{1,0:T(8,128)(2,1)S(1)} fusion(bf16[1024,1536]{1,0:T(8,128)(2,1)S(1)} %copy-done.34, bf16[1024,1024]{1,0:T(8,128)(2,1)S(1)} %copy-done.35), kind=kOutput, calls=%fused_computation | convolution fusion | flops 3222798336 | bytes 8388608 | tf_op jit(solution)/shard_map/dot_general | solution.py:20
  103.2 3.5 %split.1 = (bf16[8,96,1024]{2,1,0:T(8,128)(2,1)}, bf16[8,96,1024]{2,1,0:T(8,128)(2,1)S(1)}) custom-call(s32[7]{0:T(128)S(1)} %stack.31.core.s, bf16[1536,1024]{1,0:T(8,128)(2,1)S(1)} %convolution_convert_fusion.down_g.down_k, bf16[1536,1024]{1,0:T(8,128)(2,1)S(1)} %convolution_convert_fusion.down_g.down_k), custom_call_target="tpu_custom_call" | custom-call | tf_op jit(solution)/shard_map/split/pallas_call | solution.py:373
  109.5 2.4 %collective-permute-start.7 = (bf16[8,16,1536]{2,1,0:T(8,128)(2,1)}, bf16[8,16,1536]{2,1,0:T(8,128)(2,1)}, u32[]{:S(2)}, u32[]{:S(2)}) collective-permute-start(bf16[8,16,1536]{2,1,0:T(8,128)(2,1)} %get-tuple-element.176), channel_id=1, source_target_pairs={{0,4},{1,5},{2,6},{3,7},{4,0},{5,1},{6,2},{7,3},{8,12},{9,13},{10,... | collective-permute-start | bytes 1179656 | tf_op jit(solution)/shard_map/ppermute | solution.py:924
  111.9 10.5 %ssm_bwd.3 = (bf16[32,64,128]{2,1,0:T(8,128)(2,1)}, f32[2,2,2,64,128]{4,3,2,1,0:T(8,128)S(1)}) custom-call(s32[1]{0:T(128)} %bitcast.10.groups, f32[32]{0:T(128)S(1)} %copy-done.20, bf16[32,64,128]{2,1,0:T(8,128)(2,1)S(1)} %bitcast.103, bf16[32,64,128]{2,1,0:T(8,128)(2,1)S(1)} %bitcast.105, ...), custom_call_target="tpu_custom_call", output_to_operand_aliasing={{0}: (12, {}), {1}: (13, {})} | custom-call | flops 20000000000 | bytes 10000000 | tf_op jit(solution)/shard_map/ssm_bwd/pallas_call | solution.py:309
  124.9 4.1 %all-to-all-start.3 = ((bf16[8,4,64,128]{3,2,1,0:T(8,128)(2,1)}), bf16[8,4,64,128]{3,2,1,0:T(8,128)(2,1)}, u32[]{:S(2)}, u32[]{:S(2)}) async-start(bf16[8,4,64,128]{3,2,1,0:T(8,128)(2,1)} %bitcast.110), calls=%async_computation.3 | async-start | bytes 1048576 | tf_op jit(solution)/shard_map/all_to_all | solution.py:927
  129.1 1.9 collective-permute-start.8
  132.1 12.4 %block.1 = (f32[512,1024]{1,0:T(8,128)}, f32[512,1024]{1,0:T(8,128)}, bf16[2,512,1024]{2,1,0:T(8,128)(2,1)}) custom-call(s32[7]{0:T(128)S(1)} %copy-done.18, bf16[1024,1536]{1,0:T(8,128)(2,1)} %get-tuple-element.170.gate, bf16[1024,1536]{1,0:T(8,128)(2,1)} %get-tuple-element.171.d_upre, bf16[3072,1024]{1,0:T(8,128)(2,1)} %refs_1_.1, ...), custom_call_target="tpu_custom_call" | custom-call | tf_op jit(solution)/shard_map/block/pallas_call | solution.py:373
  148.6 2.2 %halve.15 = (bf16[4,32,1536]{2,1,0:T(8,128)(2,1)S(1)}, bf16[4,32,1536]{2,1,0:T(8,128)(2,1)S(1)}) custom-call(s32[1]{0:T(128)} %bitcast.4.bit, bf16[2,4,32,1536]{3,2,1,0:T(8,128)(2,1)S(1)} %bitcast.71, bf16[2,4,32,1536]{3,2,1,0:T(8,128)(2,1)} %bitcast.25.got_g.got_k, bf16[2,4,32,1536]{3,2,1,0:T(8,128)(2,1)S(1)} %bitcast.72, ...), custom_call_target="tpu_custom_call" | custom-call | tf_op jit(solution)/shard_map/halve/pallas_call | solution.py:373
  150.8 1.9 collective-permute-start.11
  155.4 2.0 halve.16
  160.9 1.6 collective-permute-done.11
  162.4 2.8 %collective-permute-done.13 = bf16[8,16,1024]{2,1,0:T(8,128)(2,1)S(1)} collective-permute-done((bf16[8,16,1024]{2,1,0:T(8,128)(2,1)S(1)}, bf16[8,16,1024]{2,1,0:T(8,128)(2,1)S(1)}, u32[]{:S(2)}, u32[]{:S(2)}) %collective-permute-start.13) | collective-permute-done | bytes 262176 | tf_op jit(solution)/shard_map/ppermute | solution.py:924
  167.3 2.4 %collective-permute-start.17 = (bf16[2,32,1536]{2,1,0:T(8,128)(2,1)S(1)}, bf16[2,32,1536]{2,1,0:T(8,128)(2,1)S(1)}, u32[]{:S(2)}, u32[]{:S(2)}) collective-permute-start(bf16[2,32,1536]{2,1,0:T(8,128)(2,1)S(1)} %get-tuple-element.212), channel_id=1, source_target_pairs={{0,4},{1,5},{2,6},{3,7},{4,0},{5,1},{6,2},{7,3},{8,12},{9,13},{10,... | collective-permute-start | bytes 589832 | tf_op jit(solution)/shard_map/ppermute | solution.py:924
  172.4 7.2 %norm_back.1 = (bf16[512,1024]{1,0:T(8,128)(2,1)}, f32[512,1024]{1,0:T(8,128)}, f32[32,128]{1,0:T(8,128)S(1)}) custom-call(bf16[512,1024]{1,0:T(8,128)(2,1)} %tok.3, bf16[512,1024]{1,0:T(8,128)(2,1)} %grad.1, f32[1,1024]{1,0:T(1,128)} %bitcast.116, f32[512,1024]{1,0:T(8,128)} %get-tuple-element.172.block_own, ...), custom_call_target="tpu_custom_call" | custom-call | tf_op jit(solution)/shard_map/norm_back/pallas_call | solution.py:373
  180.3 1.6 collective-permute-start.25
  185.3 1.8 collective-permute-start.21
  189.3 3.2 %collective-permute-done.26 = f32[32,128]{1,0:T(8,128)S(1)} collective-permute-done((f32[32,128]{1,0:T(8,128)S(1)}, f32[32,128]{1,0:T(8,128)S(1)}, u32[]{:S(2)}, u32[]{:S(2)}) %collective-permute-start.26) | collective-permute-done | bytes 16416 | tf_op jit(solution)/shard_map/ppermute | solution.py:924
  195.0 2.0 collective-permute-start.28
  197.0 2.6 %collective-permute-done.28 = f32[32,128]{1,0:T(8,128)S(1)} collective-permute-done((f32[32,128]{1,0:T(8,128)S(1)}, f32[32,128]{1,0:T(8,128)S(1)}, u32[]{:S(2)}, u32[]{:S(2)}) %collective-permute-start.28) | collective-permute-done | bytes 16416 | tf_op jit(solution)/shard_map/ppermute | solution.py:924
  (159 shorter events, 38.7 us)
Async XLA Ops:
  6.9 12.1 %collective-permute-start = (bf16[512,1024]{1,0:T(8,128)(2,1)S(1)}, bf16[512,1024]{1,0:T(8,128)(2,1)}, u32[]{:S(2)}, u32[]{:S(2)}) collective-permute-start(bf16[512,1024]{1,0:T(8,128)(2,1)S(1)} %get-tuple-element.129.n_own), channel_id=1, source_target_pairs={{0,8},{1,9},{2,10},{3,11},{4,12},{5,13},{6,14},{7,15},{8,0},{9,1},... | collective-permute-start | bytes 3145736 | tf_op jit(solution)/shard_map/ppermute | solution.py:924
  7.3 11.6 %collective-permute-start.1 = (bf16[512,1024]{1,0:T(8,128)(2,1)S(1)}, bf16[512,1024]{1,0:T(8,128)(2,1)}, u32[]{:S(2)}, u32[]{:S(2)}) collective-permute-start(bf16[512,1024]{1,0:T(8,128)(2,1)S(1)} %copy-done.33), channel_id=1, source_target_pairs={{0,8},{1,9},{2,10},{3,11},{4,12},{5,13},{6,14},{7,15},{8,0},{9,1},... | collective-permute-start | bytes 3145736 | tf_op jit(solution)/shard_map/ppermute | solution.py:924
  7.4 22.5 %all-to-all-start = ((bf16[8,4,64,128]{3,2,1,0:T(8,128)(2,1)}), bf16[8,4,64,128]{3,2,1,0:T(8,128)(2,1)S(1)}, u32[]{:S(2)}, u32[]{:S(2)}) async-start(bf16[8,4,64,128]{3,2,1,0:T(8,128)(2,1)} %get-tuple-element.128), calls=%async_computation | async-start | bytes 1048576 | tf_op jit(solution)/shard_map/all_to_all | solution.py:927
  42.2 21.7 %all-to-all-start.1 = ((bf16[8,4,64,128]{3,2,1,0:T(8,128)(2,1)}), bf16[8,4,64,128]{3,2,1,0:T(8,128)(2,1)S(1)}, u32[]{:S(2)}, u32[]{:S(2)}) async-start(bf16[8,4,64,128]{3,2,1,0:T(8,128)(2,1)} %bitcast.111), calls=%async_computation.1 | async-start | bytes 1048576 | tf_op jit(solution)/shard_map/all_to_all | solution.py:927
  63.9 6.2 %collective-permute-start.3 = (bf16[8,4,64,128]{3,2,1,0:T(8,128)(2,1)S(1)}, bf16[8,4,64,128]{3,2,1,0:T(8,128)(2,1)S(1)}, u32[]{:S(2)}, u32[]{:S(2)}) collective-permute-start(bf16[8,4,64,128]{3,2,1,0:T(8,128)(2,1)S(1)} %all-to-all-done.1.y_own), channel_id=1, source_target_pairs={{0,8},{1,9},{2,10},{3,11},{4,12},{5,13},{6,14},{7,15},{8,0},{9,1},... | collective-permute-start | bytes 1572872 | tf_op jit(solution)/shard_map/ppermute | solution.py:924
  64.1 21.3 %all-to-all-start.2 = ((bf16[8,4,64,128]{3,2,1,0:T(8,128)(2,1)}), bf16[8,4,64,128]{3,2,1,0:T(8,128)(2,1)S(1)}, u32[]{:S(2)}, u32[]{:S(2)}) async-start(bf16[8,4,64,128]{3,2,1,0:T(8,128)(2,1)} %add_convert_fusion), calls=%async_computation.2 | async-start | bytes 1048576 | tf_op jit(solution)/shard_map/all_to_all | solution.py:927
  85.4 21.4 %collective-permute-start.4 = (bf16[16,32,1536]{2,1,0:T(8,128)(2,1)}, bf16[16,32,1536]{2,1,0:T(8,128)(2,1)S(1)}, u32[]{:S(2)}, u32[]{:S(2)}) collective-permute-start(bf16[16,32,1536]{2,1,0:T(8,128)(2,1)} %get-tuple-element.152), channel_id=1, source_target_pairs={{0,16},{1,17},{2,18},{3,19},{4,20},{5,21},{6,22},{7,23},{8,9},{9,8... | collective-permute-start | bytes 4718600 | tf_op jit(solution)/shard_map/ppermute | solution.py:924
  86.9 19.8 %collective-permute-start.5 = (bf16[16,16,1536]{2,1,0:T(8,128)(2,1)}, bf16[16,16,1536]{2,1,0:T(8,128)(2,1)S(1)}, u32[]{:S(2)}, u32[]{:S(2)}) collective-permute-start(bf16[16,16,1536]{2,1,0:T(8,128)(2,1)} %get-tuple-element.153), channel_id=1, source_target_pairs={{0,2},{1,3},{2,0},{3,1},{4,6},{5,7},{6,4},{7,5},{8,10},{9,11},{10,... | collective-permute-start | bytes 2359304 | tf_op jit(solution)/shard_map/ppermute | solution.py:924
  106.8 22.4 %collective-permute-start.6 = (bf16[8,96,1024]{2,1,0:T(8,128)(2,1)}, bf16[8,96,1024]{2,1,0:T(8,128)(2,1)S(1)}, u32[]{:S(2)}, u32[]{:S(2)}) collective-permute-start(bf16[8,96,1024]{2,1,0:T(8,128)(2,1)} %get-tuple-element.173), channel_id=1, source_target_pairs={{0,16},{1,17},{2,18},{3,19},{4,20},{5,21},{6,22},{7,23},{8,9},{9,8... | collective-permute-start | bytes 4718600 | tf_op jit(solution)/shard_map/ppermute | solution.py:924
  109.5 19.6 %collective-permute-start.7 = (bf16[8,16,1536]{2,1,0:T(8,128)(2,1)}, bf16[8,16,1536]{2,1,0:T(8,128)(2,1)}, u32[]{:S(2)}, u32[]{:S(2)}) collective-permute-start(bf16[8,16,1536]{2,1,0:T(8,128)(2,1)} %get-tuple-element.176), channel_id=1, source_target_pairs={{0,4},{1,5},{2,6},{3,7},{4,0},{5,1},{6,2},{7,3},{8,12},{9,13},{10,... | collective-permute-start | bytes 1179656 | tf_op jit(solution)/shard_map/ppermute | solution.py:924
  124.9 21.8 %all-to-all-start.3 = ((bf16[8,4,64,128]{3,2,1,0:T(8,128)(2,1)}), bf16[8,4,64,128]{3,2,1,0:T(8,128)(2,1)}, u32[]{:S(2)}, u32[]{:S(2)}) async-start(bf16[8,4,64,128]{3,2,1,0:T(8,128)(2,1)} %bitcast.110), calls=%async_computation.3 | async-start | bytes 1048576 | tf_op jit(solution)/shard_map/all_to_all | solution.py:927
  129.1 17.6 %collective-permute-start.8 = (bf16[8,32,1536]{2,1,0:T(8,128)(2,1)}, bf16[8,32,1536]{2,1,0:T(8,128)(2,1)}, u32[]{:S(2)}, u32[]{:S(2)}) collective-permute-start(bf16[8,32,1536]{2,1,0:T(8,128)(2,1)} %copy-done.22), channel_id=1, source_target_pairs={{0,1},{1,0},{2,3},{3,2},{4,5},{5,4},{6,7},{7,6},{8,24},{9,25},{10,... | collective-permute-start | bytes 2359304 | tf_op jit(solution)/shard_map/ppermute | solution.py:924
  132.0 14.7 %collective-permute-start.9 = (f32[2,2,64,128]{3,2,1,0:T(8,128)S(1)}, f32[2,2,64,128]{3,2,1,0:T(8,128)}, u32[]{:S(2)}, u32[]{:S(2)}) collective-permute-start(f32[2,2,64,128]{3,2,1,0:T(8,128)S(1)} %dynamic-slice_bitcast_fusion), channel_id=1, source_target_pairs={{0,8},{1,9},{2,10},{3,11},{4,12},{5,13},{6,14},{7,15},{8,0},{9,1},... | collective-permute-start | bytes 393224 | tf_op jit(solution)/shard_map/ppermute | solution.py:924
  146.7 18.5 %collective-permute-start.14 = (bf16[2,512,1024]{2,1,0:T(8,128)(2,1)}, bf16[2,512,1024]{2,1,0:T(8,128)(2,1)}, u32[]{:S(2)}, u32[]{:S(2)}) collective-permute-start(bf16[2,512,1024]{2,1,0:T(8,128)(2,1)} %get-tuple-element.199), channel_id=1, source_target_pairs={{0,8},{1,9},{2,10},{3,11},{4,12},{5,13},{6,14},{7,15},{8,0},{9,1},... | collective-permute-start | bytes 6291464 | tf_op jit(solution)/shard_map/ppermute | solution.py:924
  147.3 18.0 %collective-permute-start.10 = (bf16[4,96,1024]{2,1,0:T(8,128)(2,1)}, bf16[4,96,1024]{2,1,0:T(8,128)(2,1)S(1)}, u32[]{:S(2)}, u32[]{:S(2)}) collective-permute-start(bf16[4,96,1024]{2,1,0:T(8,128)(2,1)} %copy-done.21), channel_id=1, source_target_pairs={{0,1},{1,0},{2,3},{3,2},{4,5},{5,4},{6,7},{7,6},{8,24},{9,25},{10,... | collective-permute-start | bytes 2359304 | tf_op jit(solution)/shard_map/ppermute | solution.py:924
  150.8 11.7 %collective-permute-start.11 = (bf16[4,32,1536]{2,1,0:T(8,128)(2,1)S(1)}, bf16[4,32,1536]{2,1,0:T(8,128)(2,1)S(1)}, u32[]{:S(2)}, u32[]{:S(2)}) collective-permute-start(bf16[4,32,1536]{2,1,0:T(8,128)(2,1)S(1)} %get-tuple-element.191), channel_id=1, source_target_pairs={{0,2},{1,3},{2,0},{3,1},{4,6},{5,7},{6,4},{7,5},{8,10},{9,11},{10,... | collective-permute-start | bytes 1179656 | tf_op jit(solution)/shard_map/ppermute | solution.py:924
  153.9 3.5 %collective-permute-start.12 = (bf16[4,4,64,128]{3,2,1,0:T(8,128)(2,1)S(1)}, bf16[4,4,64,128]{3,2,1,0:T(8,128)(2,1)S(1)}, u32[]{:S(2)}, u32[]{:S(2)}) collective-permute-start(bf16[4,4,64,128]{3,2,1,0:T(8,128)(2,1)S(1)} %multiply_convert_fusion.1), channel_id=1, source_target_pairs={{0,8},{1,9},{2,10},{3,11},{4,12},{5,13},{6,14},{7,15},{8,0},{9,1},... | collective-permute-start | bytes 786440 | tf_op jit(solution)/shard_map/ppermute | solution.py:924
  158.8 6.4 %collective-permute-start.13 = (bf16[8,16,1024]{2,1,0:T(8,128)(2,1)S(1)}, bf16[8,16,1024]{2,1,0:T(8,128)(2,1)S(1)}, u32[]{:S(2)}, u32[]{:S(2)}) collective-permute-start(bf16[8,16,1024]{2,1,0:T(8,128)(2,1)S(1)} %get-tuple-element.197), channel_id=1, source_target_pairs={{0,16},{1,17},{2,18},{3,19},{4,20},{5,21},{6,22},{7,23},{8,9},{9,8... | collective-permute-start | bytes 786440 | tf_op jit(solution)/shard_map/ppermute | solution.py:924
  165.5 14.8 %collective-permute-start.15 = (bf16[2,96,1024]{2,1,0:T(8,128)(2,1)S(1)}, bf16[2,96,1024]{2,1,0:T(8,128)(2,1)S(1)}, u32[]{:S(2)}, u32[]{:S(2)}) collective-permute-start(bf16[2,96,1024]{2,1,0:T(8,128)(2,1)S(1)} %get-tuple-element.210), channel_id=1, source_target_pairs={{0,2},{1,3},{2,0},{3,1},{4,6},{5,7},{6,4},{7,5},{8,10},{9,11},{10,... | collective-permute-start | bytes 1179656 | tf_op jit(solution)/shard_map/ppermute | solution.py:924
  166.1 13.6 %collective-permute-start.16 = (bf16[4,16,1536]{2,1,0:T(8,128)(2,1)S(1)}, bf16[4,16,1536]{2,1,0:T(8,128)(2,1)S(1)}, u32[]{:S(2)}, u32[]{:S(2)}) collective-permute-start(bf16[4,16,1536]{2,1,0:T(8,128)(2,1)S(1)} %get-tuple-element.211), channel_id=1, source_target_pairs={{0,16},{1,17},{2,18},{3,19},{4,20},{5,21},{6,22},{7,23},{8,9},{9,8... | collective-permute-start | bytes 589832 | tf_op jit(solution)/shard_map/ppermute | solution.py:924
  167.3 12.4 %collective-permute-start.17 = (bf16[2,32,1536]{2,1,0:T(8,128)(2,1)S(1)}, bf16[2,32,1536]{2,1,0:T(8,128)(2,1)S(1)}, u32[]{:S(2)}, u32[]{:S(2)}) collective-permute-start(bf16[2,32,1536]{2,1,0:T(8,128)(2,1)S(1)} %get-tuple-element.212), channel_id=1, source_target_pairs={{0,4},{1,5},{2,6},{3,7},{4,0},{5,1},{6,2},{7,3},{8,12},{9,13},{10,... | collective-permute-start | bytes 589832 | tf_op jit(solution)/shard_map/ppermute | solution.py:924
  169.9 9.8 %collective-permute-start.18 = (bf16[4,16,1024]{2,1,0:T(8,128)(2,1)S(1)}, bf16[4,16,1024]{2,1,0:T(8,128)(2,1)S(1)}, u32[]{:S(2)}, u32[]{:S(2)}) collective-permute-start(bf16[4,16,1024]{2,1,0:T(8,128)(2,1)S(1)} %get-tuple-element.215), channel_id=1, source_target_pairs={{0,1},{1,0},{2,3},{3,2},{4,5},{5,4},{6,7},{7,6},{8,24},{9,25},{10,... | collective-permute-start | bytes 393224 | tf_op jit(solution)/shard_map/ppermute | solution.py:924
  171.1 8.5 %collective-permute-start.19 = (f32[2,64,128]{2,1,0:T(8,128)S(1)}, f32[2,64,128]{2,1,0:T(8,128)S(1)}, u32[]{:S(2)}, u32[]{:S(2)}) collective-permute-start(f32[2,64,128]{2,1,0:T(8,128)S(1)} %dynamic-slice_bitcast_fusion.1), channel_id=1, source_target_pairs={{0,16},{1,17},{2,18},{3,19},{4,20},{5,21},{6,22},{7,23},{8,24},{9,... | collective-permute-start | bytes 196616 | tf_op jit(solution)/shard_map/ppermute | solution.py:924
  180.3 6.8 %collective-permute-start.25 = (f32[32,128]{1,0:T(8,128)S(1)}, f32[32,128]{1,0:T(8,128)S(1)}, u32[]{:S(2)}, u32[]{:S(2)}) collective-permute-start(f32[32,128]{1,0:T(8,128)S(1)} %get-tuple-element.229), channel_id=1, source_target_pairs={{0,17},{1,16},{2,19},{3,18},{4,21},{5,20},{6,23},{7,22},{8,25},{9,... | collective-permute-start | bytes 49160 | tf_op jit(solution)/shard_map/ppermute | solution.py:924
  182.0 6.7 %collective-permute-start.24 = (f32[32,128]{1,0:T(8,128)S(1)}, f32[32,128]{1,0:T(8,128)S(1)}, u32[]{:S(2)}, u32[]{:S(2)}) collective-permute-start(f32[32,128]{1,0:T(8,128)S(1)} %get-tuple-element.229), channel_id=1, source_target_pairs={{0,1},{1,0},{2,3},{3,2},{4,5},{5,4},{6,7},{7,6},{8,24},{9,25},{10,... | collective-permute-start | bytes 49160 | tf_op jit(solution)/shard_map/ppermute | solution.py:924
  182.7 6.0 %collective-permute-start.23 = (f32[32,128]{1,0:T(8,128)S(1)}, f32[32,128]{1,0:T(8,128)S(1)}, u32[]{:S(2)}, u32[]{:S(2)}) collective-permute-start(f32[32,128]{1,0:T(8,128)S(1)} %get-tuple-element.229), channel_id=1, source_target_pairs={{0,16},{1,17},{2,18},{3,19},{4,20},{5,21},{6,22},{7,23},{8,9},{9,8... | collective-permute-start | bytes 49160 | tf_op jit(solution)/shard_map/ppermute | solution.py:924
  183.9 10.1 %collective-permute-start.20 = (bf16[1,96,1024]{2,1,0:T(8,128)(2,1)S(1)}, bf16[1,96,1024]{2,1,0:T(8,128)(2,1)S(1)}, u32[]{:S(2)}, u32[]{:S(2)}) collective-permute-start(bf16[1,96,1024]{2,1,0:T(8,128)(2,1)S(1)} %get-tuple-element.224), channel_id=1, source_target_pairs={{0,4},{1,5},{2,6},{3,7},{4,0},{5,1},{6,2},{7,3},{8,12},{9,13},{10,... | collective-permute-start | bytes 589832 | tf_op jit(solution)/shard_map/ppermute | solution.py:924
  185.3 7.3 %collective-permute-start.21 = (bf16[2,16,1536]{2,1,0:T(8,128)(2,1)S(1)}, bf16[2,16,1536]{2,1,0:T(8,128)(2,1)S(1)}, u32[]{:S(2)}, u32[]{:S(2)}) collective-permute-start(bf16[2,16,1536]{2,1,0:T(8,128)(2,1)S(1)} %get-tuple-element.225), channel_id=1, source_target_pairs={{0,1},{1,0},{2,3},{3,2},{4,5},{5,4},{6,7},{7,6},{8,24},{9,25},{10,... | collective-permute-start | bytes 294920 | tf_op jit(solution)/shard_map/ppermute | solution.py:924
  187.1 5.4 %collective-permute-start.22 = (bf16[2,16,1024]{2,1,0:T(8,128)(2,1)S(1)}, bf16[2,16,1024]{2,1,0:T(8,128)(2,1)S(1)}, u32[]{:S(2)}, u32[]{:S(2)}) collective-permute-start(bf16[2,16,1024]{2,1,0:T(8,128)(2,1)S(1)} %get-tuple-element.228), channel_id=1, source_target_pairs={{0,2},{1,3},{2,0},{3,1},{4,6},{5,7},{6,4},{7,5},{8,10},{9,11},{10,... | collective-permute-start | bytes 196616 | tf_op jit(solution)/shard_map/ppermute | solution.py:924
  188.7 3.8 %collective-permute-start.26 = (f32[32,128]{1,0:T(8,128)S(1)}, f32[32,128]{1,0:T(8,128)S(1)}, u32[]{:S(2)}, u32[]{:S(2)}) collective-permute-start(f32[32,128]{1,0:T(8,128)S(1)} %add_add_fusion), channel_id=1, source_target_pairs={{0,2},{1,3},{2,0},{3,1},{4,6},{5,7},{6,4},{7,5},{8,10},{9,11},{10,... | collective-permute-start | bytes 49160 | tf_op jit(solution)/shard_map/ppermute | solution.py:924
  194.0 5.6 %collective-permute-start.27 = (bf16[1,16,1024]{2,1,0:T(8,128)(2,1)S(1)}, bf16[1,16,1024]{2,1,0:T(8,128)(2,1)S(1)}, u32[]{:S(2)}, u32[]{:S(2)}) collective-permute-start(bf16[1,16,1024]{2,1,0:T(8,128)(2,1)S(1)} %get-tuple-element.236), channel_id=1, source_target_pairs={{0,4},{1,5},{2,6},{3,7},{4,0},{5,1},{6,2},{7,3},{8,12},{9,13},{10,... | collective-permute-start | bytes 98312 | tf_op jit(solution)/shard_map/ppermute | solution.py:924
  195.0 4.6 %collective-permute-start.28 = (f32[32,128]{1,0:T(8,128)S(1)}, f32[32,128]{1,0:T(8,128)S(1)}, u32[]{:S(2)}, u32[]{:S(2)}) collective-permute-start(f32[32,128]{1,0:T(8,128)S(1)} %add.101), channel_id=1, source_target_pairs={{0,4},{1,5},{2,6},{3,7},{4,0},{5,1},{6,2},{7,3},{8,12},{9,13},{10,... | collective-permute-start | bytes 49160 | tf_op jit(solution)/shard_map/ppermute | solution.py:924
  (41 other events, 629.1 us)

commit v3 on v2

--- a/solution.py
+++ b/solution.py
@@ -1,3 +1,5 @@
+import functools
+
 import jax
 import jax.numpy as jnp
 from jax import lax
@@ -87,7 +89,7 @@
     return ref[pl.ds(c, rows, stride=GROUP), :]
 
 
-def fwd_kernel(groups, keep, x, rate, coef, ins, insj, head, tailj, y, hs, toe, pt, ss, near, xs, kr):
+def fwd_kernel(sm, x, rate, coef, ins, insj, head, tailj, y, hs, toe, pt, ss, near, xs, kr):
     rows = ins.shape[0]
     n = rate.shape[1]
     flip = flip_matrix()
@@ -129,9 +131,9 @@
             hs[sub, :, w, :] = h
             s = ss[:, w, :]
             ss[:, w, :] = h * ce
-            h = h * (fade * keep[b]) + s
-
-        @pl.loop(1, groups[0])
+            h = h * (fade * sm[0, b].astype(f32)) + s
+
+        @pl.loop(1, sm[1, 0])
         def _(g):
             m = seg_masks(ins[...], g)
             for c in range(SUB):
@@ -145,7 +147,7 @@
 
 
 def bwd_kernel(
-    groups, keep, x, dy, rate, coef, ins, insj, head, tailj, hs, toe, *rest
+    sm, x, dy, rate, coef, ins, insj, head, tailj, hs, toe, *rest
 ):
     dv, rates, pt, s1, e0, e1, near, gacc, nr, xs, ys = rest[-11:]
     rows = ins.shape[0]
@@ -182,7 +184,7 @@
             near[c] = fold(mm(rep(dja[sl]) * mjb, toe[lo + c]), mj, rows)
             gacc[c : c + 1, :] = lags(da[sl], xja[sl], mn, mjb)
 
-        @pl.loop(1, groups[0])
+        @pl.loop(1, sm[1, 0])
         def _(g):
             m = seg_masks(ins[...], g).astype(bf16)
             k = seg_masks(insj[...], g)
@@ -221,7 +223,7 @@
             w = slice(b * SUB, (b + 1) * SUB)
             h = hs[sub, :, w, :]
             e = e0[:, w, :]
-            kf = fade * keep[b]
+            kf = fade * sm[0, b].astype(f32)
             ar = ar + dh * (kf * (float(T) * h) + s1[:, w, :])
             ae = ae + h * e1[:, w, :]
             ac = ac + h * e
@@ -244,22 +246,39 @@
     dv[...] = xs[...].reshape(rows, GROUP, T).astype(bf16)
 
 
+def mask_kernel(st, sm, ins, insj, head, tailj, *, blocks):
+    rows = st.shape[0]
+    s = st[...]
+    tri = (iota((T, T), 0) <= iota((T, T), 1)).astype(f32).astype(bf16)
+    first = s[:, 0:1]
+    seg = mm(s.astype(f32).astype(bf16), tri) - first.astype(f32)
+    last = seg[:, T - 1 : T]
+    cont = (first == 0) & (iota((rows, 1), 0) % blocks != 0)
+    back = mm(seg.astype(bf16), flip_matrix())
+    ins[...] = seg.astype(jnp.int32)
+    insj[...] = back.astype(jnp.int32)
+    head[...] = jnp.where((seg == 0) & cont, 1.0, 0.0)
+    tailj[...] = jnp.where(back == last, 1.0, 0.0).astype(bf16)
+    keep = jnp.where(cont & (last == 0), 1, 0)
+    place = iota((rows, T), 0) == iota((rows, T), 1)
+    keep = jnp.sum(jnp.where(place, keep, 0), axis=0, keepdims=True)
+    most = jnp.max(jnp.broadcast_to(last.astype(jnp.int32), (rows, T)), axis=0, keepdims=True)
+    row = iota((8, T), 0)
+    sm[...] = jnp.where(row == 0, keep, jnp.where(row == 1, most // SEG + 1, 0))
+
+
 def ssm_masks(starts):
     seqs, length = starts.shape
     blocks = length // T
     rows = seqs * blocks
-    st = starts.reshape(rows, T)
-    tri = (iota((T, T), 0) <= iota((T, T), 1)).astype(bf16)
-    ins = mm(st.astype(bf16), tri).astype(jnp.int32) - st[:, :1]
-    cont = (st[:, :1] == 0) & (iota((rows, 1), 0) % blocks != 0)
-    last = ins[:, -1:]
-    head = ((ins == 0) & cont).astype(f32)
-    back = (iota((T, T), 0) + iota((T, T), 1) == T - 1).astype(bf16)
-    insj = mm(ins.astype(bf16), back).astype(jnp.int32)
-    tailj = (insj == last).astype(bf16)
-    keep = (cont & (last == 0)).astype(f32)[:, 0]
-    groups = (jnp.max(last) // SEG + 1).reshape(1).astype(jnp.int32)
-    return groups, keep, ins, insj, head, tailj
+    shape = (rows, T)
+    kinds = (jnp.int32, jnp.int32, f32, bf16)
+    return pl.pallas_call(
+        functools.partial(mask_kernel, blocks=blocks),
+        out_shape=[jax.ShapeDtypeStruct((8, T), jnp.int32)]
+        + [jax.ShapeDtypeStruct(shape, kind) for kind in kinds],
+        name="masks",
+    )(starts.reshape(shape))
 
 
 def ssm_specs(rows, n, first=0):
@@ -286,7 +305,7 @@
     return pl.pallas_call(
         fwd_kernel,
         grid=(chans // GROUP,),
-        in_specs=[s["sm"], s["sm"], s["ch"], s["par"], s["par"]] + [s["full"]] * 4,
+        in_specs=[s["sm"], s["ch"], s["par"], s["par"]] + [s["full"]] * 4,
         out_specs=[s["ch"], s["hs"], s["toe"]],
         out_shape=[
             pltpu.HBM(x.shape, bf16),
@@ -297,7 +316,7 @@
         compiler_params=pltpu.CompilerParams(vmem_limit_bytes=16 * 2**20),
         cost_estimate=s["cost"],
         name="ssm_fwd",
-    )(masks[0], masks[1], x, rate, coef, *masks[2:])
+    )(masks[0], x, rate, coef, *masks[1:])
 
 
 def ssm_bwd(x, dy, rate, coef, masks, hs, toe, row_n, part=0, parts=1, held=()):
@@ -309,7 +328,7 @@
     return pl.pallas_call(
         bwd_kernel,
         grid=(steps,),
-        in_specs=[s["sm"], s["sm"], s["ch"], s["ch"], s["par"], s["par"]]
+        in_specs=[s["sm"], s["ch"], s["ch"], s["par"], s["par"]]
         + [s["full"]] * 4
         + [s["hs"], s["toe"]]
         + [raw] * len(held),
@@ -334,9 +353,9 @@
         ],
         compiler_params=pltpu.CompilerParams(vmem_limit_bytes=16 * 2**20),
         cost_estimate=s["cost"],
-        input_output_aliases={12 + i: i for i in range(len(held))},
+        input_output_aliases={11 + i: i for i in range(len(held))},
         name="ssm_bwd",
-    )(masks[0], masks[1], x, dy, rate, coef, *masks[2:], *from_hbm(hs, toe), *held)
+    )(masks[0], x, dy, rate, coef, *masks[1:], *from_hbm(hs, toe), *held)
 
 
 epsilon = 1e-05
@@ -416,7 +435,7 @@
         (quads,),
         [rows, whole((1, width)), whole((1, width)), whole(w_val.shape)],
         [rows, block, block],
-        [struct((own, width), bf16), struct(spread, bf16), struct(spread, f32)],
+        [struct((own, width), bf16), struct(spread, bf16), in_hbm(spread, f32)],
         from_hbm(tokens, gain[None], bias[None], w_val),
     )
 
@@ -819,9 +838,10 @@
     )
 
 
-def finish_kernel(s, u_keep, u_got, m_keep, m_got, d_keep, d_got, v_keep, v_got, norm, down, mine, other):
+def finish_kernel(s, u_keep, u_got, m_keep, m_got, d_keep, d_got, v_keep, *rest):
+    *v_gots, norm, down, mine, other = rest
     down[...] = d_keep[0].astype(f32) + d_got[0].astype(f32)
-    v = v_keep[0].astype(f32) + v_got[0].astype(f32)
+    v = sum([g[0].astype(f32) for g in v_gots], v_keep[0].astype(f32))
     half = v.shape[1]
     um, mx = u_keep.shape[1], m_keep.shape[1]
     tail = um + mx + 8
@@ -898,7 +918,9 @@
         core = row % 2
         me = row * chan_n + chan
         there = (row ^ 1) * chan_n + chan
-        scal = jnp.stack([core, row // 2, chan % 2, (chan // 2) % 2, chan // 4, me, there])
+        y_bit = chan % 2
+        b_bit = jnp.where(core == 0, y_bit, row // 2)
+        scal = jnp.stack([core, row // 2, y_bit, (chan // 2) % 2, chan // 4, me, there, b_bit])
         scal = scal.astype(jnp.int32)
         bit_x, bit_y = scal[1], scal[2]
         bit_a = jnp.where(core == 0, bit_x, bit_y).reshape(1)
@@ -992,39 +1014,43 @@
         d_vpre = (d_v.astype(f32) * v_slope).astype(bf16)
         v_give, v_keep = val_call(scal, d_vpre, v_got, normed_t)
         v_got = send(v_give, "a")
-        m_give, m_keep = step_call(bit_a, m_keep, m_got)
-        rates = lax.dynamic_index_in_dim(rates, core, 0, keepdims=False) + rates_got
-        rates_give = lax.dynamic_index_in_dim(rates, 1 - bit_x, 0, keepdims=False)
-        d_got, u_got, m_give, v_got, rates_give, d_vpre, bd_got = after(
-            (d_got, u_got, m_give, v_got, rates_give, d_vpre, bd_got)
-        )
-
-        rates_got = send(rates_give, "x")
+        v_give, d_vpre = after((v_give, d_vpre))
+        block_out, tokens_grad, norm_part = tail_call(
+            tokens, out_grad, layer_norm_gain, block_own, bd_got, dn_own, d_vpre, w_val,
+            row_n * chan_n,
+        )
+        d_got, u_got, m_got, v_got, norm_part = after((d_got, u_got, m_got, v_got, norm_part))
+
         d_give, d_keep = step_call(bit_low, d_keep, d_got)
         d_got = send(d_give, "low")
         u_give, u_keep = step_call(bit_high, u_keep, u_got)
+        u_give, norm_part = after((u_give, norm_part))
         u_got = send(u_give, "high")
+        m_give, m_keep = step_call(bit_a, m_keep, m_got)
         m_got = send(m_give, "a")
+        rates = lax.dynamic_index_in_dim(rates, core, 0, keepdims=False) + rates_got
+        rates_give = lax.dynamic_index_in_dim(rates, 1 - bit_x, 0, keepdims=False)
         v_give, v_keep = step_call(bit_b, v_keep, v_got)
         v_got = send(v_give, "b")
-        block_out, tokens_grad, norm_part = tail_call(
-            tokens, out_grad, layer_norm_gain, block_own, bd_got, dn_own, d_vpre, w_val,
-            row_n * chan_n,
-        )
-        d_got, m_got, u_got, v_got, norm_part, rates_got = after(
-            (d_got, m_got, u_got, v_got, norm_part, rates_got)
-        )
-        rates = lax.dynamic_index_in_dim(rates, bit_x, 0, keepdims=False) + rates_got
+        norm_part = norm_part + send(norm_part, "a")
+        norm_part = norm_part + send(norm_part, "b")
+        d_got, m_got, u_got, v_got, norm_part, rates_give = after(
+            (d_got, m_got, u_got, v_got, norm_part, rates_give)
+        )
 
         d_give, d_keep = step_call(bit_high, d_keep, d_got)
+        d_give, norm_part, rates_give = after((d_give, norm_part, rates_give))
         d_got = send(d_give, "high")
+        rates_got = send(rates_give, "x")
         m_give, m_keep = step_call(bit_b, m_keep, m_got)
         m_got = send(m_give, "b")
         v_give, v_keep = step_call(bit_low, v_keep, v_got)
         v_got = send(v_give, "low")
-        norm_part = norm_part + send(norm_part, "a") + send(norm_part, "b") + send(norm_part, "ab")
         norm_part = norm_part + send(norm_part, "low")
-        d_got, m_got, v_got, norm_part = after((d_got, m_got, v_got, norm_part))
+        d_got, m_got, norm_part, v_got, rates_got = after(
+            (d_got, m_got, norm_part, v_got, rates_got)
+        )
+        rates = lax.dynamic_index_in_dim(rates, bit_x, 0, keepdims=False) + rates_got
 
         v_give, v_keep = step_call(bit_high, v_keep, v_got)
         v_got = send(v_give, "high")

time: 206 us -> 202 us (0.981)
  starting transfers between devices: 55.5 us -> 50.8 us
  waiting for transfers between devices: 15.6 us -> 18.7 us
  Pallas kernels: 110 us -> 113 us
  between operations: 3.97 us -> 1.18 us
    ppermute x30 -> x29, starting transfers between devices: 32.1 us -> 29.3 us  [send(): return lax.ppermute(value, ('row', 'chan'), pairs)]
    pallas_call x2 -> x3, Pallas kernels: 20.9 us -> 22.6 us  [the longest x2 20.9 us: ssm_bwd(): pl.pallas_call(bwd_kernel, grid=(steps,), in_specs=[s['sm'], s['ch'], s['...]
    ppermute x30 -> x29, waiting for transfers between devices: 15.6 us -> 16.7 us  [send(): return lax.ppermute(value, ('row', 'chan'), pairs)]
    unnamed x78 -> x70, local copies, waits for them, and re-layouts: 6.98 us -> 6.08 us
  transfers between devices with their start and end apart: 34 -> 33, of which waited for: 8 -> 9; matrix products, arithmetic and copies ran while one was open for 6% -> 5% of each run, Pallas kernels for 44% -> 45%
where the time goes in v3:
time: 202 us; the launch traced here: 201 us
  Pallas kernels  113 us (56%)
  starting transfers between devices  50.8 us (25%)
  waiting for transfers between devices  18.7 us (9%)
  local copies, waits for them, and re-layouts  8.29 us (4%)
  other arithmetic  5.64 us (3%)
  matrix products  3.74 us (2%)
    pallas_call x22, Pallas kernels, call(): pl.pallas_call(kernel, grid_spec=pltpu.PrefetchScalarGridSpec(num_scalar_...  77.7 us
    ppermute x29, starting transfers between devices, send(): return lax.ppermute(value, ('row', 'chan'), pairs)  29.3 us
    all_to_all x4, starting transfers between devices, on_device(): lax.all_to_all(v, 'chan', split_axis=0, concat_axis=0, tiled=True)  21.5 us
    pallas_call x2, Pallas kernels, ssm_bwd(): pl.pallas_call(bwd_kernel, grid=(steps,), in_specs=[s['sm'], s['ch'], s['...  20.9 us
    ppermute x29, waiting for transfers between devices, send(): return lax.ppermute(value, ('row', 'chan'), pairs)  16.7 us
    pallas_call x1, Pallas kernels, ssm_fwd(): pl.pallas_call(fwd_kernel, grid=(chans // GROUP,), in_specs=[s['sm'], s['...  12.3 us
    unnamed x70, local copies, waits for them, and re-layouts  6.08 us
  transfers between devices with their start and end apart: 33, of which 9 were waited for; matrix products, arithmetic and copies ran while one was open for 5% of the time, Pallas kernels for 45%

profile of v3, /device:TPU:0, one launch (start us, length us, event | category | flops | bytes accessed | tf_op | source)
XLA Modules:
  0.0 200.8 jit_solution(13241052888032798913)
XLA Ops:
  0.7 5.4 %norm_val.1 = (bf16[512,1024]{1,0:T(8,128)(2,1)S(1)}, bf16[8,4,64,128]{3,2,1,0:T(8,128)(2,1)}, f32[8,4,64,128]{3,2,1,0:T(8,128)}) custom-call(bf16[512,1024]{1,0:T(8,128)(2,1)} %tok.3, f32[1,1024]{1,0:T(1,128)} %bitcast.109, f32[1,1024]{1,0:T(1,128)} %bitcast.112, bf16[1024,512]{1,0:T(8,128)(2,1)} %w_val.3), custom_call_target="tpu_custom_call" | custom-call | tf_op jit(solution)/shard_map/norm_val/pallas_call | solution.py:392
  6.6 7.3 %all-to-all-start = ((bf16[8,4,64,128]{3,2,1,0:T(8,128)(2,1)}), bf16[8,4,64,128]{3,2,1,0:T(8,128)(2,1)S(1)}, u32[]{:S(2)}, u32[]{:S(2)}) async-start(bf16[8,4,64,128]{3,2,1,0:T(8,128)(2,1)} %get-tuple-element.139), calls=%async_computation | async-start | bytes 1048576 | tf_op jit(solution)/shard_map/all_to_all | solution.py:949
  15.6 11.0 %gate_first.1 = (bf16[1024,1536]{1,0:T(8,128)(2,1)}, bf16[1024,1536]{1,0:T(8,128)(2,1)}, bf16[1024,1536]{1,0:T(8,128)(2,1)}, bf16[1024,1024]{1,0:T(8,128)(2,1)},...) custom-call(s32[8]{0:T(128)S(1)} %stack.35.core.s, bf16[512,1024]{1,0:T(8,128)(2,1)} %copy-done.8, ...), custom_call_target="tpu_custom_call" | custom-call | tf_op jit(solution)/shard_map/gate_first/pallas_call | solution.py:392
  26.6 1.9 all-to-all-done
  28.6 12.3 %ssm_fwd.1 = (bf16[32,64,128]{2,1,0:T(8,128)(2,1)}, f32[8,4,256,128]{3,2,1,0:T(8,128)}, bf16[64,128,128]{2,1,0:T(8,128)(2,1)}) custom-call(s32[8,128]{1,0:T(8,128)S(1)} %copy-done.28, bf16[32,64,128]{2,1,0:T(8,128)(2,1)S(1)} %bitcast.98, f32[64,512]{1,0:T(8,128)S(1)} %copy-done.17, f32[64,512]{1,0:T(8,128)S(1)} %copy-done.19, s32[32,128]{1,0:T(8,128)S(1)} %copy-done.21, ...), custom_call_target="tpu_custom_call" | custom-call | flops 20000000000 | bytes 10000000 | tf_op jit(solution)/shard_map/ssm_fwd/pallas_call | solution.py:305
  41.0 4.1 %all-to-all-start.1 = ((bf16[8,4,64,128]{3,2,1,0:T(8,128)(2,1)}), bf16[8,4,64,128]{3,2,1,0:T(8,128)(2,1)S(1)}, u32[]{:S(2)}, u32[]{:S(2)}) async-start(bf16[8,4,64,128]{3,2,1,0:T(8,128)(2,1)} %bitcast.108), calls=%async_computation.1 | async-start | bytes 1048576 | tf_op jit(solution)/shard_map/all_to_all | solution.py:949
  45.1 11.5 %gate_last.1 = (bf16[1024,1536]{1,0:T(8,128)(2,1)}, bf16[1024,1536]{1,0:T(8,128)(2,1)}, bf16[1024,1536]{1,0:T(8,128)(2,1)}, bf16[1024,1024]{1,0:T(8,128)(2,1)}, ...) custom-call(s32[8]{0:T(128)S(1)} %stack.35.core.s, ...), custom_call_target="tpu_custom_call", output_to_operand_aliasing={{0}: (7, {}), {1}: (8, {}), {2}: (9, {})} | custom-call | tf_op jit(solution)/shard_map/gate_last/pallas_call | solution.py:392
  56.6 2.1 %collective-permute-done.2 = bf16[8,4,64,128]{3,2,1,0:T(8,128)(2,1)S(1)} collective-permute-done((bf16[8,4,64,128]{3,2,1,0:T(8,128)(2,1)}, bf16[8,4,64,128]{3,2,1,0:T(8,128)(2,1)S(1)}, u32[]{:S(2)}, u32[]{:S(2)}) %collective-permute-start.2) | collective-permute-done | bytes 524320 | tf_op jit(solution)/shard_map/ppermute | solution.py:946
  58.7 2.2 %add_convert_fusion = bf16[8,4,64,128]{3,2,1,0:T(8,128)(2,1)} fusion(f32[8,4,64,128]{3,2,1,0:T(8,128)} %get-tuple-element.156, bf16[8,4,64,128]{3,2,1,0:T(8,128)(2,1)S(1)} %collective-permute-done.2), kind=kLoop, calls=%fused_computation.2 | loop fusion | flops 786432 | bytes 2097152 | tf_op jit(solution)/shard_map/convert_element_type | solution.py:969
  61.1 6.0 %all-to-all-start.2 = ((bf16[8,4,64,128]{3,2,1,0:T(8,128)(2,1)}), bf16[8,4,64,128]{3,2,1,0:T(8,128)(2,1)S(1)}, u32[]{:S(2)}, u32[]{:S(2)}) async-start(bf16[8,4,64,128]{3,2,1,0:T(8,128)(2,1)} %add_convert_fusion), calls=%async_computation.2 | async-start | bytes 1048576 | tf_op jit(solution)/shard_map/all_to_all | solution.py:949
  67.9 14.6 %mix_up.1 = (bf16[1024,1536]{1,0:T(8,128)(2,1)}, bf16[1024,1536]{1,0:T(8,128)(2,1)}, bf16[16,32,1536]{2,1,0:T(8,128)(2,1)}, bf16[16,32,1536]{2,1,0:T(8,128)(2,1)...) custom-call(s32[8]{0:T(128)S(1)} %stack.35.core.s, bf16[8,4,64,128]{3,2,1,0:T(8,128)(2,1)} %copy-done.33, ...), custom_call_target="tpu_custom_call" | custom-call | flops 10000000000 | bytes 10000000 | tf_op jit(solution)/shard_map/mix_up/pallas_call | solution.py:392
  84.1 2.0 %collective-permute-start.5 = (bf16[16,16,1536]{2,1,0:T(8,128)(2,1)}, bf16[16,16,1536]{2,1,0:T(8,128)(2,1)S(1)}, u32[]{:S(2)}, u32[]{:S(2)}) collective-permute-start(bf16[16,16,1536]{2,1,0:T(8,128)(2,1)} %get-tuple-element.168), channel_id=1, source_target_pairs={{0,2},{1,3},{2,0},{3,1},{4,6},{5,7},{6,4},{7,5},{8,10},{9,11},{10,... | collective-permute-start | bytes 2359304 | tf_op jit(solution)/shard_map/ppermute | solution.py:946
  86.2 10.4 %ssm_bwd.2 = (bf16[32,64,128]{2,1,0:T(8,128)(2,1)}, f32[2,2,2,64,128]{4,3,2,1,0:T(8,128)S(1)}) custom-call(s32[8,128]{1,0:T(8,128)S(1)} %copy-done.28, bf16[32,64,128]{2,1,0:T(8,128)(2,1)S(1)} %bitcast.99, bf16[32,64,128]{2,1,0:T(8,128)(2,1)S(1)} %bitcast.101, f32[64,512]{1,0:T(8,128)S(1)} %copy-done.17, f32[64,512]{1,0:T(8,128)S(1)} %copy-done.19, ...), custom_call_target="tpu_custom_call" | custom-call | flops 20000000000 | bytes 10000000 | tf_op jit(solution)/shard_map/ssm_bwd/pallas_call | solution.py:328
  96.6 3.7 %convolution_convert_fusion.down_g.down_k = bf16[1536,1024]{1,0:T(8,128)(2,1)S(1)} fusion(bf16[1024,1536]{1,0:T(8,128)(2,1)S(1)} %copy-done.30, bf16[1024,1024]{1,0:T(8,128)(2,1)S(1)} %copy-done.32), kind=kOutput, calls=%fused_computation | convolution fusion | flops 3222798336 | bytes 8388608 | tf_op jit(solution)/shard_map/dot_general | solution.py:22
  100.4 3.5 %split.1 = (bf16[8,96,1024]{2,1,0:T(8,128)(2,1)}, bf16[8,96,1024]{2,1,0:T(8,128)(2,1)S(1)}) custom-call(s32[8]{0:T(128)S(1)} %stack.35.core.s, bf16[1536,1024]{1,0:T(8,128)(2,1)S(1)} %convolution_convert_fusion.down_g.down_k, bf16[1536,1024]{1,0:T(8,128)(2,1)S(1)} %convolution_convert_fusion.down_g.down_k), custom_call_target="tpu_custom_call" | custom-call | tf_op jit(solution)/shard_map/split/pallas_call | solution.py:392
  106.6 2.5 %collective-permute-start.7 = (bf16[8,16,1536]{2,1,0:T(8,128)(2,1)}, bf16[8,16,1536]{2,1,0:T(8,128)(2,1)}, u32[]{:S(2)}, u32[]{:S(2)}) collective-permute-start(bf16[8,16,1536]{2,1,0:T(8,128)(2,1)} %get-tuple-element.191), channel_id=1, source_target_pairs={{0,4},{1,5},{2,6},{3,7},{4,0},{5,1},{6,2},{7,3},{8,12},{9,13},{10,... | collective-permute-start | bytes 1179656 | tf_op jit(solution)/shard_map/ppermute | solution.py:946
  109.1 10.5 %ssm_bwd.3 = (bf16[32,64,128]{2,1,0:T(8,128)(2,1)}, f32[2,2,2,64,128]{4,3,2,1,0:T(8,128)S(1)}) custom-call(s32[8,128]{1,0:T(8,128)S(1)} %copy-done.28, bf16[32,64,128]{2,1,0:T(8,128)(2,1)S(1)} %bitcast.100, bf16[32,64,128]{2,1,0:T(8,128)(2,1)S(1)} %bitcast.102, f32[64,512]{1,0:T(8,128)S(1)} %copy-done.18, ...), custom_call_target="tpu_custom_call", output_to_operand_aliasing={{0}: (11, {}), {1}: (12, {})} | custom-call | flops 20000000000 | bytes 10000000 | tf_op jit(solution)/shard_map/ssm_bwd/pallas_call | solution.py:328
  122.2 4.1 %all-to-all-start.3 = ((bf16[8,4,64,128]{3,2,1,0:T(8,128)(2,1)}), bf16[8,4,64,128]{3,2,1,0:T(8,128)(2,1)}, u32[]{:S(2)}, u32[]{:S(2)}) async-start(bf16[8,4,64,128]{3,2,1,0:T(8,128)(2,1)} %bitcast.107), calls=%async_computation.3 | async-start | bytes 1048576 | tf_op jit(solution)/shard_map/all_to_all | solution.py:949
  126.4 1.9 collective-permute-start.8
  129.3 12.4 %block.1 = (f32[512,1024]{1,0:T(8,128)}, f32[512,1024]{1,0:T(8,128)}, bf16[2,512,1024]{2,1,0:T(8,128)(2,1)}) custom-call(s32[8]{0:T(128)S(1)} %stack.35.core.s, bf16[1024,1536]{1,0:T(8,128)(2,1)} %get-tuple-element.185.gate, bf16[1024,1536]{1,0:T(8,128)(2,1)} %get-tuple-element.186.d_upre, bf16[3072,1024]{1,0:T(8,128)(2,1)} %refs_1_.1, ...), custom_call_target="tpu_custom_call" | custom-call | tf_op jit(solution)/shard_map/block/pallas_call | solution.py:392
  145.9 2.2 %halve.15 = (bf16[4,32,1536]{2,1,0:T(8,128)(2,1)S(1)}, bf16[4,32,1536]{2,1,0:T(8,128)(2,1)S(1)}) custom-call(s32[1]{0:T(128)} %bitcast.4.bit, bf16[2,4,32,1536]{3,2,1,0:T(8,128)(2,1)S(1)} %bitcast.68, bf16[2,4,32,1536]{3,2,1,0:T(8,128)(2,1)} %bitcast.23.got_g.got_k, bf16[2,4,32,1536]{3,2,1,0:T(8,128)(2,1)S(1)} %bitcast.69, ...), custom_call_target="tpu_custom_call" | custom-call | tf_op jit(solution)/shard_map/halve/pallas_call | solution.py:392
  155.4 7.3 %norm_back.1 = (bf16[512,1024]{1,0:T(8,128)(2,1)}, f32[512,1024]{1,0:T(8,128)}, f32[32,128]{1,0:T(8,128)S(1)}) custom-call(bf16[512,1024]{1,0:T(8,128)(2,1)} %tok.3, bf16[512,1024]{1,0:T(8,128)(2,1)} %grad.1, f32[1,1024]{1,0:T(1,128)} %bitcast.110, f32[512,1024]{1,0:T(8,128)} %get-tuple-element.187.block_own, ...), custom_call_target="tpu_custom_call" | custom-call | tf_op jit(solution)/shard_map/norm_back/pallas_call | solution.py:392
  164.2 1.8 halve.18
  167.1 2.5 %collective-permute-start.17 = (bf16[2,32,1536]{2,1,0:T(8,128)(2,1)S(1)}, bf16[2,32,1536]{2,1,0:T(8,128)(2,1)S(1)}, u32[]{:S(2)}, u32[]{:S(2)}) collective-permute-start(bf16[2,32,1536]{2,1,0:T(8,128)(2,1)S(1)} %get-tuple-element.228), channel_id=1, source_target_pairs={{0,4},{1,5},{2,6},{3,7},{4,0},{5,1},{6,2},{7,3},{8,12},{9,13},{10,... | collective-permute-start | bytes 589832 | tf_op jit(solution)/shard_map/ppermute | solution.py:946
  173.0 2.1 %collective-permute-done.19 = f32[32,128]{1,0:T(8,128)S(1)} collective-permute-done((f32[32,128]{1,0:T(8,128)S(1)}, f32[32,128]{1,0:T(8,128)S(1)}, u32[]{:S(2)}, u32[]{:S(2)}) %collective-permute-start.19) | collective-permute-done | bytes 16416 | tf_op jit(solution)/shard_map/ppermute | solution.py:946
  175.5 3.3 %collective-permute-done.20 = f32[32,128]{1,0:T(8,128)S(1)} collective-permute-done((f32[32,128]{1,0:T(8,128)S(1)}, f32[32,128]{1,0:T(8,128)S(1)}, u32[]{:S(2)}, u32[]{:S(2)}) %collective-permute-start.20) | collective-permute-done | bytes 16416 | tf_op jit(solution)/shard_map/ppermute | solution.py:946
  179.4 1.6 collective-permute-start.21
  181.9 2.4 %collective-permute-start.24 = (bf16[2,16,1024]{2,1,0:T(8,128)(2,1)S(1)}, bf16[2,16,1024]{2,1,0:T(8,128)(2,1)S(1)}, u32[]{:S(2)}, u32[]{:S(2)}) collective-permute-start(bf16[2,16,1024]{2,1,0:T(8,128)(2,1)S(1)} %get-tuple-element.248), channel_id=1, source_target_pairs={{0,2},{1,3},{2,0},{3,1},{4,6},{5,7},{6,4},{7,5},{8,10},{9,11},{10,... | collective-permute-start | bytes 196616 | tf_op jit(solution)/shard_map/ppermute | solution.py:946
  185.0 3.7 %collective-permute-done.23 = f32[32,128]{1,0:T(8,128)S(1)} collective-permute-done((f32[32,128]{1,0:T(8,128)S(1)}, f32[32,128]{1,0:T(8,128)S(1)}, u32[]{:S(2)}, u32[]{:S(2)}) %collective-permute-start.23) | collective-permute-done | bytes 16416 | tf_op jit(solution)/shard_map/ppermute | solution.py:946
  188.7 2.0 collective-permute-done.21.d_got
  190.8 2.9 %collective-permute-start.27 = (f32[32,128]{1,0:T(8,128)S(1)}, f32[32,128]{1,0:T(8,128)S(1)}, u32[]{:S(2)}, u32[]{:S(2)}) collective-permute-start(f32[32,128]{1,0:T(8,128)S(1)} %add.73), channel_id=1, source_target_pairs={{0,4},{1,5},{2,6},{3,7},{4,0},{5,1},{6,2},{7,3},{8,12},{9,13},{10,... | collective-permute-start | bytes 49160 | tf_op jit(solution)/shard_map/ppermute | solution.py:946
  193.7 2.1 %collective-permute-done.27 = f32[32,128]{1,0:T(8,128)S(1)} collective-permute-done((f32[32,128]{1,0:T(8,128)S(1)}, f32[32,128]{1,0:T(8,128)S(1)}, u32[]{:S(2)}, u32[]{:S(2)}) %collective-permute-start.27) | collective-permute-done | bytes 16416 | tf_op jit(solution)/shard_map/ppermute | solution.py:946
  (145 shorter events, 36.1 us)
Async XLA Ops:
  6.1 9.6 %collective-permute-start = (bf16[512,1024]{1,0:T(8,128)(2,1)S(1)}, bf16[512,1024]{1,0:T(8,128)(2,1)}, u32[]{:S(2)}, u32[]{:S(2)}) collective-permute-start(bf16[512,1024]{1,0:T(8,128)(2,1)S(1)} %get-tuple-element.140.n_own), channel_id=1, source_target_pairs={{0,8},{1,9},{2,10},{3,11},{4,12},{5,13},{6,14},{7,15},{8,0},{9,1},... | collective-permute-start | bytes 3145736 | tf_op jit(solution)/shard_map/ppermute | solution.py:946
  6.5 9.1 %collective-permute-start.1 = (bf16[512,1024]{1,0:T(8,128)(2,1)S(1)}, bf16[512,1024]{1,0:T(8,128)(2,1)}, u32[]{:S(2)}, u32[]{:S(2)}) collective-permute-start(bf16[512,1024]{1,0:T(8,128)(2,1)S(1)} %copy-done.29), channel_id=1, source_target_pairs={{0,8},{1,9},{2,10},{3,11},{4,12},{5,13},{6,14},{7,15},{8,0},{9,1},... | collective-permute-start | bytes 3145736 | tf_op jit(solution)/shard_map/ppermute | solution.py:946
  6.6 22.0 %all-to-all-start = ((bf16[8,4,64,128]{3,2,1,0:T(8,128)(2,1)}), bf16[8,4,64,128]{3,2,1,0:T(8,128)(2,1)S(1)}, u32[]{:S(2)}, u32[]{:S(2)}) async-start(bf16[8,4,64,128]{3,2,1,0:T(8,128)(2,1)} %get-tuple-element.139), calls=%async_computation | async-start | bytes 1048576 | tf_op jit(solution)/shard_map/all_to_all | solution.py:949
  41.0 19.9 %all-to-all-start.1 = ((bf16[8,4,64,128]{3,2,1,0:T(8,128)(2,1)}), bf16[8,4,64,128]{3,2,1,0:T(8,128)(2,1)S(1)}, u32[]{:S(2)}, u32[]{:S(2)}) async-start(bf16[8,4,64,128]{3,2,1,0:T(8,128)(2,1)} %bitcast.108), calls=%async_computation.1 | async-start | bytes 1048576 | tf_op jit(solution)/shard_map/all_to_all | solution.py:949
  56.6 2.1 %collective-permute-start.2 = (bf16[8,4,64,128]{3,2,1,0:T(8,128)(2,1)}, bf16[8,4,64,128]{3,2,1,0:T(8,128)(2,1)S(1)}, u32[]{:S(2)}, u32[]{:S(2)}) collective-permute-start(bf16[8,4,64,128]{3,2,1,0:T(8,128)(2,1)} %get-tuple-element.157), channel_id=1, source_target_pairs={{0,8},{1,9},{2,10},{3,11},{4,12},{5,13},{6,14},{7,15},{8,0},{9,1},... | collective-permute-start | bytes 1572872 | tf_op jit(solution)/shard_map/ppermute | solution.py:946
  60.9 6.2 %collective-permute-start.3 = (bf16[8,4,64,128]{3,2,1,0:T(8,128)(2,1)S(1)}, bf16[8,4,64,128]{3,2,1,0:T(8,128)(2,1)S(1)}, u32[]{:S(2)}, u32[]{:S(2)}) collective-permute-start(bf16[8,4,64,128]{3,2,1,0:T(8,128)(2,1)S(1)} %all-to-all-done.1.y_own), channel_id=1, source_target_pairs={{0,8},{1,9},{2,10},{3,11},{4,12},{5,13},{6,14},{7,15},{8,0},{9,1},... | collective-permute-start | bytes 1572872 | tf_op jit(solution)/shard_map/ppermute | solution.py:946
  61.1 21.5 %all-to-all-start.2 = ((bf16[8,4,64,128]{3,2,1,0:T(8,128)(2,1)}), bf16[8,4,64,128]{3,2,1,0:T(8,128)(2,1)S(1)}, u32[]{:S(2)}, u32[]{:S(2)}) async-start(bf16[8,4,64,128]{3,2,1,0:T(8,128)(2,1)} %add_convert_fusion), calls=%async_computation.2 | async-start | bytes 1048576 | tf_op jit(solution)/shard_map/all_to_all | solution.py:949
  82.6 21.4 %collective-permute-start.4 = (bf16[16,32,1536]{2,1,0:T(8,128)(2,1)}, bf16[16,32,1536]{2,1,0:T(8,128)(2,1)S(1)}, u32[]{:S(2)}, u32[]{:S(2)}) collective-permute-start(bf16[16,32,1536]{2,1,0:T(8,128)(2,1)} %get-tuple-element.167), channel_id=1, source_target_pairs={{0,16},{1,17},{2,18},{3,19},{4,20},{5,21},{6,22},{7,23},{8,9},{9,8... | collective-permute-start | bytes 4718600 | tf_op jit(solution)/shard_map/ppermute | solution.py:946
  84.1 19.8 %collective-permute-start.5 = (bf16[16,16,1536]{2,1,0:T(8,128)(2,1)}, bf16[16,16,1536]{2,1,0:T(8,128)(2,1)S(1)}, u32[]{:S(2)}, u32[]{:S(2)}) collective-permute-start(bf16[16,16,1536]{2,1,0:T(8,128)(2,1)} %get-tuple-element.168), channel_id=1, source_target_pairs={{0,2},{1,3},{2,0},{3,1},{4,6},{5,7},{6,4},{7,5},{8,10},{9,11},{10,... | collective-permute-start | bytes 2359304 | tf_op jit(solution)/shard_map/ppermute | solution.py:946
  104.0 22.4 %collective-permute-start.6 = (bf16[8,96,1024]{2,1,0:T(8,128)(2,1)}, bf16[8,96,1024]{2,1,0:T(8,128)(2,1)S(1)}, u32[]{:S(2)}, u32[]{:S(2)}) collective-permute-start(bf16[8,96,1024]{2,1,0:T(8,128)(2,1)} %get-tuple-element.188), channel_id=1, source_target_pairs={{0,16},{1,17},{2,18},{3,19},{4,20},{5,21},{6,22},{7,23},{8,9},{9,8... | collective-permute-start | bytes 4718600 | tf_op jit(solution)/shard_map/ppermute | solution.py:946
  106.6 19.8 %collective-permute-start.7 = (bf16[8,16,1536]{2,1,0:T(8,128)(2,1)}, bf16[8,16,1536]{2,1,0:T(8,128)(2,1)}, u32[]{:S(2)}, u32[]{:S(2)}) collective-permute-start(bf16[8,16,1536]{2,1,0:T(8,128)(2,1)} %get-tuple-element.191), channel_id=1, source_target_pairs={{0,4},{1,5},{2,6},{3,7},{4,0},{5,1},{6,2},{7,3},{8,12},{9,13},{10,... | collective-permute-start | bytes 1179656 | tf_op jit(solution)/shard_map/ppermute | solution.py:946
  122.2 21.9 %all-to-all-start.3 = ((bf16[8,4,64,128]{3,2,1,0:T(8,128)(2,1)}), bf16[8,4,64,128]{3,2,1,0:T(8,128)(2,1)}, u32[]{:S(2)}, u32[]{:S(2)}) async-start(bf16[8,4,64,128]{3,2,1,0:T(8,128)(2,1)} %bitcast.107), calls=%async_computation.3 | async-start | bytes 1048576 | tf_op jit(solution)/shard_map/all_to_all | solution.py:949
  126.4 17.7 %collective-permute-start.8 = (bf16[8,32,1536]{2,1,0:T(8,128)(2,1)}, bf16[8,32,1536]{2,1,0:T(8,128)(2,1)}, u32[]{:S(2)}, u32[]{:S(2)}) collective-permute-start(bf16[8,32,1536]{2,1,0:T(8,128)(2,1)} %copy-done.16), channel_id=1, source_target_pairs={{0,1},{1,0},{2,3},{3,2},{4,5},{5,4},{6,7},{7,6},{8,24},{9,25},{10,... | collective-permute-start | bytes 2359304 | tf_op jit(solution)/shard_map/ppermute | solution.py:946
  129.2 14.9 %collective-permute-start.9 = (f32[2,2,64,128]{3,2,1,0:T(8,128)S(1)}, f32[2,2,64,128]{3,2,1,0:T(8,128)}, u32[]{:S(2)}, u32[]{:S(2)}) collective-permute-start(f32[2,2,64,128]{3,2,1,0:T(8,128)S(1)} %dynamic-slice_bitcast_fusion), channel_id=1, source_target_pairs={{0,8},{1,9},{2,10},{3,11},{4,12},{5,13},{6,14},{7,15},{8,0},{9,1},... | collective-permute-start | bytes 393224 | tf_op jit(solution)/shard_map/ppermute | solution.py:946
  144.1 11.3 %collective-permute-start.10 = (bf16[2,512,1024]{2,1,0:T(8,128)(2,1)}, bf16[2,512,1024]{2,1,0:T(8,128)(2,1)}, u32[]{:S(2)}, u32[]{:S(2)}) collective-permute-start(bf16[2,512,1024]{2,1,0:T(8,128)(2,1)} %get-tuple-element.200), channel_id=1, source_target_pairs={{0,8},{1,9},{2,10},{3,11},{4,12},{5,13},{6,14},{7,15},{8,0},{9,1},... | collective-permute-start | bytes 6291464 | tf_op jit(solution)/shard_map/ppermute | solution.py:946
  144.7 18.1 %collective-permute-start.12 = (bf16[4,96,1024]{2,1,0:T(8,128)(2,1)}, bf16[4,96,1024]{2,1,0:T(8,128)(2,1)S(1)}, u32[]{:S(2)}, u32[]{:S(2)}) collective-permute-start(bf16[4,96,1024]{2,1,0:T(8,128)(2,1)} %copy-done.15), channel_id=1, source_target_pairs={{0,1},{1,0},{2,3},{3,2},{4,5},{5,4},{6,7},{7,6},{8,24},{9,25},{10,... | collective-permute-start | bytes 2359304 | tf_op jit(solution)/shard_map/ppermute | solution.py:946
  149.5 3.3 %collective-permute-start.11 = (bf16[4,4,64,128]{3,2,1,0:T(8,128)(2,1)S(1)}, bf16[4,4,64,128]{3,2,1,0:T(8,128)(2,1)S(1)}, u32[]{:S(2)}, u32[]{:S(2)}) collective-permute-start(bf16[4,4,64,128]{3,2,1,0:T(8,128)(2,1)S(1)} %multiply_convert_fusion.1), channel_id=1, source_target_pairs={{0,8},{1,9},{2,10},{3,11},{4,12},{5,13},{6,14},{7,15},{8,0},{9,1},... | collective-permute-start | bytes 786440 | tf_op jit(solution)/shard_map/ppermute | solution.py:946
  150.0 12.7 %collective-permute-start.13 = (bf16[4,32,1536]{2,1,0:T(8,128)(2,1)S(1)}, bf16[4,32,1536]{2,1,0:T(8,128)(2,1)S(1)}, u32[]{:S(2)}, u32[]{:S(2)}) collective-permute-start(bf16[4,32,1536]{2,1,0:T(8,128)(2,1)S(1)} %get-tuple-element.215), channel_id=1, source_target_pairs={{0,2},{1,3},{2,0},{3,1},{4,6},{5,7},{6,4},{7,5},{8,10},{9,11},{10,... | collective-permute-start | bytes 1179656 | tf_op jit(solution)/shard_map/ppermute | solution.py:946
  154.2 8.6 %collective-permute-start.14 = (bf16[8,16,1024]{2,1,0:T(8,128)(2,1)S(1)}, bf16[8,16,1024]{2,1,0:T(8,128)(2,1)S(1)}, u32[]{:S(2)}, u32[]{:S(2)}) collective-permute-start(bf16[8,16,1024]{2,1,0:T(8,128)(2,1)S(1)} %get-tuple-element.209), channel_id=1, source_target_pairs={{0,16},{1,17},{2,18},{3,19},{4,20},{5,21},{6,22},{7,23},{8,9},{9,8... | collective-permute-start | bytes 786440 | tf_op jit(solution)/shard_map/ppermute | solution.py:946
  163.7 15.6 %collective-permute-start.15 = (bf16[2,96,1024]{2,1,0:T(8,128)(2,1)}, bf16[2,96,1024]{2,1,0:T(8,128)(2,1)S(1)}, u32[]{:S(2)}, u32[]{:S(2)}) collective-permute-start(bf16[2,96,1024]{2,1,0:T(8,128)(2,1)} %get-tuple-element.222), channel_id=1, source_target_pairs={{0,2},{1,3},{2,0},{3,1},{4,6},{5,7},{6,4},{7,5},{8,10},{9,11},{10,... | collective-permute-start | bytes 1179656 | tf_op jit(solution)/shard_map/ppermute | solution.py:946
  166.1 12.8 %collective-permute-start.16 = (bf16[4,16,1536]{2,1,0:T(8,128)(2,1)S(1)}, bf16[4,16,1536]{2,1,0:T(8,128)(2,1)S(1)}, u32[]{:S(2)}, u32[]{:S(2)}) collective-permute-start(bf16[4,16,1536]{2,1,0:T(8,128)(2,1)S(1)} %get-tuple-element.225), channel_id=1, source_target_pairs={{0,16},{1,17},{2,18},{3,19},{4,20},{5,21},{6,22},{7,23},{8,9},{9,8... | collective-permute-start | bytes 589832 | tf_op jit(solution)/shard_map/ppermute | solution.py:946
  167.1 11.8 %collective-permute-start.17 = (bf16[2,32,1536]{2,1,0:T(8,128)(2,1)S(1)}, bf16[2,32,1536]{2,1,0:T(8,128)(2,1)S(1)}, u32[]{:S(2)}, u32[]{:S(2)}) collective-permute-start(bf16[2,32,1536]{2,1,0:T(8,128)(2,1)S(1)} %get-tuple-element.228), channel_id=1, source_target_pairs={{0,4},{1,5},{2,6},{3,7},{4,0},{5,1},{6,2},{7,3},{8,12},{9,13},{10,... | collective-permute-start | bytes 589832 | tf_op jit(solution)/shard_map/ppermute | solution.py:946
  169.7 9.2 %collective-permute-start.18 = (bf16[4,16,1024]{2,1,0:T(8,128)(2,1)S(1)}, bf16[4,16,1024]{2,1,0:T(8,128)(2,1)S(1)}, u32[]{:S(2)}, u32[]{:S(2)}) collective-permute-start(bf16[4,16,1024]{2,1,0:T(8,128)(2,1)S(1)} %get-tuple-element.231), channel_id=1, source_target_pairs={{0,1},{1,0},{2,3},{3,2},{4,5},{5,4},{6,7},{7,6},{8,24},{9,25},{10,... | collective-permute-start | bytes 393224 | tf_op jit(solution)/shard_map/ppermute | solution.py:946
  171.2 3.9 %collective-permute-start.19 = (f32[32,128]{1,0:T(8,128)S(1)}, f32[32,128]{1,0:T(8,128)S(1)}, u32[]{:S(2)}, u32[]{:S(2)}) collective-permute-start(f32[32,128]{1,0:T(8,128)S(1)} %get-tuple-element.232), channel_id=1, source_target_pairs={{0,16},{1,17},{2,18},{3,19},{4,20},{5,21},{6,22},{7,23},{8,9},{9,8... | collective-permute-start | bytes 49160 | tf_op jit(solution)/shard_map/ppermute | solution.py:946
  175.1 3.7 %collective-permute-start.20 = (f32[32,128]{1,0:T(8,128)S(1)}, f32[32,128]{1,0:T(8,128)S(1)}, u32[]{:S(2)}, u32[]{:S(2)}) collective-permute-start(f32[32,128]{1,0:T(8,128)S(1)} %add.68), channel_id=1, source_target_pairs={{0,1},{1,0},{2,3},{3,2},{4,5},{5,4},{6,7},{7,6},{8,24},{9,25},{10,... | collective-permute-start | bytes 49160 | tf_op jit(solution)/shard_map/ppermute | solution.py:946
  179.4 11.3 %collective-permute-start.21 = (bf16[1,96,1024]{2,1,0:T(8,128)(2,1)S(1)}, bf16[1,96,1024]{2,1,0:T(8,128)(2,1)S(1)}, u32[]{:S(2)}, u32[]{:S(2)}) collective-permute-start(bf16[1,96,1024]{2,1,0:T(8,128)(2,1)S(1)} %get-tuple-element.243), channel_id=1, source_target_pairs={{0,4},{1,5},{2,6},{3,7},{4,0},{5,1},{6,2},{7,3},{8,12},{9,13},{10,... | collective-permute-start | bytes 589832 | tf_op jit(solution)/shard_map/ppermute | solution.py:946
  181.1 7.6 %collective-permute-start.22 = (bf16[2,16,1536]{2,1,0:T(8,128)(2,1)S(1)}, bf16[2,16,1536]{2,1,0:T(8,128)(2,1)S(1)}, u32[]{:S(2)}, u32[]{:S(2)}) collective-permute-start(bf16[2,16,1536]{2,1,0:T(8,128)(2,1)S(1)} %get-tuple-element.244), channel_id=1, source_target_pairs={{0,1},{1,0},{2,3},{3,2},{4,5},{5,4},{6,7},{7,6},{8,24},{9,25},{10,... | collective-permute-start | bytes 294920 | tf_op jit(solution)/shard_map/ppermute | solution.py:946
  181.9 6.8 %collective-permute-start.24 = (bf16[2,16,1024]{2,1,0:T(8,128)(2,1)S(1)}, bf16[2,16,1024]{2,1,0:T(8,128)(2,1)S(1)}, u32[]{:S(2)}, u32[]{:S(2)}) collective-permute-start(bf16[2,16,1024]{2,1,0:T(8,128)(2,1)S(1)} %get-tuple-element.248), channel_id=1, source_target_pairs={{0,2},{1,3},{2,0},{3,1},{4,6},{5,7},{6,4},{7,5},{8,10},{9,11},{10,... | collective-permute-start | bytes 196616 | tf_op jit(solution)/shard_map/ppermute | solution.py:946
  184.2 4.5 %collective-permute-start.25 = (f32[2,64,128]{2,1,0:T(8,128)S(1)}, f32[2,64,128]{2,1,0:T(8,128)S(1)}, u32[]{:S(2)}, u32[]{:S(2)}) collective-permute-start(f32[2,64,128]{2,1,0:T(8,128)S(1)} %dynamic-slice_bitcast_fusion.1), channel_id=1, source_target_pairs={{0,16},{1,17},{2,18},{3,19},{4,20},{5,21},{6,22},{7,23},{8,24},{9,... | collective-permute-start | bytes 196616 | tf_op jit(solution)/shard_map/ppermute | solution.py:946
  184.9 3.7 %collective-permute-start.23 = (f32[32,128]{1,0:T(8,128)S(1)}, f32[32,128]{1,0:T(8,128)S(1)}, u32[]{:S(2)}, u32[]{:S(2)}) collective-permute-start(f32[32,128]{1,0:T(8,128)S(1)} %add.69), channel_id=1, source_target_pairs={{0,2},{1,3},{2,0},{3,1},{4,6},{5,7},{6,4},{7,5},{8,10},{9,11},{10,... | collective-permute-start | bytes 49160 | tf_op jit(solution)/shard_map/ppermute | solution.py:946
  190.7 5.1 %collective-permute-start.26 = (bf16[1,16,1024]{2,1,0:T(8,128)(2,1)S(1)}, bf16[1,16,1024]{2,1,0:T(8,128)(2,1)S(1)}, u32[]{:S(2)}, u32[]{:S(2)}) collective-permute-start(bf16[1,16,1024]{2,1,0:T(8,128)(2,1)S(1)} %get-tuple-element.256), channel_id=1, source_target_pairs={{0,4},{1,5},{2,6},{3,7},{4,0},{5,1},{6,2},{7,3},{8,12},{9,13},{10,... | collective-permute-start | bytes 98312 | tf_op jit(solution)/shard_map/ppermute | solution.py:946
  190.8 5.0 %collective-permute-start.27 = (f32[32,128]{1,0:T(8,128)S(1)}, f32[32,128]{1,0:T(8,128)S(1)}, u32[]{:S(2)}, u32[]{:S(2)}) collective-permute-start(f32[32,128]{1,0:T(8,128)S(1)} %add.73), channel_id=1, source_target_pairs={{0,4},{1,5},{2,6},{3,7},{4,0},{5,1},{6,2},{7,3},{8,12},{9,13},{10,... | collective-permute-start | bytes 49160 | tf_op jit(solution)/shard_map/ppermute | solution.py:946
  (36 other events, 296.0 us)

commit v4 on v3

--- a/solution.py
+++ b/solution.py
@@ -361,6 +361,8 @@
 epsilon = 1e-05
 TILE = 768
 BLOCK_COLS = 256
+NORM_STEPS = 2
+TAIL_STEPS = 2
 
 
 def gauss_cdf(a):
@@ -418,8 +420,13 @@
     normed[...] = n
     v = mm(n, w_val[...])
     cdf = gauss_cdf(v)
-    v_act[...] = (v * cdf).T.astype(bf16).reshape(v_act.shape)
-    v_slope[...] = (cdf + v * gauss_pdf(v)).T.reshape(v_slope.shape)
+    act = (v * cdf).T.astype(bf16)
+    slope = (cdf + v * gauss_pdf(v)).T
+    shape = (v_act.shape[0], v_act.shape[2], T)
+    for q in range(v_act.shape[1]):
+        cut = slice(q * T, (q + 1) * T)
+        v_act[:, q] = act[:, cut].reshape(shape)
+        v_slope[:, q] = slope[:, cut].reshape(shape)
 
 
 def norm_call(tokens, gain, bias, w_val, chan_n):
@@ -427,12 +434,13 @@
     inner = w_val.shape[1]
     quads = own // T
     spread = (chan_n, quads, inner // chan_n, T)
-    block = pl.BlockSpec((chan_n, 1, inner // chan_n, T), lambda i: (0, i, 0, 0))
-    rows = pl.BlockSpec((T, width), lambda i: (i, 0))
+    steps = NORM_STEPS
+    block = pl.BlockSpec((chan_n, quads // steps, inner // chan_n, T), lambda i: (0, i, 0, 0))
+    rows = pl.BlockSpec((own // steps, width), lambda i: (i, 0))
     return call(
         norm_kernel,
         "norm_val",
-        (quads,),
+        (steps,),
         [rows, whole((1, width)), whole((1, width)), whole(w_val.shape)],
         [rows, block, block],
         [struct((own, width), bf16), struct(spread, bf16), in_hbm(spread, f32)],
@@ -625,7 +633,7 @@
         [in_hbm((2 * own, half), bf16)] * 2
         + [in_hbm((16, um, half), bf16)] * 2
         + [in_hbm((16, mx, half), bf16)] * 2,
-        from_hbm(y_own, y_oth, w_mix, u_act, d_slope, d_yproj, normed_t),
+        (y_own, y_oth, *from_hbm(w_mix, u_act, d_slope, d_yproj, normed_t)),
         scalars=scal,
         scratch=[
             pltpu.VMEM((inner, 2 * own), bf16),
@@ -675,31 +683,32 @@
 
 
 def split_kernel(s, down_g, down_k, d_give, d_keep):
-    d_give[0] = down_g[...]
-    d_keep[0] = down_k[...]
+    for src, dst in ((down_g, d_give), (down_k, d_keep)):
+        for low in (0, 1):
+            for high in (0, 1):
+                dst[low * 2 + high] = src[high * 2 + low]
 
 
 def split_call(scal, down):
     rows, width = down.shape[0] // 16, down.shape[1]
+    view = down.reshape(2, 4, 2, rows, width)
 
     def block_of(sel):
         def at(i, s):
-            a, b, low, high = mine_a(s) ^ sel, i // 4, (i // 2) % 2, i % 2
-            x = jnp.where(s[0] == 0, a, b)
-            y = jnp.where(s[0] == 0, b, a)
-            return x * 8 + high * 4 + low * 2 + y, 0
-
-        return pl.BlockSpec((rows, width), at)
-
-    out = pl.BlockSpec((1, rows, width), lambda i, s: (i, 0, 0))
+            a = mine_a(s) ^ sel
+            return jnp.where(s[0] == 0, a, i), 0, jnp.where(s[0] == 0, i, a), 0, 0
+
+        return pl.BlockSpec((None, 4, None, rows, width), at)
+
+    out = pl.BlockSpec((4, rows, width), lambda i, s: (i, 0, 0))
     return call(
         split_kernel,
         "split",
-        (8,),
+        (2,),
         [block_of(1), block_of(0)],
         [out, out],
         [struct((8, rows, width), bf16)] * 2,
-        (down, down),
+        (view, view),
         scalars=scal,
     )
 
@@ -783,7 +792,9 @@
     x = tok[...].astype(f32)
     x_hat, inv_std = normalise(x)
     block_out[...] = (x + block_own[...] + got[0].astype(f32)).astype(bf16)
-    dv = d_vpre[...].reshape(w_val.shape[1], T).T
+    dv = jnp.concatenate(
+        [d_vpre[:, q].reshape(w_val.shape[1], T).T for q in range(d_vpre.shape[1])], 0
+    )
     dn = dn_own[...] + got[1].astype(f32) + mm(dv, w_val[...], NT)
     dx = dn * gain[...]
     tokens_grad[...] = grad[...].astype(f32) + inv_std * (
@@ -815,26 +826,28 @@
 
 def tail_call(tokens, grad, gain, block_own, got, dn_own, d_vpre, w_val, parts):
     own, width = tokens.shape
-    rows = pl.BlockSpec((T, width), lambda i: (i, 0))
-    chan_n, _, group, _ = d_vpre.shape
+    steps = TAIL_STEPS
+    rows = pl.BlockSpec((own // steps, width), lambda i: (i, 0))
+    chan_n, quads, group, _ = d_vpre.shape
     return call(
         tail_kernel,
         "norm_back",
-        (own // T,),
+        (steps,),
         [
             rows,
             rows,
             whole((1, width)),
             rows,
-            pl.BlockSpec((2, T, width), lambda i: (0, i, 0)),
+            pl.BlockSpec((2, own // steps, width), lambda i: (0, i, 0)),
             rows,
-            pl.BlockSpec((chan_n, 1, group, T), lambda i: (0, i, 0, 0)),
+            pl.BlockSpec((chan_n, quads // steps, group, T), lambda i: (0, i, 0, 0)),
             whole(w_val.shape),
         ],
         [rows, rows, whole((parts, T))],
         [struct((own, width), bf16), struct((own, width), f32), struct((parts, T), f32)],
         from_hbm(tokens, grad, gain[None], block_own, got, dn_own, d_vpre, w_val),
         scratch=[pltpu.VMEM((2, width), f32)],
+        vmem=32,
     )
 
 
@@ -1024,7 +1037,7 @@
         d_give, d_keep = step_call(bit_low, d_keep, d_got)
         d_got = send(d_give, "low")
         u_give, u_keep = step_call(bit_high, u_keep, u_got)
-        u_give, norm_part = after((u_give, norm_part))
+        u_give, norm_part, m_got, v_got = after((u_give, norm_part, m_got, v_got))
         u_got = send(u_give, "high")
         m_give, m_keep = step_call(bit_a, m_keep, m_got)
         m_got = send(m_give, "a")

time: 202 us -> 198 us (0.980)
  Pallas kernels: 113 us -> 108 us
    pallas_call x22, Pallas kernels: 77.7 us -> 73.6 us  [call(): pl.pallas_call(kernel, grid_spec=pltpu.PrefetchScalarGridSpec(num_scalar_...]
    unnamed x70 -> x66, local copies, waits for them, and re-layouts: 6.08 us -> 5.24 us
  transfers between devices with their start and end apart: 33 -> 33, of which waited for: 9 -> 12; matrix products, arithmetic and copies ran while one was open for 5% -> 6% of each run, Pallas kernels for 45% -> 45%
where the time goes in v4:
time: 198 us; the launch traced here: 197 us
  Pallas kernels  108 us (55%)
  starting transfers between devices  51.6 us (26%)
  waiting for transfers between devices  19.4 us (10%)
  local copies, waits for them, and re-layouts  7.45 us (4%)
  other arithmetic  5.64 us (3%)
  matrix products  3.73 us (2%)
    pallas_call x22, Pallas kernels, call(): pl.pallas_call(kernel, grid_spec=pltpu.PrefetchScalarGridSpec(num_scalar_...  73.6 us
    ppermute x29, starting transfers between devices, send(): return lax.ppermute(value, ('row', 'chan'), pairs)  30.2 us
    all_to_all x4, starting transfers between devices, on_device(): lax.all_to_all(v, 'chan', split_axis=0, concat_axis=0, tiled=True)  21.4 us
    pallas_call x2, Pallas kernels, ssm_bwd(): pl.pallas_call(bwd_kernel, grid=(steps,), in_specs=[s['sm'], s['ch'], s['...  21 us
    ppermute x29, waiting for transfers between devices, send(): return lax.ppermute(value, ('row', 'chan'), pairs)  16.5 us
    pallas_call x1, Pallas kernels, ssm_fwd(): pl.pallas_call(fwd_kernel, grid=(chans // GROUP,), in_specs=[s['sm'], s['...  12.3 us
    unnamed x66, local copies, waits for them, and re-layouts  5.24 us
  transfers between devices with their start and end apart: 33, of which 12 were waited for; matrix products, arithmetic and copies ran while one was open for 6% of the time, Pallas kernels for 45%

profile of v4, /device:TPU:0, one launch (start us, length us, event | category | flops | bytes accessed | tf_op | source)
XLA Modules:
  0.0 197.4 jit_solution(10492126870536854896)
XLA Ops:
  0.7 4.4 %norm_val.1 = (bf16[512,1024]{1,0:T(8,128)(2,1)S(1)}, bf16[8,4,64,128]{3,2,1,0:T(8,128)(2,1)}, f32[8,4,64,128]{3,2,1,0:T(8,128)}) custom-call(bf16[512,1024]{1,0:T(8,128)(2,1)} %tok.3, f32[1,1024]{1,0:T(1,128)} %bitcast.112, f32[1,1024]{1,0:T(1,128)} %bitcast.115, bf16[1024,512]{1,0:T(8,128)(2,1)} %w_val.3), custom_call_target="tpu_custom_call" | custom-call | tf_op jit(solution)/shard_map/norm_val/pallas_call | solution.py:394
  5.6 7.3 %all-to-all-start = ((bf16[8,4,64,128]{3,2,1,0:T(8,128)(2,1)}), bf16[8,4,64,128]{3,2,1,0:T(8,128)(2,1)S(1)}, u32[]{:S(2)}, u32[]{:S(2)}) async-start(bf16[8,4,64,128]{3,2,1,0:T(8,128)(2,1)} %get-tuple-element.141), calls=%async_computation | async-start | bytes 1048576 | tf_op jit(solution)/shard_map/all_to_all | solution.py:962
  12.9 1.6 masks.1
  14.7 10.9 %gate_first.1 = (bf16[1024,1536]{1,0:T(8,128)(2,1)}, bf16[1024,1536]{1,0:T(8,128)(2,1)}, bf16[1024,1536]{1,0:T(8,128)(2,1)}, bf16[1024,1024]{1,0:T(8,128)(2,1)},...) custom-call(s32[8]{0:T(128)S(1)} %stack.35.core.s, bf16[512,1024]{1,0:T(8,128)(2,1)} %copy-done.8, ...), custom_call_target="tpu_custom_call" | custom-call | tf_op jit(solution)/shard_map/gate_first/pallas_call | solution.py:394
  25.6 2.0 %all-to-all-done = bf16[8,4,64,128]{3,2,1,0:T(8,128)(2,1)S(1)} async-done(((bf16[8,4,64,128]{3,2,1,0:T(8,128)(2,1)}), bf16[8,4,64,128]{3,2,1,0:T(8,128)(2,1)S(1)}, u32[]{:S(2)}, u32[]{:S(2)}) %all-to-all-start) | async-done | bytes 524320 | tf_op jit(solution)/shard_map/all_to_all | solution.py:962
  27.7 12.3 %ssm_fwd.1 = (bf16[32,64,128]{2,1,0:T(8,128)(2,1)}, f32[8,4,256,128]{3,2,1,0:T(8,128)}, bf16[64,128,128]{2,1,0:T(8,128)(2,1)}) custom-call(s32[8,128]{1,0:T(8,128)S(1)} %copy-done.28, bf16[32,64,128]{2,1,0:T(8,128)(2,1)S(1)} %bitcast.101, f32[64,512]{1,0:T(8,128)S(1)} %copy-done.17, f32[64,512]{1,0:T(8,128)S(1)} %copy-done.19, s32[32,128]{1,0:T(8,128)S(1)} %copy-done.21, ...), custom_call_target="tpu_custom_call" | custom-call | flops 20000000000 | bytes 10000000 | tf_op jit(solution)/shard_map/ssm_fwd/pallas_call | solution.py:305
  40.1 4.0 %all-to-all-start.1 = ((bf16[8,4,64,128]{3,2,1,0:T(8,128)(2,1)}), bf16[8,4,64,128]{3,2,1,0:T(8,128)(2,1)S(1)}, u32[]{:S(2)}, u32[]{:S(2)}) async-start(bf16[8,4,64,128]{3,2,1,0:T(8,128)(2,1)} %bitcast.111), calls=%async_computation.1 | async-start | bytes 1048576 | tf_op jit(solution)/shard_map/all_to_all | solution.py:962
  44.0 11.5 %gate_last.1 = (bf16[1024,1536]{1,0:T(8,128)(2,1)}, bf16[1024,1536]{1,0:T(8,128)(2,1)}, bf16[1024,1536]{1,0:T(8,128)(2,1)}, bf16[1024,1024]{1,0:T(8,128)(2,1)}, ...) custom-call(s32[8]{0:T(128)S(1)} %stack.35.core.s, ...), custom_call_target="tpu_custom_call", output_to_operand_aliasing={{0}: (7, {}), {1}: (8, {}), {2}: (9, {})} | custom-call | tf_op jit(solution)/shard_map/gate_last/pallas_call | solution.py:394
  55.6 2.1 %collective-permute-done.2 = bf16[8,4,64,128]{3,2,1,0:T(8,128)(2,1)S(1)} collective-permute-done((bf16[8,4,64,128]{3,2,1,0:T(8,128)(2,1)}, bf16[8,4,64,128]{3,2,1,0:T(8,128)(2,1)S(1)}, u32[]{:S(2)}, u32[]{:S(2)}) %collective-permute-start.2) | collective-permute-done | bytes 524320 | tf_op jit(solution)/shard_map/ppermute | solution.py:959
  57.7 2.2 %add_convert_fusion = bf16[8,4,64,128]{3,2,1,0:T(8,128)(2,1)} fusion(f32[8,4,64,128]{3,2,1,0:T(8,128)} %get-tuple-element.158, bf16[8,4,64,128]{3,2,1,0:T(8,128)(2,1)S(1)} %collective-permute-done.2), kind=kLoop, calls=%fused_computation.2 | loop fusion | flops 786432 | bytes 2097152 | tf_op jit(solution)/shard_map/convert_element_type | solution.py:982
  60.0 6.0 %all-to-all-start.2 = ((bf16[8,4,64,128]{3,2,1,0:T(8,128)(2,1)}), bf16[8,4,64,128]{3,2,1,0:T(8,128)(2,1)S(1)}, u32[]{:S(2)}, u32[]{:S(2)}) async-start(bf16[8,4,64,128]{3,2,1,0:T(8,128)(2,1)} %add_convert_fusion), calls=%async_computation.2 | async-start | bytes 1048576 | tf_op jit(solution)/shard_map/all_to_all | solution.py:962
  66.0 14.1 %mix_up.1 = (bf16[1024,1536]{1,0:T(8,128)(2,1)}, bf16[1024,1536]{1,0:T(8,128)(2,1)}, bf16[16,32,1536]{2,1,0:T(8,128)(2,1)}, bf16[16,32,1536]{2,1,0:T(8,128)(2,1)...) custom-call(s32[8]{0:T(128)S(1)} %stack.35.core.s, bf16[8,4,64,128]{3,2,1,0:T(8,128)(2,1)S(1)} %all-to-all-done.1.y_own, ...), custom_call_target="tpu_custom_call" | custom-call | flops 10000000000 | bytes 10000000 | tf_op jit(solution)/shard_map/mix_up/pallas_call | solution.py:394
  83.7 10.4 %ssm_bwd.2 = (bf16[32,64,128]{2,1,0:T(8,128)(2,1)}, f32[2,2,2,64,128]{4,3,2,1,0:T(8,128)S(1)}) custom-call(s32[8,128]{1,0:T(8,128)S(1)} %copy-done.28, bf16[32,64,128]{2,1,0:T(8,128)(2,1)S(1)} %bitcast.102, bf16[32,64,128]{2,1,0:T(8,128)(2,1)S(1)} %bitcast.104, f32[64,512]{1,0:T(8,128)S(1)} %copy-done.17, f32[64,512]{1,0:T(8,128)S(1)} %copy-done.19, ...), custom_call_target="tpu_custom_call" | custom-call | flops 20000000000 | bytes 10000000 | tf_op jit(solution)/shard_map/ssm_bwd/pallas_call | solution.py:328
  94.2 3.7 %convolution_convert_fusion = bf16[1536,1024]{1,0:T(8,128)(2,1)S(1)} fusion(bf16[1024,1536]{1,0:T(8,128)(2,1)S(1)} %copy-done.30, bf16[1024,1024]{1,0:T(8,128)(2,1)S(1)} %copy-done.32), kind=kOutput, calls=%fused_computation | convolution fusion | flops 3222798336 | bytes 8388608 | tf_op jit(solution)/shard_map/dot_general | solution.py:22
  97.9 2.1 %split.1 = (bf16[8,96,1024]{2,1,0:T(8,128)(2,1)}, bf16[8,96,1024]{2,1,0:T(8,128)(2,1)S(1)}) custom-call(s32[8]{0:T(128)S(1)} %stack.35.core.s, bf16[2,4,2,96,1024]{4,3,2,1,0:T(8,128)(2,1)S(1)} %bitcast.59, bf16[2,4,2,96,1024]{4,3,2,1,0:T(8,128)(2,1)S(1)} %bitcast.60), custom_call_target="tpu_custom_call" | custom-call | tf_op jit(solution)/shard_map/split/pallas_call | solution.py:394
  104.5 2.2 %collective-permute-start.7 = (bf16[8,16,1536]{2,1,0:T(8,128)(2,1)}, bf16[8,16,1536]{2,1,0:T(8,128)(2,1)}, u32[]{:S(2)}, u32[]{:S(2)}) collective-permute-start(bf16[8,16,1536]{2,1,0:T(8,128)(2,1)} %get-tuple-element.193), channel_id=1, source_target_pairs={{0,4},{1,5},{2,6},{3,7},{4,0},{5,1},{6,2},{7,3},{8,12},{9,13},{10,... | collective-permute-start | bytes 1179656 | tf_op jit(solution)/shard_map/ppermute | solution.py:959
  106.7 10.5 %ssm_bwd.3 = (bf16[32,64,128]{2,1,0:T(8,128)(2,1)}, f32[2,2,2,64,128]{4,3,2,1,0:T(8,128)S(1)}) custom-call(s32[8,128]{1,0:T(8,128)S(1)} %copy-done.28, bf16[32,64,128]{2,1,0:T(8,128)(2,1)S(1)} %bitcast.103, bf16[32,64,128]{2,1,0:T(8,128)(2,1)S(1)} %bitcast.105, f32[64,512]{1,0:T(8,128)S(1)} %copy-done.18, ...), custom_call_target="tpu_custom_call", output_to_operand_aliasing={{0}: (11, {}), {1}: (12, {})} | custom-call | flops 20000000000 | bytes 10000000 | tf_op jit(solution)/shard_map/ssm_bwd/pallas_call | solution.py:328
  119.8 4.1 %all-to-all-start.3 = ((bf16[8,4,64,128]{3,2,1,0:T(8,128)(2,1)}), bf16[8,4,64,128]{3,2,1,0:T(8,128)(2,1)}, u32[]{:S(2)}, u32[]{:S(2)}) async-start(bf16[8,4,64,128]{3,2,1,0:T(8,128)(2,1)} %bitcast.110), calls=%async_computation.3 | async-start | bytes 1048576 | tf_op jit(solution)/shard_map/all_to_all | solution.py:962
  123.9 1.9 collective-permute-start.8
  126.9 12.4 %block.1 = (f32[512,1024]{1,0:T(8,128)}, f32[512,1024]{1,0:T(8,128)}, bf16[2,512,1024]{2,1,0:T(8,128)(2,1)}) custom-call(s32[8]{0:T(128)S(1)} %stack.35.core.s, bf16[1024,1536]{1,0:T(8,128)(2,1)} %get-tuple-element.187.gate, bf16[1024,1536]{1,0:T(8,128)(2,1)} %get-tuple-element.188.d_upre, bf16[3072,1024]{1,0:T(8,128)(2,1)} %refs_1_.1, ...), custom_call_target="tpu_custom_call" | custom-call | tf_op jit(solution)/shard_map/block/pallas_call | solution.py:394
  143.5 2.2 %halve.15 = (bf16[4,32,1536]{2,1,0:T(8,128)(2,1)S(1)}, bf16[4,32,1536]{2,1,0:T(8,128)(2,1)S(1)}) custom-call(s32[1]{0:T(128)} %bitcast.4.bit, bf16[2,4,32,1536]{3,2,1,0:T(8,128)(2,1)S(1)} %bitcast.71, bf16[2,4,32,1536]{3,2,1,0:T(8,128)(2,1)} %bitcast.24.got_g.got_k, bf16[2,4,32,1536]{3,2,1,0:T(8,128)(2,1)S(1)} %bitcast.72, ...), custom_call_target="tpu_custom_call" | custom-call | tf_op jit(solution)/shard_map/halve/pallas_call | solution.py:394
  147.3 1.8 collective-permute-start.13
  153.0 6.3 %norm_back.1 = (bf16[512,1024]{1,0:T(8,128)(2,1)}, f32[512,1024]{1,0:T(8,128)}, f32[32,128]{1,0:T(8,128)S(1)}) custom-call(bf16[512,1024]{1,0:T(8,128)(2,1)} %tok.3, bf16[512,1024]{1,0:T(8,128)(2,1)} %grad.1, f32[1,1024]{1,0:T(1,128)} %bitcast.113, f32[512,1024]{1,0:T(8,128)} %get-tuple-element.189.block_own, ...), custom_call_target="tpu_custom_call" | custom-call | tf_op jit(solution)/shard_map/norm_back/pallas_call | solution.py:394
  161.6 1.8 halve.18
  164.3 2.4 %collective-permute-start.17 = (bf16[2,32,1536]{2,1,0:T(8,128)(2,1)S(1)}, bf16[2,32,1536]{2,1,0:T(8,128)(2,1)S(1)}, u32[]{:S(2)}, u32[]{:S(2)}) collective-permute-start(bf16[2,32,1536]{2,1,0:T(8,128)(2,1)S(1)} %get-tuple-element.232), channel_id=1, source_target_pairs={{0,4},{1,5},{2,6},{3,7},{4,0},{5,1},{6,2},{7,3},{8,12},{9,13},{10,... | collective-permute-start | bytes 589832 | tf_op jit(solution)/shard_map/ppermute | solution.py:959
  172.8 2.8 %collective-permute-done.20 = f32[32,128]{1,0:T(8,128)S(1)} collective-permute-done((f32[32,128]{1,0:T(8,128)S(1)}, f32[32,128]{1,0:T(8,128)S(1)}, u32[]{:S(2)}, u32[]{:S(2)}) %collective-permute-start.20) | collective-permute-done | bytes 16416 | tf_op jit(solution)/shard_map/ppermute | solution.py:959
  175.9 1.8 collective-permute-start.21
  179.3 1.6 collective-permute-start.24
  182.0 3.2 %collective-permute-done.23 = f32[32,128]{1,0:T(8,128)S(1)} collective-permute-done((f32[32,128]{1,0:T(8,128)S(1)}, f32[32,128]{1,0:T(8,128)S(1)}, u32[]{:S(2)}, u32[]{:S(2)}) %collective-permute-start.23) | collective-permute-done | bytes 16416 | tf_op jit(solution)/shard_map/ppermute | solution.py:959
  185.2 2.0 %collective-permute-done.21.d_got = bf16[1,96,1024]{2,1,0:T(8,128)(2,1)S(1)} collective-permute-done((bf16[1,96,1024]{2,1,0:T(8,128)(2,1)S(1)}, bf16[1,96,1024]{2,1,0:T(8,128)(2,1)S(1)}, u32[]{:S(2)}, u32[]{:S(2)}) %collective-permute-start.21) | collective-permute-done | bytes 196640 | tf_op jit(solution)/shard_map/ppermute | solution.py:959
  187.7 2.5 %collective-permute-start.27 = (f32[32,128]{1,0:T(8,128)S(1)}, f32[32,128]{1,0:T(8,128)S(1)}, u32[]{:S(2)}, u32[]{:S(2)}) collective-permute-start(f32[32,128]{1,0:T(8,128)S(1)} %add.73), channel_id=1, source_target_pairs={{0,4},{1,5},{2,6},{3,7},{4,0},{5,1},{6,2},{7,3},{8,12},{9,13},{10,... | collective-permute-start | bytes 49160 | tf_op jit(solution)/shard_map/ppermute | solution.py:959
  190.2 2.2 %collective-permute-done.27 = f32[32,128]{1,0:T(8,128)S(1)} collective-permute-done((f32[32,128]{1,0:T(8,128)S(1)}, f32[32,128]{1,0:T(8,128)S(1)}, u32[]{:S(2)}, u32[]{:S(2)}) %collective-permute-start.27) | collective-permute-done | bytes 16416 | tf_op jit(solution)/shard_map/ppermute | solution.py:959
  (141 shorter events, 39.9 us)
Async XLA Ops:
  5.1 9.6 %collective-permute-start = (bf16[512,1024]{1,0:T(8,128)(2,1)S(1)}, bf16[512,1024]{1,0:T(8,128)(2,1)}, u32[]{:S(2)}, u32[]{:S(2)}) collective-permute-start(bf16[512,1024]{1,0:T(8,128)(2,1)S(1)} %get-tuple-element.142.n_own), channel_id=1, source_target_pairs={{0,8},{1,9},{2,10},{3,11},{4,12},{5,13},{6,14},{7,15},{8,0},{9,1},... | collective-permute-start | bytes 3145736 | tf_op jit(solution)/shard_map/ppermute | solution.py:959
  5.6 9.1 %collective-permute-start.1 = (bf16[512,1024]{1,0:T(8,128)(2,1)S(1)}, bf16[512,1024]{1,0:T(8,128)(2,1)}, u32[]{:S(2)}, u32[]{:S(2)}) collective-permute-start(bf16[512,1024]{1,0:T(8,128)(2,1)S(1)} %copy-done.29), channel_id=1, source_target_pairs={{0,8},{1,9},{2,10},{3,11},{4,12},{5,13},{6,14},{7,15},{8,0},{9,1},... | collective-permute-start | bytes 3145736 | tf_op jit(solution)/shard_map/ppermute | solution.py:959
  5.6 22.0 %all-to-all-start = ((bf16[8,4,64,128]{3,2,1,0:T(8,128)(2,1)}), bf16[8,4,64,128]{3,2,1,0:T(8,128)(2,1)S(1)}, u32[]{:S(2)}, u32[]{:S(2)}) async-start(bf16[8,4,64,128]{3,2,1,0:T(8,128)(2,1)} %get-tuple-element.141), calls=%async_computation | async-start | bytes 1048576 | tf_op jit(solution)/shard_map/all_to_all | solution.py:962
  40.1 19.8 %all-to-all-start.1 = ((bf16[8,4,64,128]{3,2,1,0:T(8,128)(2,1)}), bf16[8,4,64,128]{3,2,1,0:T(8,128)(2,1)S(1)}, u32[]{:S(2)}, u32[]{:S(2)}) async-start(bf16[8,4,64,128]{3,2,1,0:T(8,128)(2,1)} %bitcast.111), calls=%async_computation.1 | async-start | bytes 1048576 | tf_op jit(solution)/shard_map/all_to_all | solution.py:962
  55.6 2.1 %collective-permute-start.2 = (bf16[8,4,64,128]{3,2,1,0:T(8,128)(2,1)}, bf16[8,4,64,128]{3,2,1,0:T(8,128)(2,1)S(1)}, u32[]{:S(2)}, u32[]{:S(2)}) collective-permute-start(bf16[8,4,64,128]{3,2,1,0:T(8,128)(2,1)} %get-tuple-element.159), channel_id=1, source_target_pairs={{0,8},{1,9},{2,10},{3,11},{4,12},{5,13},{6,14},{7,15},{8,0},{9,1},... | collective-permute-start | bytes 1572872 | tf_op jit(solution)/shard_map/ppermute | solution.py:959
  59.9 6.2 %collective-permute-start.3 = (bf16[8,4,64,128]{3,2,1,0:T(8,128)(2,1)S(1)}, bf16[8,4,64,128]{3,2,1,0:T(8,128)(2,1)S(1)}, u32[]{:S(2)}, u32[]{:S(2)}) collective-permute-start(bf16[8,4,64,128]{3,2,1,0:T(8,128)(2,1)S(1)} %all-to-all-done.1.y_own), channel_id=1, source_target_pairs={{0,8},{1,9},{2,10},{3,11},{4,12},{5,13},{6,14},{7,15},{8,0},{9,1},... | collective-permute-start | bytes 1572872 | tf_op jit(solution)/shard_map/ppermute | solution.py:959
  60.0 21.0 %all-to-all-start.2 = ((bf16[8,4,64,128]{3,2,1,0:T(8,128)(2,1)}), bf16[8,4,64,128]{3,2,1,0:T(8,128)(2,1)S(1)}, u32[]{:S(2)}, u32[]{:S(2)}) async-start(bf16[8,4,64,128]{3,2,1,0:T(8,128)(2,1)} %add_convert_fusion), calls=%async_computation.2 | async-start | bytes 1048576 | tf_op jit(solution)/shard_map/all_to_all | solution.py:962
  81.0 20.6 %collective-permute-start.4 = (bf16[16,32,1536]{2,1,0:T(8,128)(2,1)}, bf16[16,32,1536]{2,1,0:T(8,128)(2,1)S(1)}, u32[]{:S(2)}, u32[]{:S(2)}) collective-permute-start(bf16[16,32,1536]{2,1,0:T(8,128)(2,1)} %get-tuple-element.169), channel_id=1, source_target_pairs={{0,16},{1,17},{2,18},{3,19},{4,20},{5,21},{6,22},{7,23},{8,9},{9,8... | collective-permute-start | bytes 4718600 | tf_op jit(solution)/shard_map/ppermute | solution.py:959
  82.5 18.9 %collective-permute-start.5 = (bf16[16,16,1536]{2,1,0:T(8,128)(2,1)}, bf16[16,16,1536]{2,1,0:T(8,128)(2,1)S(1)}, u32[]{:S(2)}, u32[]{:S(2)}) collective-permute-start(bf16[16,16,1536]{2,1,0:T(8,128)(2,1)} %get-tuple-element.170), channel_id=1, source_target_pairs={{0,2},{1,3},{2,0},{3,1},{4,6},{5,7},{6,4},{7,5},{8,10},{9,11},{10,... | collective-permute-start | bytes 2359304 | tf_op jit(solution)/shard_map/ppermute | solution.py:959
  101.7 22.3 %collective-permute-start.6 = (bf16[8,96,1024]{2,1,0:T(8,128)(2,1)}, bf16[8,96,1024]{2,1,0:T(8,128)(2,1)S(1)}, u32[]{:S(2)}, u32[]{:S(2)}) collective-permute-start(bf16[8,96,1024]{2,1,0:T(8,128)(2,1)} %get-tuple-element.190), channel_id=1, source_target_pairs={{0,16},{1,17},{2,18},{3,19},{4,20},{5,21},{6,22},{7,23},{8,9},{9,8... | collective-permute-start | bytes 4718600 | tf_op jit(solution)/shard_map/ppermute | solution.py:959
  104.5 19.4 %collective-permute-start.7 = (bf16[8,16,1536]{2,1,0:T(8,128)(2,1)}, bf16[8,16,1536]{2,1,0:T(8,128)(2,1)}, u32[]{:S(2)}, u32[]{:S(2)}) collective-permute-start(bf16[8,16,1536]{2,1,0:T(8,128)(2,1)} %get-tuple-element.193), channel_id=1, source_target_pairs={{0,4},{1,5},{2,6},{3,7},{4,0},{5,1},{6,2},{7,3},{8,12},{9,13},{10,... | collective-permute-start | bytes 1179656 | tf_op jit(solution)/shard_map/ppermute | solution.py:959
  119.8 21.9 %all-to-all-start.3 = ((bf16[8,4,64,128]{3,2,1,0:T(8,128)(2,1)}), bf16[8,4,64,128]{3,2,1,0:T(8,128)(2,1)}, u32[]{:S(2)}, u32[]{:S(2)}) async-start(bf16[8,4,64,128]{3,2,1,0:T(8,128)(2,1)} %bitcast.110), calls=%async_computation.3 | async-start | bytes 1048576 | tf_op jit(solution)/shard_map/all_to_all | solution.py:962
  123.9 17.7 %collective-permute-start.8 = (bf16[8,32,1536]{2,1,0:T(8,128)(2,1)}, bf16[8,32,1536]{2,1,0:T(8,128)(2,1)}, u32[]{:S(2)}, u32[]{:S(2)}) collective-permute-start(bf16[8,32,1536]{2,1,0:T(8,128)(2,1)} %copy-done.16), channel_id=1, source_target_pairs={{0,1},{1,0},{2,3},{3,2},{4,5},{5,4},{6,7},{7,6},{8,24},{9,25},{10,... | collective-permute-start | bytes 2359304 | tf_op jit(solution)/shard_map/ppermute | solution.py:959
  126.8 14.8 %collective-permute-start.9 = (f32[2,2,64,128]{3,2,1,0:T(8,128)S(1)}, f32[2,2,64,128]{3,2,1,0:T(8,128)}, u32[]{:S(2)}, u32[]{:S(2)}) collective-permute-start(f32[2,2,64,128]{3,2,1,0:T(8,128)S(1)} %dynamic-slice_bitcast_fusion), channel_id=1, source_target_pairs={{0,8},{1,9},{2,10},{3,11},{4,12},{5,13},{6,14},{7,15},{8,0},{9,1},... | collective-permute-start | bytes 393224 | tf_op jit(solution)/shard_map/ppermute | solution.py:959
  141.7 11.3 %collective-permute-start.10 = (bf16[2,512,1024]{2,1,0:T(8,128)(2,1)}, bf16[2,512,1024]{2,1,0:T(8,128)(2,1)}, u32[]{:S(2)}, u32[]{:S(2)}) collective-permute-start(bf16[2,512,1024]{2,1,0:T(8,128)(2,1)} %get-tuple-element.202), channel_id=1, source_target_pairs={{0,8},{1,9},{2,10},{3,11},{4,12},{5,13},{6,14},{7,15},{8,0},{9,1},... | collective-permute-start | bytes 6291464 | tf_op jit(solution)/shard_map/ppermute | solution.py:959
  142.2 17.0 %collective-permute-start.12 = (bf16[4,96,1024]{2,1,0:T(8,128)(2,1)}, bf16[4,96,1024]{2,1,0:T(8,128)(2,1)S(1)}, u32[]{:S(2)}, u32[]{:S(2)}) collective-permute-start(bf16[4,96,1024]{2,1,0:T(8,128)(2,1)} %copy-done.15), channel_id=1, source_target_pairs={{0,1},{1,0},{2,3},{3,2},{4,5},{5,4},{6,7},{7,6},{8,24},{9,25},{10,... | collective-permute-start | bytes 2359304 | tf_op jit(solution)/shard_map/ppermute | solution.py:959
  147.1 3.2 %collective-permute-start.11 = (bf16[4,4,64,128]{3,2,1,0:T(8,128)(2,1)S(1)}, bf16[4,4,64,128]{3,2,1,0:T(8,128)(2,1)S(1)}, u32[]{:S(2)}, u32[]{:S(2)}) collective-permute-start(bf16[4,4,64,128]{3,2,1,0:T(8,128)(2,1)S(1)} %multiply_convert_fusion.1), channel_id=1, source_target_pairs={{0,8},{1,9},{2,10},{3,11},{4,12},{5,13},{6,14},{7,15},{8,0},{9,1},... | collective-permute-start | bytes 786440 | tf_op jit(solution)/shard_map/ppermute | solution.py:959
  147.3 11.9 %collective-permute-start.13 = (bf16[4,32,1536]{2,1,0:T(8,128)(2,1)S(1)}, bf16[4,32,1536]{2,1,0:T(8,128)(2,1)S(1)}, u32[]{:S(2)}, u32[]{:S(2)}) collective-permute-start(bf16[4,32,1536]{2,1,0:T(8,128)(2,1)S(1)} %get-tuple-element.217), channel_id=1, source_target_pairs={{0,2},{1,3},{2,0},{3,1},{4,6},{5,7},{6,4},{7,5},{8,10},{9,11},{10,... | collective-permute-start | bytes 1179656 | tf_op jit(solution)/shard_map/ppermute | solution.py:959
  151.7 7.5 %collective-permute-start.14 = (bf16[8,16,1024]{2,1,0:T(8,128)(2,1)S(1)}, bf16[8,16,1024]{2,1,0:T(8,128)(2,1)S(1)}, u32[]{:S(2)}, u32[]{:S(2)}) collective-permute-start(bf16[8,16,1024]{2,1,0:T(8,128)(2,1)S(1)} %get-tuple-element.211), channel_id=1, source_target_pairs={{0,16},{1,17},{2,18},{3,19},{4,20},{5,21},{6,22},{7,23},{8,9},{9,8... | collective-permute-start | bytes 786440 | tf_op jit(solution)/shard_map/ppermute | solution.py:959
  160.2 15.6 %collective-permute-start.15 = (bf16[2,96,1024]{2,1,0:T(8,128)(2,1)}, bf16[2,96,1024]{2,1,0:T(8,128)(2,1)S(1)}, u32[]{:S(2)}, u32[]{:S(2)}) collective-permute-start(bf16[2,96,1024]{2,1,0:T(8,128)(2,1)} %get-tuple-element.224), channel_id=1, source_target_pairs={{0,2},{1,3},{2,0},{3,1},{4,6},{5,7},{6,4},{7,5},{8,10},{9,11},{10,... | collective-permute-start | bytes 1179656 | tf_op jit(solution)/shard_map/ppermute | solution.py:959
  163.4 12.2 %collective-permute-start.16 = (bf16[4,16,1536]{2,1,0:T(8,128)(2,1)S(1)}, bf16[4,16,1536]{2,1,0:T(8,128)(2,1)S(1)}, u32[]{:S(2)}, u32[]{:S(2)}) collective-permute-start(bf16[4,16,1536]{2,1,0:T(8,128)(2,1)S(1)} %get-tuple-element.231), channel_id=1, source_target_pairs={{0,16},{1,17},{2,18},{3,19},{4,20},{5,21},{6,22},{7,23},{8,9},{9,8... | collective-permute-start | bytes 589832 | tf_op jit(solution)/shard_map/ppermute | solution.py:959
  164.3 11.3 %collective-permute-start.17 = (bf16[2,32,1536]{2,1,0:T(8,128)(2,1)S(1)}, bf16[2,32,1536]{2,1,0:T(8,128)(2,1)S(1)}, u32[]{:S(2)}, u32[]{:S(2)}) collective-permute-start(bf16[2,32,1536]{2,1,0:T(8,128)(2,1)S(1)} %get-tuple-element.232), channel_id=1, source_target_pairs={{0,4},{1,5},{2,6},{3,7},{4,0},{5,1},{6,2},{7,3},{8,12},{9,13},{10,... | collective-permute-start | bytes 589832 | tf_op jit(solution)/shard_map/ppermute | solution.py:959
  166.8 8.7 %collective-permute-start.18 = (bf16[4,16,1024]{2,1,0:T(8,128)(2,1)S(1)}, bf16[4,16,1024]{2,1,0:T(8,128)(2,1)S(1)}, u32[]{:S(2)}, u32[]{:S(2)}) collective-permute-start(bf16[4,16,1024]{2,1,0:T(8,128)(2,1)S(1)} %get-tuple-element.235), channel_id=1, source_target_pairs={{0,1},{1,0},{2,3},{3,2},{4,5},{5,4},{6,7},{7,6},{8,24},{9,25},{10,... | collective-permute-start | bytes 393224 | tf_op jit(solution)/shard_map/ppermute | solution.py:959
  168.1 3.7 %collective-permute-start.19 = (f32[32,128]{1,0:T(8,128)S(1)}, f32[32,128]{1,0:T(8,128)S(1)}, u32[]{:S(2)}, u32[]{:S(2)}) collective-permute-start(f32[32,128]{1,0:T(8,128)S(1)} %get-tuple-element.236), channel_id=1, source_target_pairs={{0,16},{1,17},{2,18},{3,19},{4,20},{5,21},{6,22},{7,23},{8,9},{9,8... | collective-permute-start | bytes 49160 | tf_op jit(solution)/shard_map/ppermute | solution.py:959
  171.8 3.7 %collective-permute-start.20 = (f32[32,128]{1,0:T(8,128)S(1)}, f32[32,128]{1,0:T(8,128)S(1)}, u32[]{:S(2)}, u32[]{:S(2)}) collective-permute-start(f32[32,128]{1,0:T(8,128)S(1)} %add.68), channel_id=1, source_target_pairs={{0,1},{1,0},{2,3},{3,2},{4,5},{5,4},{6,7},{7,6},{8,24},{9,25},{10,... | collective-permute-start | bytes 49160 | tf_op jit(solution)/shard_map/ppermute | solution.py:959
  175.9 11.3 %collective-permute-start.21 = (bf16[1,96,1024]{2,1,0:T(8,128)(2,1)S(1)}, bf16[1,96,1024]{2,1,0:T(8,128)(2,1)S(1)}, u32[]{:S(2)}, u32[]{:S(2)}) collective-permute-start(bf16[1,96,1024]{2,1,0:T(8,128)(2,1)S(1)} %get-tuple-element.247), channel_id=1, source_target_pairs={{0,4},{1,5},{2,6},{3,7},{4,0},{5,1},{6,2},{7,3},{8,12},{9,13},{10,... | collective-permute-start | bytes 589832 | tf_op jit(solution)/shard_map/ppermute | solution.py:959
  177.7 7.4 %collective-permute-start.22 = (bf16[2,16,1536]{2,1,0:T(8,128)(2,1)S(1)}, bf16[2,16,1536]{2,1,0:T(8,128)(2,1)S(1)}, u32[]{:S(2)}, u32[]{:S(2)}) collective-permute-start(bf16[2,16,1536]{2,1,0:T(8,128)(2,1)S(1)} %get-tuple-element.248), channel_id=1, source_target_pairs={{0,1},{1,0},{2,3},{3,2},{4,5},{5,4},{6,7},{7,6},{8,24},{9,25},{10,... | collective-permute-start | bytes 294920 | tf_op jit(solution)/shard_map/ppermute | solution.py:959
  179.3 5.8 %collective-permute-start.24 = (bf16[2,16,1024]{2,1,0:T(8,128)(2,1)S(1)}, bf16[2,16,1024]{2,1,0:T(8,128)(2,1)S(1)}, u32[]{:S(2)}, u32[]{:S(2)}) collective-permute-start(bf16[2,16,1024]{2,1,0:T(8,128)(2,1)S(1)} %get-tuple-element.252), channel_id=1, source_target_pairs={{0,2},{1,3},{2,0},{3,1},{4,6},{5,7},{6,4},{7,5},{8,10},{9,11},{10,... | collective-permute-start | bytes 196616 | tf_op jit(solution)/shard_map/ppermute | solution.py:959
  180.9 4.3 %collective-permute-start.25 = (f32[2,64,128]{2,1,0:T(8,128)S(1)}, f32[2,64,128]{2,1,0:T(8,128)S(1)}, u32[]{:S(2)}, u32[]{:S(2)}) collective-permute-start(f32[2,64,128]{2,1,0:T(8,128)S(1)} %dynamic-slice_bitcast_fusion.1), channel_id=1, source_target_pairs={{0,16},{1,17},{2,18},{3,19},{4,20},{5,21},{6,22},{7,23},{8,24},{9,... | collective-permute-start | bytes 196616 | tf_op jit(solution)/shard_map/ppermute | solution.py:959
  181.4 3.7 %collective-permute-start.23 = (f32[32,128]{1,0:T(8,128)S(1)}, f32[32,128]{1,0:T(8,128)S(1)}, u32[]{:S(2)}, u32[]{:S(2)}) collective-permute-start(f32[32,128]{1,0:T(8,128)S(1)} %add.69), channel_id=1, source_target_pairs={{0,2},{1,3},{2,0},{3,1},{4,6},{5,7},{6,4},{7,5},{8,10},{9,11},{10,... | collective-permute-start | bytes 49160 | tf_op jit(solution)/shard_map/ppermute | solution.py:959
  187.2 5.2 %collective-permute-start.26 = (bf16[1,16,1024]{2,1,0:T(8,128)(2,1)S(1)}, bf16[1,16,1024]{2,1,0:T(8,128)(2,1)S(1)}, u32[]{:S(2)}, u32[]{:S(2)}) collective-permute-start(bf16[1,16,1024]{2,1,0:T(8,128)(2,1)S(1)} %get-tuple-element.260), channel_id=1, source_target_pairs={{0,4},{1,5},{2,6},{3,7},{4,0},{5,1},{6,2},{7,3},{8,12},{9,13},{10,... | collective-permute-start | bytes 98312 | tf_op jit(solution)/shard_map/ppermute | solution.py:959
  187.7 4.6 %collective-permute-start.27 = (f32[32,128]{1,0:T(8,128)S(1)}, f32[32,128]{1,0:T(8,128)S(1)}, u32[]{:S(2)}, u32[]{:S(2)}) collective-permute-start(f32[32,128]{1,0:T(8,128)S(1)} %add.73), channel_id=1, source_target_pairs={{0,4},{1,5},{2,6},{3,7},{4,0},{5,1},{6,2},{7,3},{8,12},{9,13},{10,... | collective-permute-start | bytes 49160 | tf_op jit(solution)/shard_map/ppermute | solution.py:959
  (34 other events, 295.1 us)

commit v5 on v4

--- a/solution.py
+++ b/solution.py
@@ -1045,6 +1045,8 @@
         rates_give = lax.dynamic_index_in_dim(rates, 1 - bit_x, 0, keepdims=False)
         v_give, v_keep = step_call(bit_b, v_keep, v_got)
         v_got = send(v_give, "b")
+        v_give, v_keep = step_call(bit_low, v_keep, v_got)
+        v_got = send(v_give, "low")
         norm_part = norm_part + send(norm_part, "a")
         norm_part = norm_part + send(norm_part, "b")
         d_got, m_got, u_got, v_got, norm_part, rates_give = after(
@@ -1057,17 +1059,15 @@
         rates_got = send(rates_give, "x")
         m_give, m_keep = step_call(bit_b, m_keep, m_got)
         m_got = send(m_give, "b")
-        v_give, v_keep = step_call(bit_low, v_keep, v_got)
-        v_got = send(v_give, "low")
+        v_give, v_keep = step_call(bit_high, v_keep, v_got)
+        v_got = send(v_give, "high")
         norm_part = norm_part + send(norm_part, "low")
+        norm_part = norm_part + send(norm_part, "high")
         d_got, m_got, norm_part, v_got, rates_got = after(
             (d_got, m_got, norm_part, v_got, rates_got)
         )
         rates = lax.dynamic_index_in_dim(rates, bit_x, 0, keepdims=False) + rates_got
 
-        v_give, v_keep = step_call(bit_high, v_keep, v_got)
-        v_got = send(v_give, "high")
-        norm_part = norm_part + send(norm_part, "high")
         down_grad, mine, other = finish_call(
             scal, (u_keep, u_got), (m_keep, m_got), (d_keep, d_got), (v_keep, v_got), norm_part
         )

time: 198 us -> 196 us (0.990)
  transfers between devices with their start and end apart: 33 -> 33, of which waited for: 12 -> 11; matrix products, arithmetic and copies ran while one was open for 6% -> 6% of each run, Pallas kernels for 45% -> 45%
where the time goes in v5:
time: 196 us
  Pallas kernels  108 us (55%)
  starting transfers between devices  51.3 us (26%)
  waiting for transfers between devices  17.9 us (9%)
  local copies, waits for them, and re-layouts  7.45 us (4%)
  other arithmetic  5.64 us (3%)
  matrix products  3.73 us (2%)
    pallas_call x22, Pallas kernels, call(): pl.pallas_call(kernel, grid_spec=pltpu.PrefetchScalarGridSpec(num_scalar_...  73.6 us
    ppermute x29, starting transfers between devices, send(): return lax.ppermute(value, ('row', 'chan'), pairs)  29.9 us
    all_to_all x4, starting transfers between devices, on_device(): lax.all_to_all(v, 'chan', split_axis=0, concat_axis=0, tiled=True)  21.4 us
    pallas_call x2, Pallas kernels, ssm_bwd(): pl.pallas_call(bwd_kernel, grid=(steps,), in_specs=[s['sm'], s['ch'], s['...  21 us
    ppermute x29, waiting for transfers between devices, send(): return lax.ppermute(value, ('row', 'chan'), pairs)  15 us
    pallas_call x1, Pallas kernels, ssm_fwd(): pl.pallas_call(fwd_kernel, grid=(chans // GROUP,), in_specs=[s['sm'], s['...  12.3 us
    unnamed x66, local copies, waits for them, and re-layouts  5.24 us
  transfers between devices with their start and end apart: 33, of which 11 were waited for; matrix products, arithmetic and copies ran while one was open for 6% of the time, Pallas kernels for 45%

profile of v5, /device:TPU:0, one launch (start us, length us, event | category | flops | bytes accessed | tf_op | source)
XLA Modules:
  0.0 195.6 jit_solution(7202296129333906865)
XLA Ops:
  0.7 4.4 %norm_val.1 = (bf16[512,1024]{1,0:T(8,128)(2,1)S(1)}, bf16[8,4,64,128]{3,2,1,0:T(8,128)(2,1)}, f32[8,4,64,128]{3,2,1,0:T(8,128)}) custom-call(bf16[512,1024]{1,0:T(8,128)(2,1)} %tok.3, f32[1,1024]{1,0:T(1,128)} %bitcast.112, f32[1,1024]{1,0:T(1,128)} %bitcast.115, bf16[1024,512]{1,0:T(8,128)(2,1)} %w_val.3), custom_call_target="tpu_custom_call" | custom-call | tf_op jit(solution)/shard_map/norm_val/pallas_call | solution.py:394
  5.6 7.3 %all-to-all-start = ((bf16[8,4,64,128]{3,2,1,0:T(8,128)(2,1)}), bf16[8,4,64,128]{3,2,1,0:T(8,128)(2,1)S(1)}, u32[]{:S(2)}, u32[]{:S(2)}) async-start(bf16[8,4,64,128]{3,2,1,0:T(8,128)(2,1)} %get-tuple-element.141), calls=%async_computation | async-start | bytes 1048576 | tf_op jit(solution)/shard_map/all_to_all | solution.py:962
  12.9 1.6 masks.1
  14.7 10.9 %gate_first.1 = (bf16[1024,1536]{1,0:T(8,128)(2,1)}, bf16[1024,1536]{1,0:T(8,128)(2,1)}, bf16[1024,1536]{1,0:T(8,128)(2,1)}, bf16[1024,1024]{1,0:T(8,128)(2,1)},...) custom-call(s32[8]{0:T(128)S(1)} %stack.35.core.s, bf16[512,1024]{1,0:T(8,128)(2,1)} %copy-done.8, ...), custom_call_target="tpu_custom_call" | custom-call | tf_op jit(solution)/shard_map/gate_first/pallas_call | solution.py:394
  25.6 2.0 %all-to-all-done = bf16[8,4,64,128]{3,2,1,0:T(8,128)(2,1)S(1)} async-done(((bf16[8,4,64,128]{3,2,1,0:T(8,128)(2,1)}), bf16[8,4,64,128]{3,2,1,0:T(8,128)(2,1)S(1)}, u32[]{:S(2)}, u32[]{:S(2)}) %all-to-all-start) | async-done | bytes 524320 | tf_op jit(solution)/shard_map/all_to_all | solution.py:962
  27.7 12.3 %ssm_fwd.1 = (bf16[32,64,128]{2,1,0:T(8,128)(2,1)}, f32[8,4,256,128]{3,2,1,0:T(8,128)}, bf16[64,128,128]{2,1,0:T(8,128)(2,1)}) custom-call(s32[8,128]{1,0:T(8,128)S(1)} %copy-done.28, bf16[32,64,128]{2,1,0:T(8,128)(2,1)S(1)} %bitcast.101, f32[64,512]{1,0:T(8,128)S(1)} %copy-done.17, f32[64,512]{1,0:T(8,128)S(1)} %copy-done.19, s32[32,128]{1,0:T(8,128)S(1)} %copy-done.21, ...), custom_call_target="tpu_custom_call" | custom-call | flops 20000000000 | bytes 10000000 | tf_op jit(solution)/shard_map/ssm_fwd/pallas_call | solution.py:305
  40.1 4.0 %all-to-all-start.1 = ((bf16[8,4,64,128]{3,2,1,0:T(8,128)(2,1)}), bf16[8,4,64,128]{3,2,1,0:T(8,128)(2,1)S(1)}, u32[]{:S(2)}, u32[]{:S(2)}) async-start(bf16[8,4,64,128]{3,2,1,0:T(8,128)(2,1)} %bitcast.111), calls=%async_computation.1 | async-start | bytes 1048576 | tf_op jit(solution)/shard_map/all_to_all | solution.py:962
  44.0 11.5 %gate_last.1 = (bf16[1024,1536]{1,0:T(8,128)(2,1)}, bf16[1024,1536]{1,0:T(8,128)(2,1)}, bf16[1024,1536]{1,0:T(8,128)(2,1)}, bf16[1024,1024]{1,0:T(8,128)(2,1)}, ...) custom-call(s32[8]{0:T(128)S(1)} %stack.35.core.s, ...), custom_call_target="tpu_custom_call", output_to_operand_aliasing={{0}: (7, {}), {1}: (8, {}), {2}: (9, {})} | custom-call | tf_op jit(solution)/shard_map/gate_last/pallas_call | solution.py:394
  55.6 2.1 %collective-permute-done.2 = bf16[8,4,64,128]{3,2,1,0:T(8,128)(2,1)S(1)} collective-permute-done((bf16[8,4,64,128]{3,2,1,0:T(8,128)(2,1)}, bf16[8,4,64,128]{3,2,1,0:T(8,128)(2,1)S(1)}, u32[]{:S(2)}, u32[]{:S(2)}) %collective-permute-start.2) | collective-permute-done | bytes 524320 | tf_op jit(solution)/shard_map/ppermute | solution.py:959
  57.7 2.2 %add_convert_fusion = bf16[8,4,64,128]{3,2,1,0:T(8,128)(2,1)} fusion(f32[8,4,64,128]{3,2,1,0:T(8,128)} %get-tuple-element.158, bf16[8,4,64,128]{3,2,1,0:T(8,128)(2,1)S(1)} %collective-permute-done.2), kind=kLoop, calls=%fused_computation.2 | loop fusion | flops 786432 | bytes 2097152 | tf_op jit(solution)/shard_map/convert_element_type | solution.py:982
  60.0 6.0 %all-to-all-start.2 = ((bf16[8,4,64,128]{3,2,1,0:T(8,128)(2,1)}), bf16[8,4,64,128]{3,2,1,0:T(8,128)(2,1)S(1)}, u32[]{:S(2)}, u32[]{:S(2)}) async-start(bf16[8,4,64,128]{3,2,1,0:T(8,128)(2,1)} %add_convert_fusion), calls=%async_computation.2 | async-start | bytes 1048576 | tf_op jit(solution)/shard_map/all_to_all | solution.py:962
  66.0 14.1 %mix_up.1 = (bf16[1024,1536]{1,0:T(8,128)(2,1)}, bf16[1024,1536]{1,0:T(8,128)(2,1)}, bf16[16,32,1536]{2,1,0:T(8,128)(2,1)}, bf16[16,32,1536]{2,1,0:T(8,128)(2,1)...) custom-call(s32[8]{0:T(128)S(1)} %stack.35.core.s, bf16[8,4,64,128]{3,2,1,0:T(8,128)(2,1)S(1)} %all-to-all-done.1.y_own, ...), custom_call_target="tpu_custom_call" | custom-call | flops 10000000000 | bytes 10000000 | tf_op jit(solution)/shard_map/mix_up/pallas_call | solution.py:394
  81.0 1.5 collective-permute-start.4
  83.7 10.4 %ssm_bwd.2 = (bf16[32,64,128]{2,1,0:T(8,128)(2,1)}, f32[2,2,2,64,128]{4,3,2,1,0:T(8,128)S(1)}) custom-call(s32[8,128]{1,0:T(8,128)S(1)} %copy-done.28, bf16[32,64,128]{2,1,0:T(8,128)(2,1)S(1)} %bitcast.102, bf16[32,64,128]{2,1,0:T(8,128)(2,1)S(1)} %bitcast.104, f32[64,512]{1,0:T(8,128)S(1)} %copy-done.17, f32[64,512]{1,0:T(8,128)S(1)} %copy-done.19, ...), custom_call_target="tpu_custom_call" | custom-call | flops 20000000000 | bytes 10000000 | tf_op jit(solution)/shard_map/ssm_bwd/pallas_call | solution.py:328
  94.2 3.7 %convolution_convert_fusion = bf16[1536,1024]{1,0:T(8,128)(2,1)S(1)} fusion(bf16[1024,1536]{1,0:T(8,128)(2,1)S(1)} %copy-done.30, bf16[1024,1024]{1,0:T(8,128)(2,1)S(1)} %copy-done.32), kind=kOutput, calls=%fused_computation | convolution fusion | flops 3222798336 | bytes 8388608 | tf_op jit(solution)/shard_map/dot_general | solution.py:22
  97.9 2.1 %split.1 = (bf16[8,96,1024]{2,1,0:T(8,128)(2,1)}, bf16[8,96,1024]{2,1,0:T(8,128)(2,1)S(1)}) custom-call(s32[8]{0:T(128)S(1)} %stack.35.core.s, bf16[2,4,2,96,1024]{4,3,2,1,0:T(8,128)(2,1)S(1)} %bitcast.59, bf16[2,4,2,96,1024]{4,3,2,1,0:T(8,128)(2,1)S(1)} %bitcast.60), custom_call_target="tpu_custom_call" | custom-call | tf_op jit(solution)/shard_map/split/pallas_call | solution.py:394
  104.5 2.2 %collective-permute-start.7 = (bf16[8,16,1536]{2,1,0:T(8,128)(2,1)}, bf16[8,16,1536]{2,1,0:T(8,128)(2,1)}, u32[]{:S(2)}, u32[]{:S(2)}) collective-permute-start(bf16[8,16,1536]{2,1,0:T(8,128)(2,1)} %get-tuple-element.193), channel_id=1, source_target_pairs={{0,4},{1,5},{2,6},{3,7},{4,0},{5,1},{6,2},{7,3},{8,12},{9,13},{10,... | collective-permute-start | bytes 1179656 | tf_op jit(solution)/shard_map/ppermute | solution.py:959
  106.7 10.5 %ssm_bwd.3 = (bf16[32,64,128]{2,1,0:T(8,128)(2,1)}, f32[2,2,2,64,128]{4,3,2,1,0:T(8,128)S(1)}) custom-call(s32[8,128]{1,0:T(8,128)S(1)} %copy-done.28, bf16[32,64,128]{2,1,0:T(8,128)(2,1)S(1)} %bitcast.103, bf16[32,64,128]{2,1,0:T(8,128)(2,1)S(1)} %bitcast.105, f32[64,512]{1,0:T(8,128)S(1)} %copy-done.18, ...), custom_call_target="tpu_custom_call", output_to_operand_aliasing={{0}: (11, {}), {1}: (12, {})} | custom-call | flops 20000000000 | bytes 10000000 | tf_op jit(solution)/shard_map/ssm_bwd/pallas_call | solution.py:328
  119.8 4.1 %all-to-all-start.3 = ((bf16[8,4,64,128]{3,2,1,0:T(8,128)(2,1)}), bf16[8,4,64,128]{3,2,1,0:T(8,128)(2,1)}, u32[]{:S(2)}, u32[]{:S(2)}) async-start(bf16[8,4,64,128]{3,2,1,0:T(8,128)(2,1)} %bitcast.110), calls=%async_computation.3 | async-start | bytes 1048576 | tf_op jit(solution)/shard_map/all_to_all | solution.py:962
  123.9 1.9 collective-permute-start.8
  126.9 12.4 %block.1 = (f32[512,1024]{1,0:T(8,128)}, f32[512,1024]{1,0:T(8,128)}, bf16[2,512,1024]{2,1,0:T(8,128)(2,1)}) custom-call(s32[8]{0:T(128)S(1)} %stack.35.core.s, bf16[1024,1536]{1,0:T(8,128)(2,1)} %get-tuple-element.187.gate, bf16[1024,1536]{1,0:T(8,128)(2,1)} %get-tuple-element.188.d_upre, bf16[3072,1024]{1,0:T(8,128)(2,1)} %refs_1_.1, ...), custom_call_target="tpu_custom_call" | custom-call | tf_op jit(solution)/shard_map/block/pallas_call | solution.py:394
  143.5 2.2 %halve.15 = (bf16[4,32,1536]{2,1,0:T(8,128)(2,1)S(1)}, bf16[4,32,1536]{2,1,0:T(8,128)(2,1)S(1)}) custom-call(s32[1]{0:T(128)} %bitcast.4.bit, bf16[2,4,32,1536]{3,2,1,0:T(8,128)(2,1)S(1)} %bitcast.71, bf16[2,4,32,1536]{3,2,1,0:T(8,128)(2,1)} %bitcast.24.got_g.got_k, bf16[2,4,32,1536]{3,2,1,0:T(8,128)(2,1)S(1)} %bitcast.72, ...), custom_call_target="tpu_custom_call" | custom-call | tf_op jit(solution)/shard_map/halve/pallas_call | solution.py:394
  147.3 1.8 collective-permute-start.13
  153.0 6.3 %norm_back.1 = (bf16[512,1024]{1,0:T(8,128)(2,1)}, f32[512,1024]{1,0:T(8,128)}, f32[32,128]{1,0:T(8,128)S(1)}) custom-call(bf16[512,1024]{1,0:T(8,128)(2,1)} %tok.3, bf16[512,1024]{1,0:T(8,128)(2,1)} %grad.1, f32[1,1024]{1,0:T(1,128)} %bitcast.113, f32[512,1024]{1,0:T(8,128)} %get-tuple-element.189.block_own, ...), custom_call_target="tpu_custom_call" | custom-call | tf_op jit(solution)/shard_map/norm_back/pallas_call | solution.py:394
  161.6 1.8 halve.18
  164.3 2.4 %collective-permute-start.17 = (bf16[2,32,1536]{2,1,0:T(8,128)(2,1)S(1)}, bf16[2,32,1536]{2,1,0:T(8,128)(2,1)S(1)}, u32[]{:S(2)}, u32[]{:S(2)}) collective-permute-start(bf16[2,32,1536]{2,1,0:T(8,128)(2,1)S(1)} %get-tuple-element.232), channel_id=1, source_target_pairs={{0,4},{1,5},{2,6},{3,7},{4,0},{5,1},{6,2},{7,3},{8,12},{9,13},{10,... | collective-permute-start | bytes 589832 | tf_op jit(solution)/shard_map/ppermute | solution.py:959
  168.1 1.5 collective-permute-start.20
  173.6 2.0 %collective-permute-done.21 = f32[32,128]{1,0:T(8,128)S(1)} collective-permute-done((f32[32,128]{1,0:T(8,128)S(1)}, f32[32,128]{1,0:T(8,128)S(1)}, u32[]{:S(2)}, u32[]{:S(2)}) %collective-permute-start.21) | collective-permute-done | bytes 16416 | tf_op jit(solution)/shard_map/ppermute | solution.py:959
  175.6 1.6 collective-permute-done.19
  177.3 2.4 %collective-permute-start.22 = (bf16[1,96,1024]{2,1,0:T(8,128)(2,1)S(1)}, bf16[1,96,1024]{2,1,0:T(8,128)(2,1)S(1)}, u32[]{:S(2)}, u32[]{:S(2)}) collective-permute-start(bf16[1,96,1024]{2,1,0:T(8,128)(2,1)S(1)} %get-tuple-element.249), channel_id=1, source_target_pairs={{0,4},{1,5},{2,6},{3,7},{4,0},{5,1},{6,2},{7,3},{8,12},{9,13},{10,... | collective-permute-start | bytes 589832 | tf_op jit(solution)/shard_map/ppermute | solution.py:959
  185.0 1.7 collective-permute-start.25
  186.7 3.8 %collective-permute-done.25 = f32[32,128]{1,0:T(8,128)S(1)} collective-permute-done((f32[32,128]{1,0:T(8,128)S(1)}, f32[32,128]{1,0:T(8,128)S(1)}, u32[]{:S(2)}, u32[]{:S(2)}) %collective-permute-start.25) | collective-permute-done | bytes 16416 | tf_op jit(solution)/shard_map/ppermute | solution.py:959
  (141 shorter events, 39.5 us)
Async XLA Ops:
  5.1 9.6 %collective-permute-start = (bf16[512,1024]{1,0:T(8,128)(2,1)S(1)}, bf16[512,1024]{1,0:T(8,128)(2,1)}, u32[]{:S(2)}, u32[]{:S(2)}) collective-permute-start(bf16[512,1024]{1,0:T(8,128)(2,1)S(1)} %get-tuple-element.142.n_own), channel_id=1, source_target_pairs={{0,8},{1,9},{2,10},{3,11},{4,12},{5,13},{6,14},{7,15},{8,0},{9,1},... | collective-permute-start | bytes 3145736 | tf_op jit(solution)/shard_map/ppermute | solution.py:959
  5.6 9.1 %collective-permute-start.1 = (bf16[512,1024]{1,0:T(8,128)(2,1)S(1)}, bf16[512,1024]{1,0:T(8,128)(2,1)}, u32[]{:S(2)}, u32[]{:S(2)}) collective-permute-start(bf16[512,1024]{1,0:T(8,128)(2,1)S(1)} %copy-done.29), channel_id=1, source_target_pairs={{0,8},{1,9},{2,10},{3,11},{4,12},{5,13},{6,14},{7,15},{8,0},{9,1},... | collective-permute-start | bytes 3145736 | tf_op jit(solution)/shard_map/ppermute | solution.py:959
  5.6 22.0 %all-to-all-start = ((bf16[8,4,64,128]{3,2,1,0:T(8,128)(2,1)}), bf16[8,4,64,128]{3,2,1,0:T(8,128)(2,1)S(1)}, u32[]{:S(2)}, u32[]{:S(2)}) async-start(bf16[8,4,64,128]{3,2,1,0:T(8,128)(2,1)} %get-tuple-element.141), calls=%async_computation | async-start | bytes 1048576 | tf_op jit(solution)/shard_map/all_to_all | solution.py:962
  40.1 19.8 %all-to-all-start.1 = ((bf16[8,4,64,128]{3,2,1,0:T(8,128)(2,1)}), bf16[8,4,64,128]{3,2,1,0:T(8,128)(2,1)S(1)}, u32[]{:S(2)}, u32[]{:S(2)}) async-start(bf16[8,4,64,128]{3,2,1,0:T(8,128)(2,1)} %bitcast.111), calls=%async_computation.1 | async-start | bytes 1048576 | tf_op jit(solution)/shard_map/all_to_all | solution.py:962
  55.6 2.1 %collective-permute-start.2 = (bf16[8,4,64,128]{3,2,1,0:T(8,128)(2,1)}, bf16[8,4,64,128]{3,2,1,0:T(8,128)(2,1)S(1)}, u32[]{:S(2)}, u32[]{:S(2)}) collective-permute-start(bf16[8,4,64,128]{3,2,1,0:T(8,128)(2,1)} %get-tuple-element.159), channel_id=1, source_target_pairs={{0,8},{1,9},{2,10},{3,11},{4,12},{5,13},{6,14},{7,15},{8,0},{9,1},... | collective-permute-start | bytes 1572872 | tf_op jit(solution)/shard_map/ppermute | solution.py:959
  59.9 6.2 %collective-permute-start.3 = (bf16[8,4,64,128]{3,2,1,0:T(8,128)(2,1)S(1)}, bf16[8,4,64,128]{3,2,1,0:T(8,128)(2,1)S(1)}, u32[]{:S(2)}, u32[]{:S(2)}) collective-permute-start(bf16[8,4,64,128]{3,2,1,0:T(8,128)(2,1)S(1)} %all-to-all-done.1.y_own), channel_id=1, source_target_pairs={{0,8},{1,9},{2,10},{3,11},{4,12},{5,13},{6,14},{7,15},{8,0},{9,1},... | collective-permute-start | bytes 1572872 | tf_op jit(solution)/shard_map/ppermute | solution.py:959
  60.0 21.0 %all-to-all-start.2 = ((bf16[8,4,64,128]{3,2,1,0:T(8,128)(2,1)}), bf16[8,4,64,128]{3,2,1,0:T(8,128)(2,1)S(1)}, u32[]{:S(2)}, u32[]{:S(2)}) async-start(bf16[8,4,64,128]{3,2,1,0:T(8,128)(2,1)} %add_convert_fusion), calls=%async_computation.2 | async-start | bytes 1048576 | tf_op jit(solution)/shard_map/all_to_all | solution.py:962
  81.0 20.6 %collective-permute-start.4 = (bf16[16,32,1536]{2,1,0:T(8,128)(2,1)}, bf16[16,32,1536]{2,1,0:T(8,128)(2,1)S(1)}, u32[]{:S(2)}, u32[]{:S(2)}) collective-permute-start(bf16[16,32,1536]{2,1,0:T(8,128)(2,1)} %get-tuple-element.169), channel_id=1, source_target_pairs={{0,16},{1,17},{2,18},{3,19},{4,20},{5,21},{6,22},{7,23},{8,9},{9,8... | collective-permute-start | bytes 4718600 | tf_op jit(solution)/shard_map/ppermute | solution.py:959
  82.5 18.9 %collective-permute-start.5 = (bf16[16,16,1536]{2,1,0:T(8,128)(2,1)}, bf16[16,16,1536]{2,1,0:T(8,128)(2,1)S(1)}, u32[]{:S(2)}, u32[]{:S(2)}) collective-permute-start(bf16[16,16,1536]{2,1,0:T(8,128)(2,1)} %get-tuple-element.170), channel_id=1, source_target_pairs={{0,2},{1,3},{2,0},{3,1},{4,6},{5,7},{6,4},{7,5},{8,10},{9,11},{10,... | collective-permute-start | bytes 2359304 | tf_op jit(solution)/shard_map/ppermute | solution.py:959
  101.7 22.3 %collective-permute-start.6 = (bf16[8,96,1024]{2,1,0:T(8,128)(2,1)}, bf16[8,96,1024]{2,1,0:T(8,128)(2,1)S(1)}, u32[]{:S(2)}, u32[]{:S(2)}) collective-permute-start(bf16[8,96,1024]{2,1,0:T(8,128)(2,1)} %get-tuple-element.190), channel_id=1, source_target_pairs={{0,16},{1,17},{2,18},{3,19},{4,20},{5,21},{6,22},{7,23},{8,9},{9,8... | collective-permute-start | bytes 4718600 | tf_op jit(solution)/shard_map/ppermute | solution.py:959
  104.5 19.4 %collective-permute-start.7 = (bf16[8,16,1536]{2,1,0:T(8,128)(2,1)}, bf16[8,16,1536]{2,1,0:T(8,128)(2,1)}, u32[]{:S(2)}, u32[]{:S(2)}) collective-permute-start(bf16[8,16,1536]{2,1,0:T(8,128)(2,1)} %get-tuple-element.193), channel_id=1, source_target_pairs={{0,4},{1,5},{2,6},{3,7},{4,0},{5,1},{6,2},{7,3},{8,12},{9,13},{10,... | collective-permute-start | bytes 1179656 | tf_op jit(solution)/shard_map/ppermute | solution.py:959
  119.8 21.9 %all-to-all-start.3 = ((bf16[8,4,64,128]{3,2,1,0:T(8,128)(2,1)}), bf16[8,4,64,128]{3,2,1,0:T(8,128)(2,1)}, u32[]{:S(2)}, u32[]{:S(2)}) async-start(bf16[8,4,64,128]{3,2,1,0:T(8,128)(2,1)} %bitcast.110), calls=%async_computation.3 | async-start | bytes 1048576 | tf_op jit(solution)/shard_map/all_to_all | solution.py:962
  123.9 17.7 %collective-permute-start.8 = (bf16[8,32,1536]{2,1,0:T(8,128)(2,1)}, bf16[8,32,1536]{2,1,0:T(8,128)(2,1)}, u32[]{:S(2)}, u32[]{:S(2)}) collective-permute-start(bf16[8,32,1536]{2,1,0:T(8,128)(2,1)} %copy-done.16), channel_id=1, source_target_pairs={{0,1},{1,0},{2,3},{3,2},{4,5},{5,4},{6,7},{7,6},{8,24},{9,25},{10,... | collective-permute-start | bytes 2359304 | tf_op jit(solution)/shard_map/ppermute | solution.py:959
  126.8 14.8 %collective-permute-start.9 = (f32[2,2,64,128]{3,2,1,0:T(8,128)S(1)}, f32[2,2,64,128]{3,2,1,0:T(8,128)}, u32[]{:S(2)}, u32[]{:S(2)}) collective-permute-start(f32[2,2,64,128]{3,2,1,0:T(8,128)S(1)} %dynamic-slice_bitcast_fusion), channel_id=1, source_target_pairs={{0,8},{1,9},{2,10},{3,11},{4,12},{5,13},{6,14},{7,15},{8,0},{9,1},... | collective-permute-start | bytes 393224 | tf_op jit(solution)/shard_map/ppermute | solution.py:959
  141.7 11.3 %collective-permute-start.10 = (bf16[2,512,1024]{2,1,0:T(8,128)(2,1)}, bf16[2,512,1024]{2,1,0:T(8,128)(2,1)}, u32[]{:S(2)}, u32[]{:S(2)}) collective-permute-start(bf16[2,512,1024]{2,1,0:T(8,128)(2,1)} %get-tuple-element.202), channel_id=1, source_target_pairs={{0,8},{1,9},{2,10},{3,11},{4,12},{5,13},{6,14},{7,15},{8,0},{9,1},... | collective-permute-start | bytes 6291464 | tf_op jit(solution)/shard_map/ppermute | solution.py:959
  142.2 17.0 %collective-permute-start.12 = (bf16[4,96,1024]{2,1,0:T(8,128)(2,1)}, bf16[4,96,1024]{2,1,0:T(8,128)(2,1)S(1)}, u32[]{:S(2)}, u32[]{:S(2)}) collective-permute-start(bf16[4,96,1024]{2,1,0:T(8,128)(2,1)} %copy-done.15), channel_id=1, source_target_pairs={{0,1},{1,0},{2,3},{3,2},{4,5},{5,4},{6,7},{7,6},{8,24},{9,25},{10,... | collective-permute-start | bytes 2359304 | tf_op jit(solution)/shard_map/ppermute | solution.py:959
  147.1 3.2 %collective-permute-start.11 = (bf16[4,4,64,128]{3,2,1,0:T(8,128)(2,1)S(1)}, bf16[4,4,64,128]{3,2,1,0:T(8,128)(2,1)S(1)}, u32[]{:S(2)}, u32[]{:S(2)}) collective-permute-start(bf16[4,4,64,128]{3,2,1,0:T(8,128)(2,1)S(1)} %multiply_convert_fusion.1), channel_id=1, source_target_pairs={{0,8},{1,9},{2,10},{3,11},{4,12},{5,13},{6,14},{7,15},{8,0},{9,1},... | collective-permute-start | bytes 786440 | tf_op jit(solution)/shard_map/ppermute | solution.py:959
  147.3 11.9 %collective-permute-start.13 = (bf16[4,32,1536]{2,1,0:T(8,128)(2,1)S(1)}, bf16[4,32,1536]{2,1,0:T(8,128)(2,1)S(1)}, u32[]{:S(2)}, u32[]{:S(2)}) collective-permute-start(bf16[4,32,1536]{2,1,0:T(8,128)(2,1)S(1)} %get-tuple-element.217), channel_id=1, source_target_pairs={{0,2},{1,3},{2,0},{3,1},{4,6},{5,7},{6,4},{7,5},{8,10},{9,11},{10,... | collective-permute-start | bytes 1179656 | tf_op jit(solution)/shard_map/ppermute | solution.py:959
  151.7 7.5 %collective-permute-start.14 = (bf16[8,16,1024]{2,1,0:T(8,128)(2,1)S(1)}, bf16[8,16,1024]{2,1,0:T(8,128)(2,1)S(1)}, u32[]{:S(2)}, u32[]{:S(2)}) collective-permute-start(bf16[8,16,1024]{2,1,0:T(8,128)(2,1)S(1)} %get-tuple-element.211), channel_id=1, source_target_pairs={{0,16},{1,17},{2,18},{3,19},{4,20},{5,21},{6,22},{7,23},{8,9},{9,8... | collective-permute-start | bytes 786440 | tf_op jit(solution)/shard_map/ppermute | solution.py:959
  160.2 17.0 %collective-permute-start.15 = (bf16[2,96,1024]{2,1,0:T(8,128)(2,1)}, bf16[2,96,1024]{2,1,0:T(8,128)(2,1)S(1)}, u32[]{:S(2)}, u32[]{:S(2)}) collective-permute-start(bf16[2,96,1024]{2,1,0:T(8,128)(2,1)} %get-tuple-element.224), channel_id=1, source_target_pairs={{0,2},{1,3},{2,0},{3,1},{4,6},{5,7},{6,4},{7,5},{8,10},{9,11},{10,... | collective-permute-start | bytes 1179656 | tf_op jit(solution)/shard_map/ppermute | solution.py:959
  163.4 12.2 %collective-permute-start.16 = (bf16[4,16,1536]{2,1,0:T(8,128)(2,1)S(1)}, bf16[4,16,1536]{2,1,0:T(8,128)(2,1)S(1)}, u32[]{:S(2)}, u32[]{:S(2)}) collective-permute-start(bf16[4,16,1536]{2,1,0:T(8,128)(2,1)S(1)} %get-tuple-element.231), channel_id=1, source_target_pairs={{0,16},{1,17},{2,18},{3,19},{4,20},{5,21},{6,22},{7,23},{8,9},{9,8... | collective-permute-start | bytes 589832 | tf_op jit(solution)/shard_map/ppermute | solution.py:959
  164.3 11.3 %collective-permute-start.17 = (bf16[2,32,1536]{2,1,0:T(8,128)(2,1)S(1)}, bf16[2,32,1536]{2,1,0:T(8,128)(2,1)S(1)}, u32[]{:S(2)}, u32[]{:S(2)}) collective-permute-start(bf16[2,32,1536]{2,1,0:T(8,128)(2,1)S(1)} %get-tuple-element.232), channel_id=1, source_target_pairs={{0,4},{1,5},{2,6},{3,7},{4,0},{5,1},{6,2},{7,3},{8,12},{9,13},{10,... | collective-permute-start | bytes 589832 | tf_op jit(solution)/shard_map/ppermute | solution.py:959
  166.8 6.0 %collective-permute-start.18 = (bf16[4,16,1024]{2,1,0:T(8,128)(2,1)S(1)}, bf16[4,16,1024]{2,1,0:T(8,128)(2,1)S(1)}, u32[]{:S(2)}, u32[]{:S(2)}) collective-permute-start(bf16[4,16,1024]{2,1,0:T(8,128)(2,1)S(1)} %get-tuple-element.236), channel_id=1, source_target_pairs={{0,1},{1,0},{2,3},{3,2},{4,5},{5,4},{6,7},{7,6},{8,24},{9,25},{10,... | collective-permute-start | bytes 393224 | tf_op jit(solution)/shard_map/ppermute | solution.py:959
  168.1 3.7 %collective-permute-start.20 = (f32[32,128]{1,0:T(8,128)S(1)}, f32[32,128]{1,0:T(8,128)S(1)}, u32[]{:S(2)}, u32[]{:S(2)}) collective-permute-start(f32[32,128]{1,0:T(8,128)S(1)} %get-tuple-element.238), channel_id=1, source_target_pairs={{0,16},{1,17},{2,18},{3,19},{4,20},{5,21},{6,22},{7,23},{8,9},{9,8... | collective-permute-start | bytes 49160 | tf_op jit(solution)/shard_map/ppermute | solution.py:959
  171.8 3.7 %collective-permute-start.21 = (f32[32,128]{1,0:T(8,128)S(1)}, f32[32,128]{1,0:T(8,128)S(1)}, u32[]{:S(2)}, u32[]{:S(2)}) collective-permute-start(f32[32,128]{1,0:T(8,128)S(1)} %add.68), channel_id=1, source_target_pairs={{0,1},{1,0},{2,3},{3,2},{4,5},{5,4},{6,7},{7,6},{8,24},{9,25},{10,... | collective-permute-start | bytes 49160 | tf_op jit(solution)/shard_map/ppermute | solution.py:959
  172.9 4.3 %collective-permute-start.19 = (bf16[2,16,1024]{2,1,0:T(8,128)(2,1)S(1)}, bf16[2,16,1024]{2,1,0:T(8,128)(2,1)S(1)}, u32[]{:S(2)}, u32[]{:S(2)}) collective-permute-start(bf16[2,16,1024]{2,1,0:T(8,128)(2,1)S(1)} %get-tuple-element.237), channel_id=1, source_target_pairs={{0,2},{1,3},{2,0},{3,1},{4,6},{5,7},{6,4},{7,5},{8,10},{9,11},{10,... | collective-permute-start | bytes 196616 | tf_op jit(solution)/shard_map/ppermute | solution.py:959
  177.3 13.3 %collective-permute-start.22 = (bf16[1,96,1024]{2,1,0:T(8,128)(2,1)S(1)}, bf16[1,96,1024]{2,1,0:T(8,128)(2,1)S(1)}, u32[]{:S(2)}, u32[]{:S(2)}) collective-permute-start(bf16[1,96,1024]{2,1,0:T(8,128)(2,1)S(1)} %get-tuple-element.249), channel_id=1, source_target_pairs={{0,4},{1,5},{2,6},{3,7},{4,0},{5,1},{6,2},{7,3},{8,12},{9,13},{10,... | collective-permute-start | bytes 589832 | tf_op jit(solution)/shard_map/ppermute | solution.py:959
  179.8 10.7 %collective-permute-start.23 = (bf16[2,16,1536]{2,1,0:T(8,128)(2,1)S(1)}, bf16[2,16,1536]{2,1,0:T(8,128)(2,1)S(1)}, u32[]{:S(2)}, u32[]{:S(2)}) collective-permute-start(bf16[2,16,1536]{2,1,0:T(8,128)(2,1)S(1)} %get-tuple-element.250), channel_id=1, source_target_pairs={{0,1},{1,0},{2,3},{3,2},{4,5},{5,4},{6,7},{7,6},{8,24},{9,25},{10,... | collective-permute-start | bytes 294920 | tf_op jit(solution)/shard_map/ppermute | solution.py:959
  180.7 9.9 %collective-permute-start.27 = (f32[2,64,128]{2,1,0:T(8,128)S(1)}, f32[2,64,128]{2,1,0:T(8,128)S(1)}, u32[]{:S(2)}, u32[]{:S(2)}) collective-permute-start(f32[2,64,128]{2,1,0:T(8,128)S(1)} %dynamic-slice_bitcast_fusion.1), channel_id=1, source_target_pairs={{0,16},{1,17},{2,18},{3,19},{4,20},{5,21},{6,22},{7,23},{8,24},{9,... | collective-permute-start | bytes 196616 | tf_op jit(solution)/shard_map/ppermute | solution.py:959
  181.3 3.7 %collective-permute-start.24 = (f32[32,128]{1,0:T(8,128)S(1)}, f32[32,128]{1,0:T(8,128)S(1)}, u32[]{:S(2)}, u32[]{:S(2)}) collective-permute-start(f32[32,128]{1,0:T(8,128)S(1)} %add.69), channel_id=1, source_target_pairs={{0,2},{1,3},{2,0},{3,1},{4,6},{5,7},{6,4},{7,5},{8,10},{9,11},{10,... | collective-permute-start | bytes 49160 | tf_op jit(solution)/shard_map/ppermute | solution.py:959
  182.7 7.8 %collective-permute-start.26 = (bf16[1,16,1024]{2,1,0:T(8,128)(2,1)S(1)}, bf16[1,16,1024]{2,1,0:T(8,128)(2,1)S(1)}, u32[]{:S(2)}, u32[]{:S(2)}) collective-permute-start(bf16[1,16,1024]{2,1,0:T(8,128)(2,1)S(1)} %get-tuple-element.254), channel_id=1, source_target_pairs={{0,4},{1,5},{2,6},{3,7},{4,0},{5,1},{6,2},{7,3},{8,12},{9,13},{10,... | collective-permute-start | bytes 98312 | tf_op jit(solution)/shard_map/ppermute | solution.py:959
  185.0 5.5 %collective-permute-start.25 = (f32[32,128]{1,0:T(8,128)S(1)}, f32[32,128]{1,0:T(8,128)S(1)}, u32[]{:S(2)}, u32[]{:S(2)}) collective-permute-start(f32[32,128]{1,0:T(8,128)S(1)} %add.73), channel_id=1, source_target_pairs={{0,4},{1,5},{2,6},{3,7},{4,0},{5,1},{6,2},{7,3},{8,12},{9,13},{10,... | collective-permute-start | bytes 49160 | tf_op jit(solution)/shard_map/ppermute | solution.py:959
  (34 other events, 295.1 us)

commit v6 on v5

--- a/solution.py
+++ b/solution.py
@@ -1037,10 +1037,8 @@
         d_give, d_keep = step_call(bit_low, d_keep, d_got)
         d_got = send(d_give, "low")
         u_give, u_keep = step_call(bit_high, u_keep, u_got)
-        u_give, norm_part, m_got, v_got = after((u_give, norm_part, m_got, v_got))
+        u_give, norm_part, v_got = after((u_give, norm_part, v_got))
         u_got = send(u_give, "high")
-        m_give, m_keep = step_call(bit_a, m_keep, m_got)
-        m_got = send(m_give, "a")
         rates = lax.dynamic_index_in_dim(rates, core, 0, keepdims=False) + rates_got
         rates_give = lax.dynamic_index_in_dim(rates, 1 - bit_x, 0, keepdims=False)
         v_give, v_keep = step_call(bit_b, v_keep, v_got)
@@ -1048,6 +1046,9 @@
         v_give, v_keep = step_call(bit_low, v_keep, v_got)
         v_got = send(v_give, "low")
         norm_part = norm_part + send(norm_part, "a")
+        norm_part, m_got = after((norm_part, m_got))
+        m_give, m_keep = step_call(bit_a, m_keep, m_got)
+        m_got = send(m_give, "a")
         norm_part = norm_part + send(norm_part, "b")
         d_got, m_got, u_got, v_got, norm_part, rates_give = after(
             (d_got, m_got, u_got, v_got, norm_part, rates_give)

time: 196 us -> 196 us (level)
  no operation moved by 1% of the time
where the time goes in v6:
time: 196 us; the launch traced here: 195 us
  Pallas kernels  108 us (55%)
  starting transfers between devices  50.8 us (26%)
  waiting for transfers between devices  18.3 us (9%)
  local copies, waits for them, and re-layouts  7.45 us (4%)
  other arithmetic  5.64 us (3%)
  matrix products  3.73 us (2%)
    pallas_call x22, Pallas kernels, call(): pl.pallas_call(kernel, grid_spec=pltpu.PrefetchScalarGridSpec(num_scalar_...  72.9 us
    ppermute x29, starting transfers between devices, send(): return lax.ppermute(value, ('row', 'chan'), pairs)  29.3 us
    all_to_all x4, starting transfers between devices, on_device(): lax.all_to_all(v, 'chan', split_axis=0, concat_axis=0, tiled=True)  21.4 us
    pallas_call x2, Pallas kernels, ssm_bwd(): pl.pallas_call(bwd_kernel, grid=(steps,), in_specs=[s['sm'], s['ch'], s['...  21 us
    ppermute x29, waiting for transfers between devices, send(): return lax.ppermute(value, ('row', 'chan'), pairs)  15.4 us
    pallas_call x1, Pallas kernels, ssm_fwd(): pl.pallas_call(fwd_kernel, grid=(chans // GROUP,), in_specs=[s['sm'], s['...  12.3 us
    unnamed x66, local copies, waits for them, and re-layouts  5.24 us
  transfers between devices with their start and end apart: 33, of which 11 were waited for; matrix products, arithmetic and copies ran while one was open for 6% of the time, Pallas kernels for 45%

profile of v6, /device:TPU:0, one launch (start us, length us, event | category | flops | bytes accessed | tf_op | source)
XLA Modules:
  0.0 194.9 jit_solution(5121292093245481983)
XLA Ops:
  0.7 4.4 %norm_val.1 = (bf16[512,1024]{1,0:T(8,128)(2,1)S(1)}, bf16[8,4,64,128]{3,2,1,0:T(8,128)(2,1)}, f32[8,4,64,128]{3,2,1,0:T(8,128)}) custom-call(bf16[512,1024]{1,0:T(8,128)(2,1)} %tok.3, f32[1,1024]{1,0:T(1,128)} %bitcast.112, f32[1,1024]{1,0:T(1,128)} %bitcast.115, bf16[1024,512]{1,0:T(8,128)(2,1)} %w_val.3), custom_call_target="tpu_custom_call" | custom-call | tf_op jit(solution)/shard_map/norm_val/pallas_call | solution.py:394
  5.6 7.3 %all-to-all-start = ((bf16[8,4,64,128]{3,2,1,0:T(8,128)(2,1)}), bf16[8,4,64,128]{3,2,1,0:T(8,128)(2,1)S(1)}, u32[]{:S(2)}, u32[]{:S(2)}) async-start(bf16[8,4,64,128]{3,2,1,0:T(8,128)(2,1)} %get-tuple-element.142), calls=%async_computation | async-start | bytes 1048576 | tf_op jit(solution)/shard_map/all_to_all | solution.py:962
  12.9 1.6 masks.1
  14.7 10.9 %gate_first.1 = (bf16[1024,1536]{1,0:T(8,128)(2,1)}, bf16[1024,1536]{1,0:T(8,128)(2,1)}, bf16[1024,1536]{1,0:T(8,128)(2,1)}, bf16[1024,1024]{1,0:T(8,128)(2,1)},...) custom-call(s32[8]{0:T(128)S(1)} %stack.35.core.s, bf16[512,1024]{1,0:T(8,128)(2,1)} %copy-done.8, ...), custom_call_target="tpu_custom_call" | custom-call | tf_op jit(solution)/shard_map/gate_first/pallas_call | solution.py:394
  25.6 2.0 %all-to-all-done = bf16[8,4,64,128]{3,2,1,0:T(8,128)(2,1)S(1)} async-done(((bf16[8,4,64,128]{3,2,1,0:T(8,128)(2,1)}), bf16[8,4,64,128]{3,2,1,0:T(8,128)(2,1)S(1)}, u32[]{:S(2)}, u32[]{:S(2)}) %all-to-all-start) | async-done | bytes 524320 | tf_op jit(solution)/shard_map/all_to_all | solution.py:962
  27.7 12.3 %ssm_fwd.1 = (bf16[32,64,128]{2,1,0:T(8,128)(2,1)}, f32[8,4,256,128]{3,2,1,0:T(8,128)}, bf16[64,128,128]{2,1,0:T(8,128)(2,1)}) custom-call(s32[8,128]{1,0:T(8,128)S(1)} %copy-done.28, bf16[32,64,128]{2,1,0:T(8,128)(2,1)S(1)} %bitcast.101, f32[64,512]{1,0:T(8,128)S(1)} %copy-done.17, f32[64,512]{1,0:T(8,128)S(1)} %copy-done.19, s32[32,128]{1,0:T(8,128)S(1)} %copy-done.21, ...), custom_call_target="tpu_custom_call" | custom-call | flops 20000000000 | bytes 10000000 | tf_op jit(solution)/shard_map/ssm_fwd/pallas_call | solution.py:305
  40.1 4.0 %all-to-all-start.1 = ((bf16[8,4,64,128]{3,2,1,0:T(8,128)(2,1)}), bf16[8,4,64,128]{3,2,1,0:T(8,128)(2,1)S(1)}, u32[]{:S(2)}, u32[]{:S(2)}) async-start(bf16[8,4,64,128]{3,2,1,0:T(8,128)(2,1)} %bitcast.111), calls=%async_computation.1 | async-start | bytes 1048576 | tf_op jit(solution)/shard_map/all_to_all | solution.py:962
  44.0 11.5 %gate_last.1 = (bf16[1024,1536]{1,0:T(8,128)(2,1)}, bf16[1024,1536]{1,0:T(8,128)(2,1)}, bf16[1024,1536]{1,0:T(8,128)(2,1)}, bf16[1024,1024]{1,0:T(8,128)(2,1)}, ...) custom-call(s32[8]{0:T(128)S(1)} %stack.35.core.s, ...), custom_call_target="tpu_custom_call", output_to_operand_aliasing={{0}: (7, {}), {1}: (8, {}), {2}: (9, {})} | custom-call | tf_op jit(solution)/shard_map/gate_last/pallas_call | solution.py:394
  55.6 2.1 %collective-permute-done.2 = bf16[8,4,64,128]{3,2,1,0:T(8,128)(2,1)S(1)} collective-permute-done((bf16[8,4,64,128]{3,2,1,0:T(8,128)(2,1)}, bf16[8,4,64,128]{3,2,1,0:T(8,128)(2,1)S(1)}, u32[]{:S(2)}, u32[]{:S(2)}) %collective-permute-start.2) | collective-permute-done | bytes 524320 | tf_op jit(solution)/shard_map/ppermute | solution.py:959
  57.7 2.2 %add_convert_fusion = bf16[8,4,64,128]{3,2,1,0:T(8,128)(2,1)} fusion(f32[8,4,64,128]{3,2,1,0:T(8,128)} %get-tuple-element.159, bf16[8,4,64,128]{3,2,1,0:T(8,128)(2,1)S(1)} %collective-permute-done.2), kind=kLoop, calls=%fused_computation.2 | loop fusion | flops 786432 | bytes 2097152 | tf_op jit(solution)/shard_map/convert_element_type | solution.py:982
  60.0 6.0 %all-to-all-start.2 = ((bf16[8,4,64,128]{3,2,1,0:T(8,128)(2,1)}), bf16[8,4,64,128]{3,2,1,0:T(8,128)(2,1)S(1)}, u32[]{:S(2)}, u32[]{:S(2)}) async-start(bf16[8,4,64,128]{3,2,1,0:T(8,128)(2,1)} %add_convert_fusion), calls=%async_computation.2 | async-start | bytes 1048576 | tf_op jit(solution)/shard_map/all_to_all | solution.py:962
  66.0 14.1 %mix_up.1 = (bf16[1024,1536]{1,0:T(8,128)(2,1)}, bf16[1024,1536]{1,0:T(8,128)(2,1)}, bf16[16,32,1536]{2,1,0:T(8,128)(2,1)}, bf16[16,32,1536]{2,1,0:T(8,128)(2,1)...) custom-call(s32[8]{0:T(128)S(1)} %stack.35.core.s, bf16[8,4,64,128]{3,2,1,0:T(8,128)(2,1)S(1)} %all-to-all-done.1.y_own, ...), custom_call_target="tpu_custom_call" | custom-call | flops 10000000000 | bytes 10000000 | tf_op jit(solution)/shard_map/mix_up/pallas_call | solution.py:394
  81.0 1.5 collective-permute-start.4
  83.7 10.4 %ssm_bwd.2 = (bf16[32,64,128]{2,1,0:T(8,128)(2,1)}, f32[2,2,2,64,128]{4,3,2,1,0:T(8,128)S(1)}) custom-call(s32[8,128]{1,0:T(8,128)S(1)} %copy-done.28, bf16[32,64,128]{2,1,0:T(8,128)(2,1)S(1)} %bitcast.102, bf16[32,64,128]{2,1,0:T(8,128)(2,1)S(1)} %bitcast.104, f32[64,512]{1,0:T(8,128)S(1)} %copy-done.17, f32[64,512]{1,0:T(8,128)S(1)} %copy-done.19, ...), custom_call_target="tpu_custom_call" | custom-call | flops 20000000000 | bytes 10000000 | tf_op jit(solution)/shard_map/ssm_bwd/pallas_call | solution.py:328
  94.2 3.7 %convolution_convert_fusion = bf16[1536,1024]{1,0:T(8,128)(2,1)S(1)} fusion(bf16[1024,1536]{1,0:T(8,128)(2,1)S(1)} %copy-done.30, bf16[1024,1024]{1,0:T(8,128)(2,1)S(1)} %copy-done.32), kind=kOutput, calls=%fused_computation | convolution fusion | flops 3222798336 | bytes 8388608 | tf_op jit(solution)/shard_map/dot_general | solution.py:22
  97.9 2.1 %split.1 = (bf16[8,96,1024]{2,1,0:T(8,128)(2,1)}, bf16[8,96,1024]{2,1,0:T(8,128)(2,1)S(1)}) custom-call(s32[8]{0:T(128)S(1)} %stack.35.core.s, bf16[2,4,2,96,1024]{4,3,2,1,0:T(8,128)(2,1)S(1)} %bitcast.59, bf16[2,4,2,96,1024]{4,3,2,1,0:T(8,128)(2,1)S(1)} %bitcast.60), custom_call_target="tpu_custom_call" | custom-call | tf_op jit(solution)/shard_map/split/pallas_call | solution.py:394
  101.7 1.5 collective-permute-start.6
  104.5 2.2 %collective-permute-start.7 = (bf16[8,16,1536]{2,1,0:T(8,128)(2,1)}, bf16[8,16,1536]{2,1,0:T(8,128)(2,1)}, u32[]{:S(2)}, u32[]{:S(2)}) collective-permute-start(bf16[8,16,1536]{2,1,0:T(8,128)(2,1)} %get-tuple-element.194), channel_id=1, source_target_pairs={{0,4},{1,5},{2,6},{3,7},{4,0},{5,1},{6,2},{7,3},{8,12},{9,13},{10,... | collective-permute-start | bytes 1179656 | tf_op jit(solution)/shard_map/ppermute | solution.py:959
  106.7 10.5 %ssm_bwd.3 = (bf16[32,64,128]{2,1,0:T(8,128)(2,1)}, f32[2,2,2,64,128]{4,3,2,1,0:T(8,128)S(1)}) custom-call(s32[8,128]{1,0:T(8,128)S(1)} %copy-done.28, bf16[32,64,128]{2,1,0:T(8,128)(2,1)S(1)} %bitcast.103, bf16[32,64,128]{2,1,0:T(8,128)(2,1)S(1)} %bitcast.105, f32[64,512]{1,0:T(8,128)S(1)} %copy-done.18, ...), custom_call_target="tpu_custom_call", output_to_operand_aliasing={{0}: (11, {}), {1}: (12, {})} | custom-call | flops 20000000000 | bytes 10000000 | tf_op jit(solution)/shard_map/ssm_bwd/pallas_call | solution.py:328
  119.8 4.1 %all-to-all-start.3 = ((bf16[8,4,64,128]{3,2,1,0:T(8,128)(2,1)}), bf16[8,4,64,128]{3,2,1,0:T(8,128)(2,1)}, u32[]{:S(2)}, u32[]{:S(2)}) async-start(bf16[8,4,64,128]{3,2,1,0:T(8,128)(2,1)} %bitcast.110), calls=%async_computation.3 | async-start | bytes 1048576 | tf_op jit(solution)/shard_map/all_to_all | solution.py:962
  123.9 1.9 collective-permute-start.8
  126.9 12.4 %block.1 = (f32[512,1024]{1,0:T(8,128)}, f32[512,1024]{1,0:T(8,128)}, bf16[2,512,1024]{2,1,0:T(8,128)(2,1)}) custom-call(s32[8]{0:T(128)S(1)} %stack.35.core.s, bf16[1024,1536]{1,0:T(8,128)(2,1)} %get-tuple-element.188.gate, bf16[1024,1536]{1,0:T(8,128)(2,1)} %get-tuple-element.189.d_upre, bf16[3072,1024]{1,0:T(8,128)(2,1)} %refs_1_.1, ...), custom_call_target="tpu_custom_call" | custom-call | tf_op jit(solution)/shard_map/block/pallas_call | solution.py:394
  143.5 2.2 %halve.15 = (bf16[4,32,1536]{2,1,0:T(8,128)(2,1)S(1)}, bf16[4,32,1536]{2,1,0:T(8,128)(2,1)S(1)}) custom-call(s32[1]{0:T(128)} %bitcast.4.bit, bf16[2,4,32,1536]{3,2,1,0:T(8,128)(2,1)S(1)} %bitcast.71, bf16[2,4,32,1536]{3,2,1,0:T(8,128)(2,1)} %bitcast.24.got_g.got_k, bf16[2,4,32,1536]{3,2,1,0:T(8,128)(2,1)S(1)} %bitcast.72, ...), custom_call_target="tpu_custom_call" | custom-call | tf_op jit(solution)/shard_map/halve/pallas_call | solution.py:394
  147.3 1.8 collective-permute-start.13
  153.0 6.3 %norm_back.1 = (bf16[512,1024]{1,0:T(8,128)(2,1)}, f32[512,1024]{1,0:T(8,128)}, f32[32,128]{1,0:T(8,128)S(1)}) custom-call(bf16[512,1024]{1,0:T(8,128)(2,1)} %tok.3, bf16[512,1024]{1,0:T(8,128)(2,1)} %grad.1, f32[1,1024]{1,0:T(1,128)} %bitcast.113, f32[512,1024]{1,0:T(8,128)} %get-tuple-element.190.block_own, ...), custom_call_target="tpu_custom_call" | custom-call | tf_op jit(solution)/shard_map/norm_back/pallas_call | solution.py:394
  161.9 2.4 %collective-permute-start.18 = (bf16[2,32,1536]{2,1,0:T(8,128)(2,1)S(1)}, bf16[2,32,1536]{2,1,0:T(8,128)(2,1)S(1)}, u32[]{:S(2)}, u32[]{:S(2)}) collective-permute-start(bf16[2,32,1536]{2,1,0:T(8,128)(2,1)S(1)} %get-tuple-element.234), channel_id=1, source_target_pairs={{0,4},{1,5},{2,6},{3,7},{4,0},{5,1},{6,2},{7,3},{8,12},{9,13},{10,... | collective-permute-start | bytes 589832 | tf_op jit(solution)/shard_map/ppermute | solution.py:959
  165.7 1.8 halve.18
  167.5 1.5 collective-permute-start.17
  171.5 2.3 %collective-permute-done.21 = f32[32,128]{1,0:T(8,128)S(1)} collective-permute-done((f32[32,128]{1,0:T(8,128)S(1)}, f32[32,128]{1,0:T(8,128)S(1)}, u32[]{:S(2)}, u32[]{:S(2)}) %collective-permute-start.21) | collective-permute-done | bytes 16416 | tf_op jit(solution)/shard_map/ppermute | solution.py:959
  174.0 2.4 %collective-permute-done.20 = bf16[2,16,1024]{2,1,0:T(8,128)(2,1)S(1)} collective-permute-done((bf16[2,16,1024]{2,1,0:T(8,128)(2,1)S(1)}, bf16[2,16,1024]{2,1,0:T(8,128)(2,1)S(1)}, u32[]{:S(2)}, u32[]{:S(2)}) %collective-permute-start.20) | collective-permute-done | bytes 65568 | tf_op jit(solution)/shard_map/ppermute | solution.py:959
  176.5 2.5 %collective-permute-start.22 = (bf16[1,96,1024]{2,1,0:T(8,128)(2,1)S(1)}, bf16[1,96,1024]{2,1,0:T(8,128)(2,1)S(1)}, u32[]{:S(2)}, u32[]{:S(2)}) collective-permute-start(bf16[1,96,1024]{2,1,0:T(8,128)(2,1)S(1)} %get-tuple-element.251), channel_id=1, source_target_pairs={{0,4},{1,5},{2,6},{3,7},{4,0},{5,1},{6,2},{7,3},{8,12},{9,13},{10,... | collective-permute-start | bytes 589832 | tf_op jit(solution)/shard_map/ppermute | solution.py:959
  185.5 4.2 %collective-permute-done.25 = f32[32,128]{1,0:T(8,128)S(1)} collective-permute-done((f32[32,128]{1,0:T(8,128)S(1)}, f32[32,128]{1,0:T(8,128)S(1)}, u32[]{:S(2)}, u32[]{:S(2)}) %collective-permute-start.25) | collective-permute-done | bytes 16416 | tf_op jit(solution)/shard_map/ppermute | solution.py:959
  (141 shorter events, 37.4 us)
Async XLA Ops:
  5.1 9.6 %collective-permute-start = (bf16[512,1024]{1,0:T(8,128)(2,1)S(1)}, bf16[512,1024]{1,0:T(8,128)(2,1)}, u32[]{:S(2)}, u32[]{:S(2)}) collective-permute-start(bf16[512,1024]{1,0:T(8,128)(2,1)S(1)} %get-tuple-element.143.n_own), channel_id=1, source_target_pairs={{0,8},{1,9},{2,10},{3,11},{4,12},{5,13},{6,14},{7,15},{8,0},{9,1},... | collective-permute-start | bytes 3145736 | tf_op jit(solution)/shard_map/ppermute | solution.py:959
  5.6 9.1 %collective-permute-start.1 = (bf16[512,1024]{1,0:T(8,128)(2,1)S(1)}, bf16[512,1024]{1,0:T(8,128)(2,1)}, u32[]{:S(2)}, u32[]{:S(2)}) collective-permute-start(bf16[512,1024]{1,0:T(8,128)(2,1)S(1)} %copy-done.29), channel_id=1, source_target_pairs={{0,8},{1,9},{2,10},{3,11},{4,12},{5,13},{6,14},{7,15},{8,0},{9,1},... | collective-permute-start | bytes 3145736 | tf_op jit(solution)/shard_map/ppermute | solution.py:959
  5.6 22.0 %all-to-all-start = ((bf16[8,4,64,128]{3,2,1,0:T(8,128)(2,1)}), bf16[8,4,64,128]{3,2,1,0:T(8,128)(2,1)S(1)}, u32[]{:S(2)}, u32[]{:S(2)}) async-start(bf16[8,4,64,128]{3,2,1,0:T(8,128)(2,1)} %get-tuple-element.142), calls=%async_computation | async-start | bytes 1048576 | tf_op jit(solution)/shard_map/all_to_all | solution.py:962
  40.1 19.8 %all-to-all-start.1 = ((bf16[8,4,64,128]{3,2,1,0:T(8,128)(2,1)}), bf16[8,4,64,128]{3,2,1,0:T(8,128)(2,1)S(1)}, u32[]{:S(2)}, u32[]{:S(2)}) async-start(bf16[8,4,64,128]{3,2,1,0:T(8,128)(2,1)} %bitcast.111), calls=%async_computation.1 | async-start | bytes 1048576 | tf_op jit(solution)/shard_map/all_to_all | solution.py:962
  55.6 2.1 %collective-permute-start.2 = (bf16[8,4,64,128]{3,2,1,0:T(8,128)(2,1)}, bf16[8,4,64,128]{3,2,1,0:T(8,128)(2,1)S(1)}, u32[]{:S(2)}, u32[]{:S(2)}) collective-permute-start(bf16[8,4,64,128]{3,2,1,0:T(8,128)(2,1)} %get-tuple-element.160), channel_id=1, source_target_pairs={{0,8},{1,9},{2,10},{3,11},{4,12},{5,13},{6,14},{7,15},{8,0},{9,1},... | collective-permute-start | bytes 1572872 | tf_op jit(solution)/shard_map/ppermute | solution.py:959
  59.9 6.2 %collective-permute-start.3 = (bf16[8,4,64,128]{3,2,1,0:T(8,128)(2,1)S(1)}, bf16[8,4,64,128]{3,2,1,0:T(8,128)(2,1)S(1)}, u32[]{:S(2)}, u32[]{:S(2)}) collective-permute-start(bf16[8,4,64,128]{3,2,1,0:T(8,128)(2,1)S(1)} %all-to-all-done.1.y_own), channel_id=1, source_target_pairs={{0,8},{1,9},{2,10},{3,11},{4,12},{5,13},{6,14},{7,15},{8,0},{9,1},... | collective-permute-start | bytes 1572872 | tf_op jit(solution)/shard_map/ppermute | solution.py:959
  60.0 21.0 %all-to-all-start.2 = ((bf16[8,4,64,128]{3,2,1,0:T(8,128)(2,1)}), bf16[8,4,64,128]{3,2,1,0:T(8,128)(2,1)S(1)}, u32[]{:S(2)}, u32[]{:S(2)}) async-start(bf16[8,4,64,128]{3,2,1,0:T(8,128)(2,1)} %add_convert_fusion), calls=%async_computation.2 | async-start | bytes 1048576 | tf_op jit(solution)/shard_map/all_to_all | solution.py:962
  81.0 20.6 %collective-permute-start.4 = (bf16[16,32,1536]{2,1,0:T(8,128)(2,1)}, bf16[16,32,1536]{2,1,0:T(8,128)(2,1)S(1)}, u32[]{:S(2)}, u32[]{:S(2)}) collective-permute-start(bf16[16,32,1536]{2,1,0:T(8,128)(2,1)} %get-tuple-element.170), channel_id=1, source_target_pairs={{0,16},{1,17},{2,18},{3,19},{4,20},{5,21},{6,22},{7,23},{8,9},{9,8... | collective-permute-start | bytes 4718600 | tf_op jit(solution)/shard_map/ppermute | solution.py:959
  82.5 18.9 %collective-permute-start.5 = (bf16[16,16,1536]{2,1,0:T(8,128)(2,1)}, bf16[16,16,1536]{2,1,0:T(8,128)(2,1)S(1)}, u32[]{:S(2)}, u32[]{:S(2)}) collective-permute-start(bf16[16,16,1536]{2,1,0:T(8,128)(2,1)} %get-tuple-element.171), channel_id=1, source_target_pairs={{0,2},{1,3},{2,0},{3,1},{4,6},{5,7},{6,4},{7,5},{8,10},{9,11},{10,... | collective-permute-start | bytes 2359304 | tf_op jit(solution)/shard_map/ppermute | solution.py:959
  101.7 22.3 %collective-permute-start.6 = (bf16[8,96,1024]{2,1,0:T(8,128)(2,1)}, bf16[8,96,1024]{2,1,0:T(8,128)(2,1)S(1)}, u32[]{:S(2)}, u32[]{:S(2)}) collective-permute-start(bf16[8,96,1024]{2,1,0:T(8,128)(2,1)} %get-tuple-element.191), channel_id=1, source_target_pairs={{0,16},{1,17},{2,18},{3,19},{4,20},{5,21},{6,22},{7,23},{8,9},{9,8... | collective-permute-start | bytes 4718600 | tf_op jit(solution)/shard_map/ppermute | solution.py:959
  104.5 19.4 %collective-permute-start.7 = (bf16[8,16,1536]{2,1,0:T(8,128)(2,1)}, bf16[8,16,1536]{2,1,0:T(8,128)(2,1)}, u32[]{:S(2)}, u32[]{:S(2)}) collective-permute-start(bf16[8,16,1536]{2,1,0:T(8,128)(2,1)} %get-tuple-element.194), channel_id=1, source_target_pairs={{0,4},{1,5},{2,6},{3,7},{4,0},{5,1},{6,2},{7,3},{8,12},{9,13},{10,... | collective-permute-start | bytes 1179656 | tf_op jit(solution)/shard_map/ppermute | solution.py:959
  119.8 21.9 %all-to-all-start.3 = ((bf16[8,4,64,128]{3,2,1,0:T(8,128)(2,1)}), bf16[8,4,64,128]{3,2,1,0:T(8,128)(2,1)}, u32[]{:S(2)}, u32[]{:S(2)}) async-start(bf16[8,4,64,128]{3,2,1,0:T(8,128)(2,1)} %bitcast.110), calls=%async_computation.3 | async-start | bytes 1048576 | tf_op jit(solution)/shard_map/all_to_all | solution.py:962
  123.9 17.7 %collective-permute-start.8 = (bf16[8,32,1536]{2,1,0:T(8,128)(2,1)}, bf16[8,32,1536]{2,1,0:T(8,128)(2,1)}, u32[]{:S(2)}, u32[]{:S(2)}) collective-permute-start(bf16[8,32,1536]{2,1,0:T(8,128)(2,1)} %copy-done.16), channel_id=1, source_target_pairs={{0,1},{1,0},{2,3},{3,2},{4,5},{5,4},{6,7},{7,6},{8,24},{9,25},{10,... | collective-permute-start | bytes 2359304 | tf_op jit(solution)/shard_map/ppermute | solution.py:959
  126.8 14.8 %collective-permute-start.9 = (f32[2,2,64,128]{3,2,1,0:T(8,128)S(1)}, f32[2,2,64,128]{3,2,1,0:T(8,128)}, u32[]{:S(2)}, u32[]{:S(2)}) collective-permute-start(f32[2,2,64,128]{3,2,1,0:T(8,128)S(1)} %dynamic-slice_bitcast_fusion), channel_id=1, source_target_pairs={{0,8},{1,9},{2,10},{3,11},{4,12},{5,13},{6,14},{7,15},{8,0},{9,1},... | collective-permute-start | bytes 393224 | tf_op jit(solution)/shard_map/ppermute | solution.py:959
  141.7 11.3 %collective-permute-start.10 = (bf16[2,512,1024]{2,1,0:T(8,128)(2,1)}, bf16[2,512,1024]{2,1,0:T(8,128)(2,1)}, u32[]{:S(2)}, u32[]{:S(2)}) collective-permute-start(bf16[2,512,1024]{2,1,0:T(8,128)(2,1)} %get-tuple-element.203), channel_id=1, source_target_pairs={{0,8},{1,9},{2,10},{3,11},{4,12},{5,13},{6,14},{7,15},{8,0},{9,1},... | collective-permute-start | bytes 6291464 | tf_op jit(solution)/shard_map/ppermute | solution.py:959
  142.2 17.1 %collective-permute-start.12 = (bf16[4,96,1024]{2,1,0:T(8,128)(2,1)}, bf16[4,96,1024]{2,1,0:T(8,128)(2,1)S(1)}, u32[]{:S(2)}, u32[]{:S(2)}) collective-permute-start(bf16[4,96,1024]{2,1,0:T(8,128)(2,1)} %copy-done.15), channel_id=1, source_target_pairs={{0,1},{1,0},{2,3},{3,2},{4,5},{5,4},{6,7},{7,6},{8,24},{9,25},{10,... | collective-permute-start | bytes 2359304 | tf_op jit(solution)/shard_map/ppermute | solution.py:959
  147.1 3.2 %collective-permute-start.11 = (bf16[4,4,64,128]{3,2,1,0:T(8,128)(2,1)S(1)}, bf16[4,4,64,128]{3,2,1,0:T(8,128)(2,1)S(1)}, u32[]{:S(2)}, u32[]{:S(2)}) collective-permute-start(bf16[4,4,64,128]{3,2,1,0:T(8,128)(2,1)S(1)} %multiply_convert_fusion.1), channel_id=1, source_target_pairs={{0,8},{1,9},{2,10},{3,11},{4,12},{5,13},{6,14},{7,15},{8,0},{9,1},... | collective-permute-start | bytes 786440 | tf_op jit(solution)/shard_map/ppermute | solution.py:959
  147.3 11.9 %collective-permute-start.13 = (bf16[4,32,1536]{2,1,0:T(8,128)(2,1)S(1)}, bf16[4,32,1536]{2,1,0:T(8,128)(2,1)S(1)}, u32[]{:S(2)}, u32[]{:S(2)}) collective-permute-start(bf16[4,32,1536]{2,1,0:T(8,128)(2,1)S(1)} %get-tuple-element.218), channel_id=1, source_target_pairs={{0,2},{1,3},{2,0},{3,1},{4,6},{5,7},{6,4},{7,5},{8,10},{9,11},{10,... | collective-permute-start | bytes 1179656 | tf_op jit(solution)/shard_map/ppermute | solution.py:959
  151.7 7.5 %collective-permute-start.14 = (bf16[8,16,1024]{2,1,0:T(8,128)(2,1)S(1)}, bf16[8,16,1024]{2,1,0:T(8,128)(2,1)S(1)}, u32[]{:S(2)}, u32[]{:S(2)}) collective-permute-start(bf16[8,16,1024]{2,1,0:T(8,128)(2,1)S(1)} %get-tuple-element.212), channel_id=1, source_target_pairs={{0,16},{1,17},{2,18},{3,19},{4,20},{5,21},{6,22},{7,23},{8,9},{9,8... | collective-permute-start | bytes 786440 | tf_op jit(solution)/shard_map/ppermute | solution.py:959
  159.5 16.9 %collective-permute-start.15 = (bf16[2,96,1024]{2,1,0:T(8,128)(2,1)S(1)}, bf16[2,96,1024]{2,1,0:T(8,128)(2,1)S(1)}, u32[]{:S(2)}, u32[]{:S(2)}) collective-permute-start(bf16[2,96,1024]{2,1,0:T(8,128)(2,1)S(1)} %get-tuple-element.225), channel_id=1, source_target_pairs={{0,2},{1,3},{2,0},{3,1},{4,6},{5,7},{6,4},{7,5},{8,10},{9,11},{10,... | collective-permute-start | bytes 1179656 | tf_op jit(solution)/shard_map/ppermute | solution.py:959
  161.0 4.7 %collective-permute-start.16 = (f32[32,128]{1,0:T(8,128)S(1)}, f32[32,128]{1,0:T(8,128)S(1)}, u32[]{:S(2)}, u32[]{:S(2)}) collective-permute-start(f32[32,128]{1,0:T(8,128)S(1)} %get-tuple-element.230), channel_id=1, source_target_pairs={{0,16},{1,17},{2,18},{3,19},{4,20},{5,21},{6,22},{7,23},{8,9},{9,8... | collective-permute-start | bytes 49160 | tf_op jit(solution)/shard_map/ppermute | solution.py:959
  161.9 12.1 %collective-permute-start.18 = (bf16[2,32,1536]{2,1,0:T(8,128)(2,1)S(1)}, bf16[2,32,1536]{2,1,0:T(8,128)(2,1)S(1)}, u32[]{:S(2)}, u32[]{:S(2)}) collective-permute-start(bf16[2,32,1536]{2,1,0:T(8,128)(2,1)S(1)} %get-tuple-element.234), channel_id=1, source_target_pairs={{0,4},{1,5},{2,6},{3,7},{4,0},{5,1},{6,2},{7,3},{8,12},{9,13},{10,... | collective-permute-start | bytes 589832 | tf_op jit(solution)/shard_map/ppermute | solution.py:959
  164.4 6.2 %collective-permute-start.19 = (bf16[4,16,1024]{2,1,0:T(8,128)(2,1)S(1)}, bf16[4,16,1024]{2,1,0:T(8,128)(2,1)S(1)}, u32[]{:S(2)}, u32[]{:S(2)}) collective-permute-start(bf16[4,16,1024]{2,1,0:T(8,128)(2,1)S(1)} %get-tuple-element.238), channel_id=1, source_target_pairs={{0,1},{1,0},{2,3},{3,2},{4,5},{5,4},{6,7},{7,6},{8,24},{9,25},{10,... | collective-permute-start | bytes 393224 | tf_op jit(solution)/shard_map/ppermute | solution.py:959
  167.5 8.9 %collective-permute-start.17 = (bf16[4,16,1536]{2,1,0:T(8,128)(2,1)S(1)}, bf16[4,16,1536]{2,1,0:T(8,128)(2,1)S(1)}, u32[]{:S(2)}, u32[]{:S(2)}) collective-permute-start(bf16[4,16,1536]{2,1,0:T(8,128)(2,1)S(1)} %get-tuple-element.233), channel_id=1, source_target_pairs={{0,16},{1,17},{2,18},{3,19},{4,20},{5,21},{6,22},{7,23},{8,9},{9,8... | collective-permute-start | bytes 589832 | tf_op jit(solution)/shard_map/ppermute | solution.py:959
  170.0 3.8 %collective-permute-start.21 = (f32[32,128]{1,0:T(8,128)S(1)}, f32[32,128]{1,0:T(8,128)S(1)}, u32[]{:S(2)}, u32[]{:S(2)}) collective-permute-start(f32[32,128]{1,0:T(8,128)S(1)} %add.68), channel_id=1, source_target_pairs={{0,1},{1,0},{2,3},{3,2},{4,5},{5,4},{6,7},{7,6},{8,24},{9,25},{10,... | collective-permute-start | bytes 49160 | tf_op jit(solution)/shard_map/ppermute | solution.py:959
  170.7 5.7 %collective-permute-start.20 = (bf16[2,16,1024]{2,1,0:T(8,128)(2,1)S(1)}, bf16[2,16,1024]{2,1,0:T(8,128)(2,1)S(1)}, u32[]{:S(2)}, u32[]{:S(2)}) collective-permute-start(bf16[2,16,1024]{2,1,0:T(8,128)(2,1)S(1)} %get-tuple-element.239), channel_id=1, source_target_pairs={{0,2},{1,3},{2,0},{3,1},{4,6},{5,7},{6,4},{7,5},{8,10},{9,11},{10,... | collective-permute-start | bytes 196616 | tf_op jit(solution)/shard_map/ppermute | solution.py:959
  176.5 13.3 %collective-permute-start.22 = (bf16[1,96,1024]{2,1,0:T(8,128)(2,1)S(1)}, bf16[1,96,1024]{2,1,0:T(8,128)(2,1)S(1)}, u32[]{:S(2)}, u32[]{:S(2)}) collective-permute-start(bf16[1,96,1024]{2,1,0:T(8,128)(2,1)S(1)} %get-tuple-element.251), channel_id=1, source_target_pairs={{0,4},{1,5},{2,6},{3,7},{4,0},{5,1},{6,2},{7,3},{8,12},{9,13},{10,... | collective-permute-start | bytes 589832 | tf_op jit(solution)/shard_map/ppermute | solution.py:959
  179.0 10.7 %collective-permute-start.23 = (bf16[2,16,1536]{2,1,0:T(8,128)(2,1)S(1)}, bf16[2,16,1536]{2,1,0:T(8,128)(2,1)S(1)}, u32[]{:S(2)}, u32[]{:S(2)}) collective-permute-start(bf16[2,16,1536]{2,1,0:T(8,128)(2,1)S(1)} %get-tuple-element.252), channel_id=1, source_target_pairs={{0,1},{1,0},{2,3},{3,2},{4,5},{5,4},{6,7},{7,6},{8,24},{9,25},{10,... | collective-permute-start | bytes 294920 | tf_op jit(solution)/shard_map/ppermute | solution.py:959
  179.9 9.9 %collective-permute-start.27 = (f32[2,64,128]{2,1,0:T(8,128)S(1)}, f32[2,64,128]{2,1,0:T(8,128)S(1)}, u32[]{:S(2)}, u32[]{:S(2)}) collective-permute-start(f32[2,64,128]{2,1,0:T(8,128)S(1)} %dynamic-slice_bitcast_fusion.1), channel_id=1, source_target_pairs={{0,16},{1,17},{2,18},{3,19},{4,20},{5,21},{6,22},{7,23},{8,24},{9,... | collective-permute-start | bytes 196616 | tf_op jit(solution)/shard_map/ppermute | solution.py:959
  180.5 3.7 %collective-permute-start.24 = (f32[32,128]{1,0:T(8,128)S(1)}, f32[32,128]{1,0:T(8,128)S(1)}, u32[]{:S(2)}, u32[]{:S(2)}) collective-permute-start(f32[32,128]{1,0:T(8,128)S(1)} %add.69), channel_id=1, source_target_pairs={{0,2},{1,3},{2,0},{3,1},{4,6},{5,7},{6,4},{7,5},{8,10},{9,11},{10,... | collective-permute-start | bytes 49160 | tf_op jit(solution)/shard_map/ppermute | solution.py:959
  181.9 7.8 %collective-permute-start.26 = (bf16[1,16,1024]{2,1,0:T(8,128)(2,1)S(1)}, bf16[1,16,1024]{2,1,0:T(8,128)(2,1)S(1)}, u32[]{:S(2)}, u32[]{:S(2)}) collective-permute-start(bf16[1,16,1024]{2,1,0:T(8,128)(2,1)S(1)} %get-tuple-element.256), channel_id=1, source_target_pairs={{0,4},{1,5},{2,6},{3,7},{4,0},{5,1},{6,2},{7,3},{8,12},{9,13},{10,... | collective-permute-start | bytes 98312 | tf_op jit(solution)/shard_map/ppermute | solution.py:959
  184.2 5.5 %collective-permute-start.25 = (f32[32,128]{1,0:T(8,128)S(1)}, f32[32,128]{1,0:T(8,128)S(1)}, u32[]{:S(2)}, u32[]{:S(2)}) collective-permute-start(f32[32,128]{1,0:T(8,128)S(1)} %add.73), channel_id=1, source_target_pairs={{0,4},{1,5},{2,6},{3,7},{4,0},{5,1},{6,2},{7,3},{8,12},{9,13},{10,... | collective-permute-start | bytes 49160 | tf_op jit(solution)/shard_map/ppermute | solution.py:959
  (34 other events, 295.2 us)
